TPU v7x, 32 devices: a whole 2x2x4 slice. The times are simulated.
32 devices in a mesh: band: 4 (over x, core), grid: 8 (over z, y).
Axes of the slice: x: 2, y: 2, z: 4, core: 2. Of those that a mesh axis runs over, the one named last changes fastest.
Arguments:
- orbitals: float32 [96, 16, 16, 512], P('grid', None, None, 'band'), may hold values from -24 to 24
- potential: float32 [96, 16, 16], P('grid'), may hold values from -3 to -1
- projectors: float32 [32, 8, 13, 256], P('grid'), may hold values from -0.109375 to 0.109375
- atom_planes: int32 [32, 13], P('grid'), may hold values from 0 to 23, as said below
- kb_energy: float32 [8], replicated, may hold values from 1 to 4
Outputs:
- filtered: float32 [96, 16, 16, 512], P('grid', None, None, 'band')
- correlation_gram: float32 [512, 512], P('band')
Inputs may be any that keep to these rules, and one draw needn't show every extreme that they name: `atom_planes`: each atom's row holds 13 consecutive plane numbers; the first atom starts at plane 0 and the last atom at plane 12 - 1.
All inputs are finite; a program needn't handle non-finite values.
Results may differ from a plain program's by a relative error of at most 0.0003.
Values sent between devices are 32-bit elements; how exact they have to be, the bound alone decides.
No kernel may reach another device: no remote copies, remote signals or barrier semaphores. Data moves between devices by JAX's collectives and lax.ppermute only.
A program may use at most 128 MiB of HBM per device.

v0:
```python
import jax
import jax.numpy as jnp
from jax import lax
from jax.sharding import PartitionSpec as P

DEGREE = 4


WEIGHTS = (
    -5369.0 / 1800.0,
    12.0 / 7.0,
    -15.0 / 56.0,
    10.0 / 189.0,
    -1.0 / 112.0,
    2.0 / 1925.0,
    -1.0 / 16632.0,
)
LOWER = -4.0
CUTOFF = 1.0
UPPER = 16.0
PRECISE = lax.Precision.HIGHEST


def shifted(array, axis, by):
    peers = lax.axis_size(axis)
    return lax.ppermute(array, axis, [(i, (i + by) % peers) for i in range(peers)])


def padded(array, sides, width):
    for axis, dim in sides:
        peers, length = (lax.axis_size(axis), array.shape[dim])
        up = [(i, (i + 1) % peers) for i in range(peers)]
        down = [(j, i) for i, j in up]
        last = lax.slice_in_dim(array, length - width, length, axis=dim)
        initial = lax.slice_in_dim(array, 0, width, axis=dim)
        before = lax.ppermute(last, axis, up)
        after = lax.ppermute(initial, axis, down)
        array = jnp.concatenate([before, array, after], axis=dim)
    return array


def filter_terms(degree):
    half_span = (UPPER - CUTOFF) / 2.0
    middle = (UPPER + CUTOFF) / 2.0
    sigma_now = half_span / (LOWER - middle)
    sigma_first = sigma_now
    scales = [sigma_now / half_span]
    recall = [0.0]
    for level in range(1, degree):
        sigma_next = 1.0 / (2.0 / sigma_first - sigma_now)
        scales.append(2.0 * sigma_next / half_span)
        recall.append(sigma_now * sigma_next)
        sigma_now = sigma_next
    return (middle, scales, recall)


def second_roll(values, along):
    summed = WEIGHTS[0] * values
    for reach in range(1, 7):
        summed = summed + WEIGHTS[reach] * (
            jnp.roll(values, reach, along) + jnp.roll(values, -reach, along)
        )
    return summed


def second_planes(widened, slab_planes):
    summed = WEIGHTS[0] * widened[6 : 6 + slab_planes]
    for reach in range(1, 7):
        summed = summed + WEIGHTS[reach] * (
            widened[6 + reach : 6 + reach + slab_planes]
            + widened[6 - reach : 6 - reach + slab_planes]
        )
    return summed


def shards(orbitals, potential, projectors, atom_planes, kb_energy):
    slab_planes = orbitals.shape[0]
    orb_here = orbitals.shape[-1]
    extent = slab_planes + 12
    atom_count = atom_planes.shape[0]
    plane_marks = (
        atom_planes[:, :, None] == jnp.arange(extent, dtype=jnp.int32)[None, None, :]
    ).astype(jnp.float32)
    projector_map = jnp.einsum("abe,apbs->apes", plane_marks, projectors, precision=PRECISE)
    map_rows = atom_count * projectors.shape[1]
    projector_map = projector_map.reshape(map_rows, -1)
    energy_col = jnp.tile(kb_energy, atom_count)[:, None]
    middle, scales, recall = filter_terms(DEGREE)
    map_planes = projector_map.reshape(map_rows, extent, -1)
    low_map = map_planes[:, :6].reshape(map_rows, -1)
    high_map = map_planes[:, 6 + slab_planes :].reshape(map_rows, -1)
    map_below = shifted(high_map, "grid", 1)
    map_above = shifted(low_map, "grid", -1)
    rim_shape = (6,) + orbitals.shape[1:]
    previous = orbitals
    current = orbitals
    for level in range(DEGREE):
        widened = padded(current, (("grid", 0),), 6)
        lap = (
            second_planes(widened, slab_planes) + second_roll(current, 1) + second_roll(current, 2)
        )
        local_part = -0.5 * lap + potential[..., None] * current
        correlation = (
            jnp.dot(projector_map, widened.reshape(-1, orb_here), precision=PRECISE) * energy_col
        )
        spread = lax.dot_general(
            projector_map, correlation, (((0,), (0,)), ((), ())), precision=PRECISE
        )
        spread = spread.reshape(widened.shape)
        own_part, low_rim, high_rim, correlation = (
            local_part + spread[6 : 6 + slab_planes],
            spread[:6],
            spread[6 + slab_planes :],
            correlation,
        )
        coef_below = shifted(correlation, "grid", 1)
        coef_above = shifted(correlation, "grid", -1)
        from_below = lax.dot_general(
            map_below, coef_below, (((0,), (0,)), ((), ())), precision=PRECISE
        ).reshape(rim_shape)
        from_above = lax.dot_general(
            map_above, coef_above, (((0,), (0,)), ((), ())), precision=PRECISE
        ).reshape(rim_shape)
        applied = own_part.at[:6].add(from_below).at[slab_planes - 6 :].add(from_above)
        result = scales[level] * (applied - middle * current)
        if level > 0:
            result = result - recall[level] * previous
        previous = current
        current = result
    flattened = current.reshape(-1, orb_here)
    piece = lax.all_gather(current, "band", axis=3, tiled=True)
    gram_part = lax.dot_general(
        flattened, piece.reshape(-1, piece.shape[-1]), (((0,), (0,)), ((), ())), precision=PRECISE
    )
    gram_total = lax.psum(gram_part, "grid")
    cell_count = slab_planes * orbitals.shape[1] * orbitals.shape[2] * lax.axis_size("grid")
    correlation_gram = gram_total * (1.0 / cell_count)
    return (current, correlation_gram)


def solution(mesh):
    return jax.shard_map(
        shards,
        mesh=mesh,
        in_specs=(
            P("grid", None, None, "band"),
            P("grid", None, None),
            P("grid", None, None, None),
            P("grid", None),
            P(),
        ),
        out_specs=(P("grid", None, None, "band"), P("band", None)),
        check_vma=False,
    )
```

profile of v0, /device:TPU:0, one launch (start us, length us, event | category | flops | bytes accessed | tf_op | source)
XLA Modules:
  0.0 527.2 jit_solution(503174751346908071)
XLA Ops:
  7.2 2.7 fusion.330
  9.9 6.0 %collective-permute-start = (f32[6,16,16,128]{3,2,1,0:T(8,128)}, f32[6,16,16,128]{3,2,1,0:T(8,128)}, u32[]{:S(2)}, u32[]{:S(2)}) collective-permute-start(f32[6,16,16,128]{3,2,1,0:T(8,128)} %get-tuple-element.299), channel_id=1, source_target_pairs={{1,0},{2,1},{3,2},{4,3},{5,4},{6,5},{7,6},{0,7},{9,8},{10,9},{11,1... | collective-permute-start | bytes 2359304 | tf_op jit(solution)/shard_map/ppermute | solution.py:37
  18.1 4.7 collective-permute-start.4
  61.5 3.8 fusion.226
  65.3 4.9 collective-permute-start.5
  74.6 14.2 %fusion.105 = f32[12,16,16,128]{3,2,1,0:T(8,128)S(1)} fusion(f32[12,16,16,128]{3,2,1,0:T(8,128)} %bitcast.80, f32[18,16,16,128]{3,2,1,0:T(8,128)S(1)} %get-tuple-element.297, f32[18,16,16,128]{3,2,1,0:T(8,128)S(1)} %constant_dynamic-update-slice_fusion, f32[12,15,16,128]{3,2,1,0:T(8,128)} %get-tuple-element.293, f32[12,1,16,128]{3,2,1,0:T(8,128)} %get-tuple-element.295, ...), kind=kLoop, calls=%fused_computation.176 | loop fusion | flops 33423360 | bytes 61353984 | tf_op jit(solution)/shard_map/add | solution.py:111
  96.6 2.1 fusion.285
  98.7 2.1 fusion.287
  125.0 2.1 fusion.289
  129.2 27.9 %collective-permute-done.6 = f32[6,16,16,128]{3,2,1,0:T(8,128)S(1)} collective-permute-done((f32[6,16,16,128]{3,2,1,0:T(8,128)S(1)}, f32[6,16,16,128]{3,2,1,0:T(8,128)S(1)}, u32[]{:S(2)}, u32[]{:S(2)}) %collective-permute-start.6) | collective-permute-done | bytes 786464 | tf_op jit(solution)/shard_map/ppermute | solution.py:37
  159.7 3.8 fusion.224
  163.5 5.2 collective-permute-start.9
  168.7 19.0 %fusion.71 = f32[12,16,16,128]{3,2,1,0:T(8,128)} fusion(f32[12,16,16,128]{3,2,1,0:T(8,128)} %bitcast.77, f32[12,16,16,128]{3,2,1,0:T(8,128)S(1)} %broadcast_multiply_fusion, f32[6,16,16,128]{3,2,1,0:T(8,128)} %copy-done.8, f32[6,16,16,128]{3,2,1,0:T(8,128)S(1)} %collective-permute-done.6, f32[12,15,16,128]{3,2,1,0:T(8,128)} %get-tuple-element.243, ...), kind=kLoop, calls=%fused_computation.135 | loop fusion | flops 38928384 | bytes 47198208 | tf_op jit(solution)/shard_map/add | solution.py:111
  187.6 2.1 fusion.334
  189.8 2.1 fusion.215
  193.3 2.1 fusion.214
  233.6 26.3 %collective-permute-done.10 = f32[6,16,16,128]{3,2,1,0:T(8,128)S(1)} collective-permute-done((f32[6,16,16,128]{3,2,1,0:T(8,128)S(1)}, f32[6,16,16,128]{3,2,1,0:T(8,128)S(1)}, u32[]{:S(2)}, u32[]{:S(2)}) %collective-permute-start.10) | collective-permute-done | bytes 786464 | tf_op jit(solution)/shard_map/ppermute | solution.py:37
  262.6 3.8 fusion.222
  266.4 4.7 collective-permute-start.13
  271.1 19.0 %fusion.40 = f32[12,16,16,128]{3,2,1,0:T(8,128)} fusion(f32[12,16,16,128]{3,2,1,0:T(8,128)} %bitcast.79, f32[12,16,16,128]{3,2,1,0:T(8,128)S(1)} %multiply_subtract_fusion.2, f32[6,16,16,128]{3,2,1,0:T(8,128)} %copy-done.10, f32[6,16,16,128]{3,2,1,0:T(8,128)S(1)} %collective-permute-done.10, f32[12,15,16,128]{3,2,1,0:T(8,128)} %get-tuple-element.193, ...), kind=kLoop, calls=%fused_computation.104 | loop fusion | flops 38141952 | bytes 44052480 | tf_op jit(solution)/shard_map/add | solution.py:111
  291.5 2.1 fusion.213
  295.1 2.1 fusion.212
  301.0 2.1 fusion.235
  305.1 2.1 fusion.239
  328.9 2.2 collective-permute-start.15
  335.9 25.7 %collective-permute-done.14 = f32[6,16,16,128]{3,2,1,0:T(8,128)S(1)} collective-permute-done((f32[6,16,16,128]{3,2,1,0:T(8,128)S(1)}, f32[6,16,16,128]{3,2,1,0:T(8,128)S(1)}, u32[]{:S(2)}, u32[]{:S(2)}) %collective-permute-start.14) | collective-permute-done | bytes 786464 | tf_op jit(solution)/shard_map/ppermute | solution.py:37
  364.3 3.8 fusion.220
  368.6 4.3 collective-permute-start.17
  372.8 17.9 %fusion.9 = f32[12,16,16,128]{3,2,1,0:T(8,128)S(1)} fusion(f32[12,16,16,128]{3,2,1,0:T(8,128)} %bitcast.78, f32[12,16,16,128]{3,2,1,0:T(8,128)S(1)} %multiply_subtract_fusion.1, f32[6,16,16,128]{3,2,1,0:T(8,128)} %copy-done.9, f32[6,16,16,128]{3,2,1,0:T(8,128)S(1)} %collective-permute-done.14, f32[12,15,16,128]{3,2,1,0:T(8,128)} %get-tuple-element.143, ...), kind=kLoop, calls=%fused_computation.73 | loop fusion | flops 38141952 | bytes 44052480 | tf_op jit(solution)/shard_map/add | solution.py:111
  395.8 44.3 %all-gather.2.cloned.1.call-done = f32[12,16,16,512]{3,2,1,0:T(8,128)} async-done(((f32[12,16,16,128]{3,2,1,0:T(8,128)}), f32[12,16,16,512]{3,2,1,0:T(8,128)}) %all-gather.2.cloned.1.call-update) | async-done | bytes 6291472 | tf_op jit(solution)/shard_map/all_gather | solution.py:131
  440.1 7.4 %convolution_bitcast_fusion = f32[128,512]{1,0:T(8,128)} fusion(f32[12,16,16,128]{3,2,1,0:T(8,128)S(1)} %copy-done.3, f32[12,16,16,512]{3,2,1,0:T(8,128)} %all-gather.2.cloned.1.call-done), kind=kOutput, calls=%fused_computation.340 | convolution fusion | flops 2415919104 | bytes 8126464 | tf_op jit(solution)/shard_map/dot_general | solution.py:132
  447.5 70.7 %all-reduce.2.cloned.1.call-done = f32[128,512]{1,0:T(8,128)} async-done(((f32[128,512]{1,0:T(8,128)}), f32[128,512]{1,0:T(8,128)}) %all-reduce.2.cloned.1.call-update) | async-done | bytes 262160 | tf_op jit(solution)/shard_map/psum | solution.py:135
  (199 shorter events, 169.1 us)
Async XLA Ops:
  7.2 8.8 %copy-start = (f32[4,8,13,256]{3,1,2,0:T(8,128)S(1)}, f32[4,8,13,256]{3,1,2,0:T(8,128)}, u32[]{:S(2)}) copy-start(f32[4,8,13,256]{3,1,2,0:T(8,128)} %param.23) | copy-start | bytes 1277956
  7.2 8.8 %copy-start.18 = (s32[4,13]{1,0:T(4,128)S(1)}, s32[4,13]{1,0:T(4,128)}, u32[]{:S(2)}) copy-start(s32[4,13]{1,0:T(4,128)} %param.24) | copy-start | bytes 628
  7.2 432.9 %all-gather.2.cloned.1.call-start = ((), (), s32[]{:S(2)}) async-start(), calls=%async_computation | async-start | bytes 7864320 | tf_op jit(solution)/shard_map/all_gather | solution.py:131
  9.9 48.2 %collective-permute-start = (f32[6,16,16,128]{3,2,1,0:T(8,128)}, f32[6,16,16,128]{3,2,1,0:T(8,128)}, u32[]{:S(2)}, u32[]{:S(2)}) collective-permute-start(f32[6,16,16,128]{3,2,1,0:T(8,128)} %get-tuple-element.299), channel_id=1, source_target_pairs={{1,0},{2,1},{3,2},{4,3},{5,4},{6,5},{7,6},{0,7},{9,8},{10,9},{11,1... | collective-permute-start | bytes 2359304 | tf_op jit(solution)/shard_map/ppermute | solution.py:37
  15.9 6.9 %copy-start.2 = (f32[12,16,16,128]{3,2,1,0:T(8,128)S(1)}, f32[12,16,16,128]{3,2,1,0:T(8,128)}, u32[]{:S(2)}) copy-start(f32[12,16,16,128]{3,2,1,0:T(8,128)} %param.21) | copy-start | bytes 4718596
  15.9 42.2 %collective-permute-start.1 = (f32[6,16,16,128]{3,2,1,0:T(8,128)}, f32[6,16,16,128]{3,2,1,0:T(8,128)}, u32[]{:S(2)}, u32[]{:S(2)}) collective-permute-start(f32[6,16,16,128]{3,2,1,0:T(8,128)} %get-tuple-element.298), channel_id=1, source_target_pairs={{0,1},{1,2},{2,3},{3,4},{4,5},{5,6},{6,7},{7,0},{8,9},{9,10},{10,1... | collective-permute-start | bytes 2359304 | tf_op jit(solution)/shard_map/ppermute | solution.py:36
  17.4 71.4 %collective-permute-start.2 = (f32[32,1536]{1,0:T(8,128)}, f32[32,1536]{1,0:T(8,128)S(1)}, u32[]{:S(2)}, u32[]{:S(2)}) collective-permute-start(f32[32,1536]{1,0:T(8,128)} %bitcast.29), channel_id=1, source_target_pairs={{0,1},{1,2},{2,3},{3,4},{4,5},{5,6},{6,7},{7,0},{8,9},{9,10},{10,1... | collective-permute-start | bytes 589832 | tf_op jit(solution)/shard_map/ppermute | solution.py:26
  18.1 72.3 %collective-permute-start.4 = (f32[32,1536]{1,0:T(8,128)}, f32[32,1536]{1,0:T(8,128)S(1)}, u32[]{:S(2)}, u32[]{:S(2)}) collective-permute-start(f32[32,1536]{1,0:T(8,128)} %bitcast.31), channel_id=1, source_target_pairs={{0,7},{1,0},{2,1},{3,2},{4,3},{5,4},{6,5},{7,6},{8,15},{9,8},{10,9... | collective-permute-start | bytes 589832 | tf_op jit(solution)/shard_map/ppermute | solution.py:26
  49.0 4.1 copy-start.16
  50.8 3.2 copy-start.19
  65.3 23.5 %collective-permute-start.3 = (f32[32,128]{1,0:T(8,128)S(1)}, f32[32,128]{1,0:T(8,128)S(1)}, u32[]{:S(2)}, u32[]{:S(2)}) collective-permute-start(f32[32,128]{1,0:T(8,128)S(1)} %convolution_multiply_fusion.3), channel_id=1, source_target_pairs={{0,1},{1,2},{2,3},{3,4},{4,5},{5,6},{6,7},{7,0},{8,9},{9,10},{10,1... | collective-permute-start | bytes 49160 | tf_op jit(solution)/shard_map/ppermute | solution.py:26
  65.3 25.2 %collective-permute-start.5 = (f32[32,128]{1,0:T(8,128)S(1)}, f32[32,128]{1,0:T(8,128)S(1)}, u32[]{:S(2)}, u32[]{:S(2)}) collective-permute-start(f32[32,128]{1,0:T(8,128)S(1)} %convolution_multiply_fusion.3), channel_id=1, source_target_pairs={{0,7},{1,0},{2,1},{3,2},{4,3},{5,4},{6,5},{7,6},{8,15},{9,8},{10,9... | collective-permute-start | bytes 49160 | tf_op jit(solution)/shard_map/ppermute | solution.py:26
  70.2 3.0 copy-start.15
  88.8 201.3 %copy-start.13 = (f32[32,1536]{1,0:T(8,128)}, f32[32,1536]{1,0:T(8,128)S(1)}, u32[]{:S(2)}) copy-start(f32[32,1536]{1,0:T(8,128)S(1)} %collective-permute-done.2) | copy-start | bytes 589828
  90.5 203.2 %copy-start.11 = (f32[32,1536]{1,0:T(8,128)}, f32[32,1536]{1,0:T(8,128)S(1)}, u32[]{:S(2)}) copy-start(f32[32,1536]{1,0:T(8,128)S(1)} %collective-permute-done.4) | copy-start | bytes 589828
  122.3 34.7 %collective-permute-start.6 = (f32[6,16,16,128]{3,2,1,0:T(8,128)S(1)}, f32[6,16,16,128]{3,2,1,0:T(8,128)S(1)}, u32[]{:S(2)}, u32[]{:S(2)}) collective-permute-start(f32[6,16,16,128]{3,2,1,0:T(8,128)S(1)} %get-tuple-element.247), channel_id=1, source_target_pairs={{1,0},{2,1},{3,2},{4,3},{5,4},{6,5},{7,6},{0,7},{9,8},{10,9},{11,1... | collective-permute-start | bytes 2359304 | tf_op jit(solution)/shard_map/ppermute | solution.py:37
  122.3 34.7 %collective-permute-start.7 = (f32[6,16,16,128]{3,2,1,0:T(8,128)S(1)}, f32[6,16,16,128]{3,2,1,0:T(8,128)S(1)}, u32[]{:S(2)}, u32[]{:S(2)}) collective-permute-start(f32[6,16,16,128]{3,2,1,0:T(8,128)S(1)} %get-tuple-element.246), channel_id=1, source_target_pairs={{0,1},{1,2},{2,3},{3,4},{4,5},{5,6},{6,7},{7,0},{8,9},{9,10},{10,1... | collective-permute-start | bytes 2359304 | tf_op jit(solution)/shard_map/ppermute | solution.py:36
  163.5 24.1 %collective-permute-start.8 = (f32[32,128]{1,0:T(8,128)S(1)}, f32[32,128]{1,0:T(8,128)}, u32[]{:S(2)}, u32[]{:S(2)}) collective-permute-start(f32[32,128]{1,0:T(8,128)S(1)} %convolution_multiply_fusion.2), channel_id=1, source_target_pairs={{0,1},{1,2},{2,3},{3,4},{4,5},{5,6},{6,7},{7,0},{8,9},{9,10},{10,1... | collective-permute-start | bytes 49160 | tf_op jit(solution)/shard_map/ppermute | solution.py:26
  163.5 28.4 %collective-permute-start.9 = (f32[32,128]{1,0:T(8,128)S(1)}, f32[32,128]{1,0:T(8,128)S(1)}, u32[]{:S(2)}, u32[]{:S(2)}) collective-permute-start(f32[32,128]{1,0:T(8,128)S(1)} %convolution_multiply_fusion.2), channel_id=1, source_target_pairs={{0,7},{1,0},{2,1},{3,2},{4,3},{5,4},{6,5},{7,6},{8,15},{9,8},{10,9... | collective-permute-start | bytes 49160 | tf_op jit(solution)/shard_map/ppermute | solution.py:26
  226.7 33.2 %collective-permute-start.10 = (f32[6,16,16,128]{3,2,1,0:T(8,128)S(1)}, f32[6,16,16,128]{3,2,1,0:T(8,128)S(1)}, u32[]{:S(2)}, u32[]{:S(2)}) collective-permute-start(f32[6,16,16,128]{3,2,1,0:T(8,128)S(1)} %get-tuple-element.197), channel_id=1, source_target_pairs={{1,0},{2,1},{3,2},{4,3},{5,4},{6,5},{7,6},{0,7},{9,8},{10,9},{11,1... | collective-permute-start | bytes 2359304 | tf_op jit(solution)/shard_map/ppermute | solution.py:37
  226.9 33.1 %collective-permute-start.11 = (f32[6,16,16,128]{3,2,1,0:T(8,128)S(1)}, f32[6,16,16,128]{3,2,1,0:T(8,128)S(1)}, u32[]{:S(2)}, u32[]{:S(2)}) collective-permute-start(f32[6,16,16,128]{3,2,1,0:T(8,128)S(1)} %get-tuple-element.196), channel_id=1, source_target_pairs={{0,1},{1,2},{2,3},{3,4},{4,5},{5,6},{6,7},{7,0},{8,9},{9,10},{10,1... | collective-permute-start | bytes 2359304 | tf_op jit(solution)/shard_map/ppermute | solution.py:36
  266.4 23.7 %collective-permute-start.12 = (f32[32,128]{1,0:T(8,128)S(1)}, f32[32,128]{1,0:T(8,128)S(1)}, u32[]{:S(2)}, u32[]{:S(2)}) collective-permute-start(f32[32,128]{1,0:T(8,128)S(1)} %convolution_multiply_fusion.1), channel_id=1, source_target_pairs={{0,1},{1,2},{2,3},{3,4},{4,5},{5,6},{6,7},{7,0},{8,9},{9,10},{10,1... | collective-permute-start | bytes 49160 | tf_op jit(solution)/shard_map/ppermute | solution.py:26
  266.4 27.3 %collective-permute-start.13 = (f32[32,128]{1,0:T(8,128)S(1)}, f32[32,128]{1,0:T(8,128)S(1)}, u32[]{:S(2)}, u32[]{:S(2)}) collective-permute-start(f32[32,128]{1,0:T(8,128)S(1)} %convolution_multiply_fusion.1), channel_id=1, source_target_pairs={{0,7},{1,0},{2,1},{3,2},{4,3},{5,4},{6,5},{7,6},{8,15},{9,8},{10,9... | collective-permute-start | bytes 49160 | tf_op jit(solution)/shard_map/ppermute | solution.py:26
  328.9 32.7 %collective-permute-start.14 = (f32[6,16,16,128]{3,2,1,0:T(8,128)S(1)}, f32[6,16,16,128]{3,2,1,0:T(8,128)S(1)}, u32[]{:S(2)}, u32[]{:S(2)}) collective-permute-start(f32[6,16,16,128]{3,2,1,0:T(8,128)S(1)} %get-tuple-element.147), channel_id=1, source_target_pairs={{1,0},{2,1},{3,2},{4,3},{5,4},{6,5},{7,6},{0,7},{9,8},{10,9},{11,1... | collective-permute-start | bytes 2359304 | tf_op jit(solution)/shard_map/ppermute | solution.py:37
  328.9 32.7 %collective-permute-start.15 = (f32[6,16,16,128]{3,2,1,0:T(8,128)S(1)}, f32[6,16,16,128]{3,2,1,0:T(8,128)S(1)}, u32[]{:S(2)}, u32[]{:S(2)}) collective-permute-start(f32[6,16,16,128]{3,2,1,0:T(8,128)S(1)} %get-tuple-element.146), channel_id=1, source_target_pairs={{0,1},{1,2},{2,3},{3,4},{4,5},{5,6},{6,7},{7,0},{8,9},{9,10},{10,1... | collective-permute-start | bytes 2359304 | tf_op jit(solution)/shard_map/ppermute | solution.py:36
  364.3 8.5 %copy-start.17 = (f32[12,16,16]{2,1,0:T(8,128)S(1)}, f32[12,16,16]{2,1,0:T(8,128)}, u32[]{:S(2)}) copy-start(f32[12,16,16]{2,1,0:T(8,128)} %param.22) | copy-start | bytes 36868
  368.1 22.6 %collective-permute-start.16 = (f32[32,128]{1,0:T(8,128)S(1)}, f32[32,128]{1,0:T(8,128)S(1)}, u32[]{:S(2)}, u32[]{:S(2)}) collective-permute-start(f32[32,128]{1,0:T(8,128)S(1)} %convolution_multiply_fusion), channel_id=1, source_target_pairs={{0,1},{1,2},{2,3},{3,4},{4,5},{5,6},{6,7},{7,0},{8,9},{9,10},{10,1... | collective-permute-start | bytes 49160 | tf_op jit(solution)/shard_map/ppermute | solution.py:26
  368.6 23.8 %collective-permute-start.17 = (f32[32,128]{1,0:T(8,128)S(1)}, f32[32,128]{1,0:T(8,128)S(1)}, u32[]{:S(2)}, u32[]{:S(2)}) collective-permute-start(f32[32,128]{1,0:T(8,128)S(1)} %convolution_multiply_fusion), channel_id=1, source_target_pairs={{0,7},{1,0},{2,1},{3,2},{4,3},{5,4},{6,5},{7,6},{8,15},{9,8},{10,9... | collective-permute-start | bytes 49160 | tf_op jit(solution)/shard_map/ppermute | solution.py:26
  372.8 17.9 %copy-start.14 = (f32[32,1536]{1,0:T(8,128)S(1)}, f32[32,1536]{1,0:T(8,128)}, u32[]{:S(2)}) copy-start(f32[32,1536]{1,0:T(8,128)} %copy-done.13) | copy-start | bytes 589828
  395.5 44.7 %copy-start.3 = (f32[12,16,16,128]{3,2,1,0:T(8,128)S(1)}, f32[12,16,16,128]{3,2,1,0:T(8,128)}, u32[]{:S(2)}) copy-start(f32[12,16,16,128]{3,2,1,0:T(8,128)} %multiply_subtract_fusion) | copy-start | bytes 4718596
  395.5 122.7 %all-reduce.2.cloned.1.call-start = ((), (), s32[]{:S(2)}) async-start(), calls=%async_computation.1 | async-start | bytes 524288 | tf_op jit(solution)/shard_map/psum | solution.py:135
  440.1 79.8 %copy-start.1 = (f32[4,8,13,256]{3,1,2,0:T(8,128)S(1)}, f32[4,8,13,256]{3,1,2,0:T(8,128)}, u32[]{:S(2)}) copy-start(f32[4,8,13,256]{3,1,2,0:T(8,128)} %param.23) | copy-start | bytes 1277956
  (8 other events, 13.7 us)
Sparse Core Ops, SparseCore 0:
  395.6 44.4 all-gather.1
  447.7 70.5 all-reduce.1
where the time goes:
time: 535 us; the launch traced here: 527 us
  waiting for transfers between devices  195 us (36%)
  local copies, waits for them, and re-layouts  148 us (28%)
  other arithmetic  89.9 us (17%)
  matrix products  42 us (8%)
  starting transfers between devices  37 us (7%)
  between operations  15 us (3%)
    slice x96, local copies, waits for them, and re-layouts, second_roll(): jnp.roll(values, -reach, along)  137 us
    ppermute x4, waiting for transfers between devices, padded(): after = lax.ppermute(initial, axis, down)  80 us
    psum x1, waiting for transfers between devices, shards(): gram_total = lax.psum(gram_part, 'grid')  70.7 us
    add x4, other arithmetic, shards(): local_part + spread[6:6 + slab_planes]  70 us
    all_gather x1, waiting for transfers between devices, shards(): piece = lax.all_gather(current, 'band', axis=3, tiled=True)  44.3 us
    ppermute x10, starting transfers between devices, shifted(): lax.ppermute(array, axis, [(i, (i + by) % peers) for i in range(peers)])  24.3 us
    dot_general x4, matrix products, shards(): lax.dot_general(projector_map, correlation, (((0,), (0,)), ((), ())), pre...  15.1 us
  transfers between devices with their start and end apart: 20, of which 5 were waited for; matrix products, arithmetic and copies ran while one was open for 27% of the time, Pallas kernels for 0%

commit v1 on v0

v1 whole, which is shorter than its diff:
```python
import functools

import jax
import jax.numpy as jnp
import ml_dtypes
import numpy as np
from jax import lax
from jax.experimental import pallas as pl
from jax.experimental.pallas import tpu as pltpu
from jax.sharding import PartitionSpec as P

DEGREE = 4
REACH = 6
LANES = 128
QUARTER = 32

WEIGHTS = (
    -5369.0 / 1800.0,
    12.0 / 7.0,
    -15.0 / 56.0,
    10.0 / 189.0,
    -1.0 / 112.0,
    2.0 / 1925.0,
    -1.0 / 16632.0,
)
LOWER = -4.0
CUTOFF = 1.0
UPPER = 16.0
F32 = jnp.float32
BF16 = jnp.bfloat16


def filter_terms(degree):
    half_span = (UPPER - CUTOFF) / 2.0
    middle = (UPPER + CUTOFF) / 2.0
    sigma_now = half_span / (LOWER - middle)
    sigma_first = sigma_now
    scales = [sigma_now / half_span]
    recall = [0.0]
    for level in range(1, degree):
        sigma_next = 1.0 / (2.0 / sigma_first - sigma_now)
        scales.append(2.0 * sigma_next / half_span)
        recall.append(sigma_now * sigma_next)
        sigma_now = sigma_next
    return (middle, scales, recall)


def plane_matrix(ny, nz):
    def ring(n):
        m = np.zeros((n, n))
        for i in range(n):
            m[i, i] += WEIGHTS[0]
            for r in range(1, REACH + 1):
                m[i, (i + r) % n] += WEIGHTS[r]
                m[i, (i - r) % n] += WEIGHTS[r]
        return m

    full = -0.5 * (np.kron(ring(ny), np.eye(nz)) + np.kron(np.eye(ny), ring(nz)))
    high = full.astype(ml_dtypes.bfloat16)
    low = (full - high.astype(np.float64)).astype(ml_dtypes.bfloat16)
    return high, low


def halves(value):
    high = value.astype(BF16)
    return high, (value - high.astype(F32)).astype(BF16)


def dot3(a, b):
    def dot(p, q):
        return lax.dot_general(p, q, (((1,), (0,)), ((), ())), preferred_element_type=F32)

    return dot(a[0], b[0]) + (dot(a[0], b[1]) + dot(a[1], b[0]))


def lane_ids(shape):
    return lax.broadcasted_iota(jnp.int32, shape, len(shape) - 1)


def turn(value, shift):
    if isinstance(shift, int):
        shift = shift % LANES
        if shift == 0:
            return value
    else:
        shift = lax.rem(shift + 8 * LANES, LANES)
    return pltpu.roll(value, shift, axis=value.ndim - 1)


def pack_kernel(chunk, y_ref, x_ref, out_ref):
    y = y_ref[0]
    group = lane_ids((x_ref.shape[1], LANES)) // QUARTER
    for r in range(3):
        row = None
        for slot, plane in enumerate((r, r + 6, r + 3, r + 9)):
            piece = turn(x_ref[plane], QUARTER * slot - 64 - QUARTER * chunk + 64 * y)
            row = piece if row is None else jnp.where(group == slot, piece, row)
        out_ref[r] = row


def rim_pack(row, out_ref, r, source):
    part = row.shape[0] // 4
    group = lane_ids((part, LANES)) // QUARTER
    packed = None
    for j in range(4):
        piece = turn(row[j * part : (j + 1) * part], QUARTER * (j - source))
        packed = piece if packed is None else jnp.where(group == j, piece, packed)
    out_ref[pl.ds(r * part, part), :] = packed


def assemble_kernel(chunk, y_ref, x_ref, got_ref, v_ref, up_ref, down_ref):
    y = y_ref[0]
    group = lane_ids((x_ref.shape[1], LANES)) // QUARTER
    for r in range(6):
        first = turn(x_ref[r], -QUARTER * chunk)
        second = turn(x_ref[r + 6], QUARTER - QUARTER * chunk)
        other = turn(got_ref[r % 3], 64 * (1 - y) if r < 3 else 64 * y)
        row = jnp.where(group == 2 * y, first, jnp.where(group == 2 * y + 1, second, other))
        v_ref[r] = row
        rim_pack(row, up_ref, r, 3)
        rim_pack(row, down_ref, r, 0)


def collapse(blocks):
    group = lane_ids((32, LANES)) // QUARTER

    def block(i, s, target):
        b = 2 * i + s
        return turn(blocks[32 * b : 32 * b + 32], QUARTER * (target - i))

    low = block(0, 0, 0) + block(1, 0, 0) + block(2, 0, 0)
    high = block(1, 1, 1) + block(2, 1, 1) + block(3, 1, 1)
    below, above = block(0, 1, 2), block(3, 0, 3)
    return jnp.where(
        group == 0, low, jnp.where(group == 1, high, jnp.where(group == 2, below, above))
    )


def coef_kernel(v_ref, mh_ref, ml_ref, out_ref):
    total = None
    for r in range(6):
        term = dot3((mh_ref[r], ml_ref[r]), halves(v_ref[r]))
        total = term if total is None else total + term
    out_ref[...] = collapse(total)


def level_kernel(
    scale, recall, first, last, *refs
):
    refs = list(refs)
    v_ref = refs.pop(0)
    prev_ref = None if first else refs.pop(0)
    below_ref, above_ref = refs.pop(0), refs.pop(0)
    if first:
        below_coef, above_coef = refs.pop(0), refs.pop(0)
    own_ref, kb_ref, ch_ref, cl_ref, th_ref, tl_ref, pot_ref = refs[:7]
    refs = refs[7:]
    if last:
        y_ref, out_ref, send_ref, ext = refs
    else:
        mh_ref, ml_ref, out_ref, up_ref, down_ref, coef_ref, ext = refs
    cells = v_ref.shape[1]
    part = cells // 4
    rim = 6 * part
    group = lane_ids((cells, LANES)) // QUARTER
    part_group = lane_ids((part, LANES)) // QUARTER
    cg = lane_ids((32, LANES)) // QUARTER
    from_below = below_coef[...] if first else below_ref[pl.ds(rim, 32), :]
    from_above = above_coef[...] if first else above_ref[pl.ds(rim, 32), :]
    total = own_ref[...] + jnp.where(cg % 2 == 0, turn(from_below, 32), turn(from_above, -32))
    total = total * kb_ref[...]
    rows = []
    for i, s, source in (
        (0, 0, 0), (0, 1, 2), (1, 0, 0), (1, 1, 1), (2, 0, 0), (2, 1, 1), (3, 0, 3), (3, 1, 1),
    ):
        rows.append(jnp.where(cg == i, turn(total, QUARTER * (i - source)), 0.0))
    spread = halves(jnp.concatenate(rows, axis=0))
    for r in range(6):
        row = v_ref[r]
        ext[6 + r] = row
        before, after = turn(row, QUARTER), turn(row, -QUARTER)
        low, high = below_ref[pl.ds(r * part, part), :], above_ref[pl.ds(r * part, part), :]
        for j in range(4):
            cut = slice(j * part, (j + 1) * part)
            ext[r, cut] = jnp.where(part_group == 0, turn(low, -QUARTER * j), before[cut])
            ext[12 + r, cut] = jnp.where(part_group == 3, turn(high, 96 - QUARTER * j), after[cut])
    coef = None
    results = []
    for r in range(6):
        row = ext[6 + r]
        value = dot3((ch_ref[...], cl_ref[...]), halves(row))
        value = value + dot3((th_ref[r], tl_ref[r]), spread)
        value = value + pot_ref[r] * row
        for k in range(1, REACH + 1):
            value = value + (-0.5 * WEIGHTS[k]) * (ext[6 + r + k] + ext[6 + r - k])
        value = scale * value
        if not first:
            value = value - recall * prev_ref[r]
        out_ref[r] = value
        if last:
            results.append(value)
        else:
            rim_pack(value, up_ref, r, 3)
            rim_pack(value, down_ref, r, 0)
            term = dot3((mh_ref[r], ml_ref[r]), halves(value))
            coef = term if coef is None else coef + term
    if last:
        y = y_ref[0]
        for r in range(3):
            one = turn(out_ref[r], 64 * (1 - y))
            two = turn(out_ref[r + 3], 64 * y)
            send_ref[r] = jnp.where(group < 2, one, two)
    else:
        packed = collapse(coef)
        coef_ref[...] = packed
        up_ref[pl.ds(rim, 32), :] = packed
        down_ref[pl.ds(rim, 32), :] = packed


def unpack_kernel(yx_ref, v0_ref, v1_ref, r0_ref, r1_ref, out_ref, keep_ref, send_ref):
    y, x = yx_ref[0], yx_ref[1]
    group = lane_ids((v0_ref.shape[1], LANES)) // QUARTER
    for half in range(2):
        for r in range(6):
            row = None
            for k, (v_ref, r_ref) in enumerate(((v0_ref, r0_ref), (v1_ref, r1_ref))):
                own = turn(v_ref[r], QUARTER * (k - half))
                got = turn(
                    r_ref[r % 3],
                    64 * (1 - y) + QUARTER * (k - half) - (0 if r < 3 else 64),
                )
                mine = jnp.where(group == 2 * y + k, own, got)
                row = mine if k == 0 else jnp.where(group % 2 == k, mine, row)
            out_ref[6 * half + r] = row

    keep_ref[...] = out_ref[pl.ds(6 * x, 6)]
    send_ref[...] = out_ref[pl.ds(6 * (1 - x), 6)]


def gram_kernel(own_ref, xp_ref, sib_ref, sibxp_ref, keep_ref, send_ref):
    def dot(p, q):
        return lax.dot_general(p, q, (((0,), (0,)), ((), ())), preferred_element_type=F32)

    parts = [halves(ref[...]) for ref in (own_ref, xp_ref, sib_ref, sibxp_ref)]
    high = jnp.concatenate([p[0] for p in parts], axis=1)
    low = jnp.concatenate([p[1] for p in parts], axis=1)
    left_high, left_low = high[:, :256], low[:, :256]
    total = dot(left_high, high) + (dot(left_high, low) + dot(left_low, high))
    keep_ref[...] = total[:128]
    for j, source in enumerate((1, 0, 3, 2)):
        send_ref[:, j * 128 : (j + 1) * 128] = total[128:, source * 128 : (source + 1) * 128]


def order_kernel(factor, b_ref, keep_ref, got_ref, out_ref):
    b = b_ref[0]
    for j, flip in enumerate((0, 2, 1, 3)):
        cut = slice(j * 128, (j + 1) * 128)
        block = (keep_ref[:, cut] + got_ref[:, cut]) * factor
        target = pl.multiple_of(lax.bitwise_xor(b, flip) * 128, 128)
        out_ref[:, pl.ds(target, 128)] = block


def dense_kernel(yc_ref, planes_ref, proj_ref, e_ref, part_ref, rim_ref):
    y, c = yc_ref[0], yc_ref[1]
    e_ref[...] = jnp.zeros_like(e_ref)
    atoms, count, span, _ = proj_ref.shape
    for a in range(atoms):
        for b in range(span):
            plane = planes_ref[a, b]
            for p in range(count):
                at = (plane, pl.ds(a * count + p, 1), slice(None))
                e_ref[at] = e_ref[at] + proj_ref[a, p, pl.ds(b, 1), :]
    rows = pl.ds(pl.multiple_of(16 * c, 16), 16)
    part_ref[...] = e_ref[pl.ds(6 * (1 - y), 18), rows, :]
    rim_ref[...] = e_ref[pl.ds(18 * y, 6), rows, :]


def maps_kernel(
    yc_ref, e_ref, part_ref, part2_ref, a_ref, a2_ref, b_ref, b2_ref,
    mh_ref, ml_ref, th_ref, tl_ref,
):
    y, c = yc_ref[0], yc_ref[1]

    def whole(mine, other):
        first = jnp.where(c == 0, mine, other)
        second = jnp.where(c == 0, other, mine)
        return jnp.concatenate([first, second], axis=0)

    for r in range(6):
        one, two = whole(a_ref[r], a2_ref[r]), whole(b_ref[r], b2_ref[r])
        below, above = jnp.where(y == 1, one, two), jnp.where(y == 1, two, one)
        low = [
            jnp.where(
                y == 0, e_ref[6 + 6 * i + r], whole(part_ref[6 * i + r], part2_ref[6 * i + r])
            )
            for i in range(3)
        ]
        high = [
            jnp.where(y == 1, e_ref[6 * i + r], whole(part_ref[6 * i + r], part2_ref[6 * i + r]))
            for i in range(3)
        ]
        block = jnp.concatenate(
            [low[0], below, low[1], high[0], low[2], high[1], above, high[2]], axis=0
        )
        mh_ref[r], ml_ref[r] = halves(block)
        th_ref[r], tl_ref[r] = halves(block.T)


SMEM = pl.BlockSpec(memory_space=pltpu.SMEM)
VMEM = pl.BlockSpec(memory_space=pltpu.VMEM)


def call(kernel, out, scalars, arrays, scratch=(), flops=0):
    moved = sum(a.size * a.dtype.itemsize for a in arrays) + sum(
        int(np.prod(o.shape)) * o.dtype.itemsize for o in out
    )
    return pl.pallas_call(
        kernel,
        out_shape=out,
        in_specs=[SMEM] * len(scalars) + [VMEM] * len(arrays),
        out_specs=[VMEM] * len(out),
        scratch_shapes=list(scratch),
        compiler_params=pltpu.CompilerParams(vmem_limit_bytes=48 * 1024 * 1024),
        cost_estimate=pl.CostEstimate(flops=flops, bytes_accessed=moved, transcendentals=0),
    )(*scalars, *arrays)


def f32(*shape):
    return jax.ShapeDtypeStruct(shape, F32)


def bf16(*shape):
    return jax.ShapeDtypeStruct(shape, BF16)


def shards(orbitals, potential, projectors, atom_planes, kb_energy):
    slab, ny, nz, orb_here = orbitals.shape
    cells = ny * nz
    peers = lax.axis_size("grid")
    bands = lax.axis_size("band")
    g, b = lax.axis_index("grid"), lax.axis_index("band")
    y, c, x = lax.rem(g, 2), lax.rem(b, 2), b // 2
    y1 = y.reshape(1).astype(jnp.int32)
    b1 = b.reshape(1).astype(jnp.int32)
    yc = jnp.stack([y, c]).astype(jnp.int32)
    yx = jnp.stack([y, x]).astype(jnp.int32)

    def move(array, axis, target):
        size = lax.axis_size(axis)
        return lax.ppermute(array, axis, [(i, target(i) % size) for i in range(size)])

    def partner(array):
        return move(array, "grid", lambda i: i ^ 1)

    def up(array):
        return move(array, "grid", lambda i: i + 2)

    def down(array):
        return move(array, "grid", lambda i: i - 2)

    def sibling(array):
        return move(array, "band", lambda i: i ^ 1)

    def across(array):
        return move(array, "band", lambda i: i ^ 2)

    field = orbitals.reshape(slab, cells, orb_here)
    rim_rows = 6 * (cells // 4)
    middle, scales, recall = filter_terms(DEGREE)

    sent = [
        call(functools.partial(pack_kernel, k), [f32(3, cells, LANES)], [y1], [field])[0]
        for k in range(2)
    ]
    other = [partner(s) for s in sent]

    dense, part, rim = call(
        dense_kernel,
        [f32(24, 32, cells), f32(18, 16, cells), f32(6, 16, cells)],
        [yc, atom_planes],
        [projectors],
    )
    part = partner(part)
    rim_a = move(rim, "grid", lambda i: i + 2 if i % 2 else i - 2)
    rim_b = move(rim, "grid", lambda i: i + 1 if i % 2 else i - 1)
    mh, ml, th, tl = call(
        maps_kernel,
        [bf16(6, 256, cells)] * 2 + [bf16(6, cells, 256)] * 2,
        [yc],
        [dense, part, sibling(part), rim_a, sibling(rim_a), rim_b, sibling(rim_b)],
    )
    pot_other = partner(potential.reshape(slab, cells))
    pot_own = potential.reshape(slab, cells)
    pot = jnp.where(
        y == 0,
        jnp.concatenate([pot_own, pot_other]),
        jnp.concatenate([pot_other, pot_own]),
    )
    pot = pot - (middle + 0.5 * WEIGHTS[0])
    pot = jnp.repeat(pot.reshape(4, 6, cells).transpose(1, 2, 0), QUARTER, axis=-1)
    kb = jnp.broadcast_to(jnp.tile(kb_energy, 4)[:, None], (32, LANES))
    ch, cl = (jnp.asarray(m) for m in plane_matrix(ny, nz))

    chunks = []
    for k in range(2):
        v, rim_up, rim_down = call(
            functools.partial(assemble_kernel, k),
            [f32(6, cells, LANES), f32(rim_rows, LANES), f32(rim_rows, LANES)],
            [y1],
            [field, other[k]],
        )
        chunks.append(dict(v=v, prev=None, below=up(rim_up), above=down(rim_down)))
    for s in chunks:
        s["coef"] = call(coef_kernel, [f32(32, LANES)], [], [s["v"], mh, ml])[0]
        s["below_coef"], s["above_coef"] = up(s["coef"]), down(s["coef"])

    flops = 2 * 6 * 256 * 256 * 128
    for level in range(DEGREE):
        first, last = level == 0, level == DEGREE - 1
        for s in chunks:
            arrays = [s["v"]]
            if not first:
                arrays.append(s["prev"])
            arrays += [s["below"], s["above"]]
            if first:
                arrays += [s["below_coef"], s["above_coef"]]
            arrays += [s["coef"], kb, ch, cl, th, tl, pot]
            out = [f32(6, cells, LANES)]
            if last:
                out += [f32(3, cells, LANES)]
            else:
                arrays += [mh, ml]
                out += [f32(rim_rows + 32, LANES)] * 2 + [f32(32, LANES)]
            kernel = functools.partial(level_kernel, scales[level], recall[level], first, last)
            if last:
                order = len(arrays)
                made = pl.pallas_call(
                    kernel,
                    out_shape=out,
                    in_specs=[VMEM] * order + [SMEM],
                    out_specs=[VMEM] * 2,
                    scratch_shapes=[pltpu.VMEM((18, cells, LANES), F32)],
                    compiler_params=pltpu.CompilerParams(vmem_limit_bytes=48 * 1024 * 1024),
                    cost_estimate=pl.CostEstimate(
                        flops=6 * flops, bytes_accessed=8 << 20, transcendentals=0
                    ),
                )(*arrays, y1)
                s["prev"], s["v"] = s["v"], made[0]
                s["back"] = partner(made[1])
            else:
                made = call(
                    kernel, out, [], arrays, [pltpu.VMEM((18, cells, LANES), F32)], 9 * flops
                )
                s["prev"], s["v"], s["coef"] = s["v"], made[0], made[3]
                s["below"], s["above"] = up(made[1]), down(made[2])

    filtered, keep, send = call(
        unpack_kernel,
        [f32(slab, cells, LANES)] + [f32(6, cells, LANES)] * 2,
        [yx],
        [chunks[0]["v"], chunks[1]["v"], chunks[0]["back"], chunks[1]["back"]],
    )
    sib = sibling(keep)
    xp = across(send)
    sibxp = sibling(xp)
    flat = [a.reshape(6 * cells, LANES) for a in (keep, xp, sib, sibxp)]
    mine, theirs = call(
        gram_kernel, [f32(128, bands * 128)] * 2, [], flat, flops=6 * 6 * cells * 256 * 512
    )
    total = call(
        functools.partial(order_kernel, 1.0 / (slab * cells * peers)),
        [f32(128, bands * 128)],
        [b1],
        [mine, across(theirs)],
    )[0]
    pieces = total.reshape(peers, 128 // peers, bands * 128)
    pieces = lax.all_to_all(pieces, "grid", 0, 0)
    piece = jnp.broadcast_to(jnp.sum(pieces, axis=0, keepdims=True), pieces.shape)
    gram = lax.all_to_all(piece, "grid", 0, 0).reshape(128, bands * 128)
    return (filtered.reshape(orbitals.shape), gram)


def solution(mesh):
    return jax.shard_map(
        shards,
        mesh=mesh,
        in_specs=(
            P("grid", None, None, "band"),
            P("grid", None, None),
            P("grid", None, None, None),
            P("grid", None),
            P(),
        ),
        out_specs=(P("grid", None, None, "band"), P("band", None)),
        check_vma=False,
    )
```

time: 535 us -> 197 us (0.37); the launches traced: 527 us -> 196 us
  waiting for transfers between devices: 195 us -> 47.4 us
  local copies, waits for them, and re-layouts: 148 us -> 20.6 us
  other arithmetic: 89.9 us -> 0.18 us
  Pallas kernels: 0 us -> 48.1 us
  matrix products: 42 us -> 0 us
  blocking collectives: 0 us -> 23 us
  starting transfers between devices: 37 us -> 55.7 us
  between operations: 15 us -> 1.03 us
    slice x101 -> x0, local copies, waits for them, and re-layouts: 140 us -> none  [the longest x96 137 us: second_roll(): jnp.roll(values, -reach, along)]
    psum x1 -> x0, waiting for transfers between devices: 70.7 us -> none  [shards(): gram_total = lax.psum(gram_part, 'grid')]
    add x4 -> x0, other arithmetic: 70 us -> none  [shards(): local_part + spread[6:6 + slab_planes]]
    pallas_call x0 -> x19, Pallas kernels: none -> 48.1 us  [the longest x17 42.3 us: call(): pl.pallas_call(kernel, out_shape=out, in_specs=[SMEM] * len(scalars) + [V...]
    all_gather x1 -> x0, waiting for transfers between devices: 44.3 us -> none  [shards(): piece = lax.all_gather(current, 'band', axis=3, tiled=True)]
    dot_general x18 -> x0, matrix products: 42 us -> none  [the longest x4 15.1 us: shards(): lax.dot_general(projector_map, correlation, (((0,), (0,)), ((), ())), pre...]
    ppermute x18 -> x35, waiting for transfers between devices: 80 us -> 47.4 us  [move(): lax.ppermute(array, axis, [(i, target(i) % size) for i in range(size)])]
    all_to_all x0 -> x2, blocking collectives: none -> 23 us  [the longest x1 11.9 us: shards(): gram = lax.all_to_all(piece, 'grid', 0, 0).reshape(128, bands * 128)]
  transfers between devices with their start and end apart: 20 -> 35, of which waited for: 5 -> 13; matrix products, arithmetic and copies ran while one was open for 27% -> 1% of each run, Pallas kernels for 0% -> 22%
where the time goes in v1:
time: 197 us; the launch traced here: 196 us
  starting transfers between devices  55.7 us (28%)
  Pallas kernels  48.1 us (24%)
  waiting for transfers between devices  47.4 us (24%)
  blocking collectives  23 us (12%)
  local copies, waits for them, and re-layouts  20.6 us (10%)
    ppermute x35, starting transfers between devices, move(): lax.ppermute(array, axis, [(i, target(i) % size) for i in range(size)])  55.7 us
    ppermute x35, waiting for transfers between devices, move(): lax.ppermute(array, axis, [(i, target(i) % size) for i in range(size)])  47.4 us
    pallas_call x17, Pallas kernels, call(): pl.pallas_call(kernel, out_shape=out, in_specs=[SMEM] * len(scalars) + [V...  42.3 us
    unnamed x58, local copies, waits for them, and re-layouts  18 us
    all_to_all x1, blocking collectives, shards(): gram = lax.all_to_all(piece, 'grid', 0, 0).reshape(128, bands * 128)  11.9 us
    all_to_all x1, blocking collectives, shards(): pieces = lax.all_to_all(pieces, 'grid', 0, 0)  11.1 us
    pallas_call x2, Pallas kernels, shards(): pl.pallas_call(kernel, out_shape=out, in_specs=[VMEM] * order + [SMEM], o...  5.77 us
  transfers between devices with their start and end apart: 35, of which 13 were waited for; matrix products, arithmetic and copies ran while one was open for 1% of the time, Pallas kernels for 22%

profile of v1, /device:TPU:0, one launch (start us, length us, event | category | flops | bytes accessed | tf_op | source)
XLA Modules:
  0.0 195.9 jit_solution(10374664677373499684)
XLA Ops:
  4.5 3.0 %collective-permute-start.3 = (f32[18,16,256]{2,1,0:T(8,128)S(1)}, f32[18,16,256]{2,1,0:T(8,128)S(1)}, u32[]{:S(2)}, u32[]{:S(2)}) collective-permute-start(f32[18,16,256]{2,1,0:T(8,128)S(1)} %get-tuple-element.52), channel_id=1, source_target_pairs={{0,1},{1,0},{2,3},{3,2},{4,5},{5,4},{6,7},{7,6},{8,9},{9,8},{10,11... | collective-permute-start | bytes 884744 | tf_op jit(solution)/shard_map/ppermute | solution.py:350
  9.9 2.1 %collective-permute-start.18 = (f32[3,256,128]{2,1,0:T(8,128)S(1)}, f32[3,256,128]{2,1,0:T(8,128)S(1)}, u32[]{:S(2)}, u32[]{:S(2)}) collective-permute-start(f32[3,256,128]{2,1,0:T(8,128)S(1)} %shard_map.95), channel_id=1, source_target_pairs={{0,1},{1,0},{2,3},{3,2},{4,5},{5,4},{6,7},{7,6},{8,9},{9,8},{10,11... | collective-permute-start | bytes 1179656 | tf_op jit(solution)/shard_map/ppermute | solution.py:350
  12.0 3.3 %collective-permute-done.3.part_ref = f32[18,16,256]{2,1,0:T(8,128)S(1)} collective-permute-done((f32[18,16,256]{2,1,0:T(8,128)S(1)}, f32[18,16,256]{2,1,0:T(8,128)S(1)}, u32[]{:S(2)}, u32[]{:S(2)}) %collective-permute-start.3) | collective-permute-done | bytes 294944 | tf_op jit(solution)/shard_map/ppermute | solution.py:350
  15.3 4.1 %collective-permute-start.5 = (f32[6,16,256]{2,1,0:T(8,128)S(1)}, f32[6,16,256]{2,1,0:T(8,128)S(1)}, u32[]{:S(2)}, u32[]{:S(2)}) collective-permute-start(f32[6,16,256]{2,1,0:T(8,128)S(1)} %get-tuple-element.53), channel_id=1, source_target_pairs={{0,6},{1,3},{2,0},{3,5},{4,2},{5,7},{6,4},{7,1},{8,14},{9,11},{10,... | collective-permute-start | bytes 294920 | tf_op jit(solution)/shard_map/ppermute | solution.py:350
  20.6 4.8 %collective-permute-done.got_ref = f32[3,256,128]{2,1,0:T(8,128)S(1)} collective-permute-done((f32[3,256,128]{2,1,0:T(8,128)S(1)}, f32[3,256,128]{2,1,0:T(8,128)S(1)}, u32[]{:S(2)}, u32[]{:S(2)}) %collective-permute-start) | collective-permute-done | bytes 393248 | tf_op jit(solution)/shard_map/ppermute | solution.py:350
  28.0 2.5 %collective-permute-start.1 = (f32[384,128]{1,0:T(8,128)}, f32[384,128]{1,0:T(8,128)}, u32[]{:S(2)}, u32[]{:S(2)}) collective-permute-start(f32[384,128]{1,0:T(8,128)} %get-tuple-element.49), channel_id=1, source_target_pairs={{0,2},{1,3},{2,4},{3,5},{4,6},{5,7},{6,0},{7,1},{8,10},{9,11},{10,... | collective-permute-start | bytes 589832 | tf_op jit(solution)/shard_map/ppermute | solution.py:350
  31.8 2.0 %collective-permute-start.2 = (f32[384,128]{1,0:T(8,128)}, f32[384,128]{1,0:T(8,128)}, u32[]{:S(2)}, u32[]{:S(2)}) collective-permute-start(f32[384,128]{1,0:T(8,128)} %get-tuple-element.50), channel_id=1, source_target_pairs={{0,6},{1,7},{2,0},{3,1},{4,2},{5,3},{6,4},{7,5},{8,14},{9,15},{10,... | collective-permute-start | bytes 589832 | tf_op jit(solution)/shard_map/ppermute | solution.py:350
  40.9 2.9 %collective-permute-start.20 = (f32[384,128]{1,0:T(8,128)}, f32[384,128]{1,0:T(8,128)}, u32[]{:S(2)}, u32[]{:S(2)}) collective-permute-start(f32[384,128]{1,0:T(8,128)} %get-tuple-element.73), channel_id=1, source_target_pairs={{0,6},{1,7},{2,0},{3,1},{4,2},{5,3},{6,4},{7,5},{8,14},{9,15},{10,... | collective-permute-start | bytes 589832 | tf_op jit(solution)/shard_map/ppermute | solution.py:350
  51.4 3.8 %collective-permute-start.10 = (f32[32,128]{1,0:T(8,128)S(1)}, f32[32,128]{1,0:T(8,128)S(1)}, u32[]{:S(2)}, u32[]{:S(2)}) collective-permute-start(f32[32,128]{1,0:T(8,128)S(1)} %shard_map.90.refs_5_), channel_id=1, source_target_pairs={{0,6},{1,7},{2,0},{3,1},{4,2},{5,3},{6,4},{7,5},{8,14},{9,15},{10,... | collective-permute-start | bytes 49160 | tf_op jit(solution)/shard_map/ppermute | solution.py:350
  60.8 3.8 %collective-permute-start.22 = (f32[32,128]{1,0:T(8,128)S(1)}, f32[32,128]{1,0:T(8,128)S(1)}, u32[]{:S(2)}, u32[]{:S(2)}) collective-permute-start(f32[32,128]{1,0:T(8,128)S(1)} %shard_map.97.refs_5_), channel_id=1, source_target_pairs={{0,6},{1,7},{2,0},{3,1},{4,2},{5,3},{6,4},{7,5},{8,14},{9,15},{10,... | collective-permute-start | bytes 49160 | tf_op jit(solution)/shard_map/ppermute | solution.py:350
  64.7 4.8 %shard_map.91 = (f32[6,256,128]{2,1,0:T(8,128)S(1)}, f32[416,128]{1,0:T(8,128)S(1)}, f32[416,128]{1,0:T(8,128)S(1)}, f32[32,128]{1,0:T(8,128)S(1)}) custom-call(f32[6,256,128]{2,1,0:T(8,128)S(1)} %copy-done.9, f32[384,128]{1,0:T(8,128)} %collective-permute-done.1.refs_1_, f32[384,128]{1,0:T(8,128)} %collective-permute-done.2.refs_2_, ...), custom_call_target="tpu_custom_call" | custom-call | flops 905969664 | bytes 6668288 | tf_op jit(solution)/shard_map/pallas_call | solution.py:317
  69.6 3.8 %collective-permute-start.13 = (f32[416,128]{1,0:T(8,128)S(1)}, f32[416,128]{1,0:T(8,128)S(1)}, u32[]{:S(2)}, u32[]{:S(2)}) collective-permute-start(f32[416,128]{1,0:T(8,128)S(1)} %get-tuple-element.60), channel_id=1, source_target_pairs={{0,6},{1,7},{2,0},{3,1},{4,2},{5,3},{6,4},{7,5},{8,14},{9,15},{10,... | collective-permute-start | bytes 638984 | tf_op jit(solution)/shard_map/ppermute | solution.py:350
  73.4 4.8 %shard_map.98 = (f32[6,256,128]{2,1,0:T(8,128)S(1)}, f32[416,128]{1,0:T(8,128)S(1)}, f32[416,128]{1,0:T(8,128)S(1)}, f32[32,128]{1,0:T(8,128)S(1)}) custom-call(f32[6,256,128]{2,1,0:T(8,128)S(1)} %copy-done.11, f32[384,128]{1,0:T(8,128)} %collective-permute-done.19.refs_1_, f32[384,128]{1,0:T(8,128)} %collective-permute-done.20.refs_2_, ...), custom_call_target="tpu_custom_call" | custom-call | flops 905969664 | bytes 6668288 | tf_op jit(solution)/shard_map/pallas_call | solution.py:317
  78.3 3.8 %collective-permute-start.24 = (f32[416,128]{1,0:T(8,128)S(1)}, f32[416,128]{1,0:T(8,128)S(1)}, u32[]{:S(2)}, u32[]{:S(2)}) collective-permute-start(f32[416,128]{1,0:T(8,128)S(1)} %get-tuple-element.76), channel_id=1, source_target_pairs={{0,6},{1,7},{2,0},{3,1},{4,2},{5,3},{6,4},{7,5},{8,14},{9,15},{10,... | collective-permute-start | bytes 638984 | tf_op jit(solution)/shard_map/ppermute | solution.py:350
  82.2 5.1 %shard_map.92 = (f32[6,256,128]{2,1,0:T(8,128)S(1)}, f32[416,128]{1,0:T(8,128)S(1)}, f32[416,128]{1,0:T(8,128)S(1)}, f32[32,128]{1,0:T(8,128)S(1)}) custom-call(f32[6,256,128]{2,1,0:T(8,128)S(1)} %get-tuple-element.58.refs_0_.refs_1_, f32[6,256,128]{2,1,0:T(8,128)S(1)} %copy-done.9, f32[416,128]{1,0:T(8,128)S(1)} %collective-permute-done.12.refs_2_, ...), custom_call_target="tpu_custom_call" | custom-call | flops 905969664 | bytes 7454720 | tf_op jit(solution)/shard_map/pallas_call | solution.py:317
  87.3 3.8 %collective-permute-start.15 = (f32[416,128]{1,0:T(8,128)S(1)}, f32[416,128]{1,0:T(8,128)S(1)}, u32[]{:S(2)}, u32[]{:S(2)}) collective-permute-start(f32[416,128]{1,0:T(8,128)S(1)} %get-tuple-element.64), channel_id=1, source_target_pairs={{0,6},{1,7},{2,0},{3,1},{4,2},{5,3},{6,4},{7,5},{8,14},{9,15},{10,... | collective-permute-start | bytes 638984 | tf_op jit(solution)/shard_map/ppermute | solution.py:350
  91.1 5.0 %shard_map.99 = (f32[6,256,128]{2,1,0:T(8,128)S(1)}, f32[416,128]{1,0:T(8,128)S(1)}, f32[416,128]{1,0:T(8,128)S(1)}, f32[32,128]{1,0:T(8,128)S(1)}) custom-call(f32[6,256,128]{2,1,0:T(8,128)S(1)} %get-tuple-element.74.refs_0_.refs_1_, f32[6,256,128]{2,1,0:T(8,128)S(1)} %copy-done.12, f32[416,128]{1,0:T(8,128)S(1)} %collective-permute-done.23.refs_2_, ...), custom_call_target="tpu_custom_call" | custom-call | flops 905969664 | bytes 7454720 | tf_op jit(solution)/shard_map/pallas_call | solution.py:317
  96.2 3.8 %collective-permute-start.26 = (f32[416,128]{1,0:T(8,128)S(1)}, f32[416,128]{1,0:T(8,128)S(1)}, u32[]{:S(2)}, u32[]{:S(2)}) collective-permute-start(f32[416,128]{1,0:T(8,128)S(1)} %get-tuple-element.80), channel_id=1, source_target_pairs={{0,6},{1,7},{2,0},{3,1},{4,2},{5,3},{6,4},{7,5},{8,14},{9,15},{10,... | collective-permute-start | bytes 638984 | tf_op jit(solution)/shard_map/ppermute | solution.py:350
  101.0 5.0 %shard_map.93 = (f32[6,256,128]{2,1,0:T(8,128)S(1)}, f32[416,128]{1,0:T(8,128)S(1)}, f32[416,128]{1,0:T(8,128)S(1)}, f32[32,128]{1,0:T(8,128)S(1)}) custom-call(f32[6,256,128]{2,1,0:T(8,128)S(1)} %get-tuple-element.62.refs_0_.refs_1_, f32[6,256,128]{2,1,0:T(8,128)S(1)} %get-tuple-element.58.refs_0_.refs_1_, f32[416,128]{1,0:T(8,128)S(1)} %collective-permute-done.14.refs_2_, ...), custom_call_target="tpu_custom_call" | custom-call | flops 905969664 | bytes 7454720 | tf_op jit(solution)/shard_map/pallas_call | solution.py:317
  106.1 3.8 %collective-permute-start.17 = (f32[416,128]{1,0:T(8,128)S(1)}, f32[416,128]{1,0:T(8,128)S(1)}, u32[]{:S(2)}, u32[]{:S(2)}) collective-permute-start(f32[416,128]{1,0:T(8,128)S(1)} %get-tuple-element.68), channel_id=1, source_target_pairs={{0,6},{1,7},{2,0},{3,1},{4,2},{5,3},{6,4},{7,5},{8,14},{9,15},{10,... | collective-permute-start | bytes 638984 | tf_op jit(solution)/shard_map/ppermute | solution.py:350
  110.1 5.0 %shard_map.100 = (f32[6,256,128]{2,1,0:T(8,128)S(1)}, f32[416,128]{1,0:T(8,128)S(1)}, f32[416,128]{1,0:T(8,128)S(1)}, f32[32,128]{1,0:T(8,128)S(1)}) custom-call(f32[6,256,128]{2,1,0:T(8,128)S(1)} %get-tuple-element.78.refs_0_.refs_1_, f32[6,256,128]{2,1,0:T(8,128)S(1)} %get-tuple-element.74.refs_0_.refs_1_, f32[416,128]{1,0:T(8,128)S(1)} %collective-permute-done.25.refs_2_, ...), custom_call_target="tpu_custom_call" | custom-call | flops 905969664 | bytes 7454720 | tf_op jit(solution)/shard_map/pallas_call | solution.py:317
  115.2 3.8 %collective-permute-start.28 = (f32[416,128]{1,0:T(8,128)S(1)}, f32[416,128]{1,0:T(8,128)S(1)}, u32[]{:S(2)}, u32[]{:S(2)}) collective-permute-start(f32[416,128]{1,0:T(8,128)S(1)} %get-tuple-element.84), channel_id=1, source_target_pairs={{0,6},{1,7},{2,0},{3,1},{4,2},{5,3},{6,4},{7,5},{8,14},{9,15},{10,... | collective-permute-start | bytes 638984 | tf_op jit(solution)/shard_map/ppermute | solution.py:350
  119.5 2.9 %shard_map.94 = (f32[6,256,128]{2,1,0:T(8,128)S(1)}, f32[3,256,128]{2,1,0:T(8,128)}) custom-call(f32[6,256,128]{2,1,0:T(8,128)S(1)} %get-tuple-element.66.refs_0_, f32[6,256,128]{2,1,0:T(8,128)S(1)} %get-tuple-element.62.refs_0_.refs_1_, f32[416,128]{1,0:T(8,128)S(1)} %collective-permute-done.16.refs_2_, f32[416,128]{1,0:T(8,128)S(1)} %collective-permute-done.17.refs_3_, ...), custom_call_target="tpu_custom_call" | custom-call | flops 603979776 | bytes 8388608 | tf_op jit(solution)/shard_map/pallas_call | solution.py:437
  125.1 2.9 %shard_map.101 = (f32[6,256,128]{2,1,0:T(8,128)S(1)}, f32[3,256,128]{2,1,0:T(8,128)}) custom-call(f32[6,256,128]{2,1,0:T(8,128)S(1)} %get-tuple-element.82.refs_0_, f32[6,256,128]{2,1,0:T(8,128)S(1)} %get-tuple-element.78.refs_0_.refs_1_, f32[416,128]{1,0:T(8,128)S(1)} %collective-permute-done.27.refs_2_, f32[416,128]{1,0:T(8,128)S(1)} %collective-permute-done.28.refs_3_, ...), custom_call_target="tpu_custom_call" | custom-call | flops 603979776 | bytes 8388608 | tf_op jit(solution)/shard_map/pallas_call | solution.py:437
  129.3 2.1 %collective-permute-done.29.r0_ref = f32[3,256,128]{2,1,0:T(8,128)S(1)} collective-permute-done((f32[3,256,128]{2,1,0:T(8,128)}, f32[3,256,128]{2,1,0:T(8,128)S(1)}, u32[]{:S(2)}, u32[]{:S(2)}) %collective-permute-start.29) | collective-permute-done | bytes 393248 | tf_op jit(solution)/shard_map/ppermute | solution.py:350
  131.3 7.4 %collective-permute-done.30.r1_ref = f32[3,256,128]{2,1,0:T(8,128)S(1)} collective-permute-done((f32[3,256,128]{2,1,0:T(8,128)}, f32[3,256,128]{2,1,0:T(8,128)S(1)}, u32[]{:S(2)}, u32[]{:S(2)}) %collective-permute-start.30) | collective-permute-done | bytes 393248 | tf_op jit(solution)/shard_map/ppermute | solution.py:350
  139.9 3.0 %shard_map.102 = (f32[12,256,128]{2,1,0:T(8,128)}, f32[6,256,128]{2,1,0:T(8,128)S(1)}, f32[6,256,128]{2,1,0:T(8,128)S(1)}) custom-call(s32[2]{0:T(128)S(1)} %pad_add_fusion.yx_ref, f32[6,256,128]{2,1,0:T(8,128)S(1)} %get-tuple-element.70.v0_ref, f32[6,256,128]{2,1,0:T(8,128)S(1)} %copy-done.14, f32[3,256,128]{2,1,0:T(8,128)S(1)} %collective-permute-done.29.r0_ref, ...), custom_call_target="tpu_custom_call" | custom-call | bytes 5505024 | tf_op jit(solution)/shard_map/pallas_call | solution.py:317
  144.4 15.7 %collective-permute-done.31 = f32[6,256,128]{2,1,0:T(8,128)S(1)} collective-permute-done((f32[6,256,128]{2,1,0:T(8,128)S(1)}, f32[6,256,128]{2,1,0:T(8,128)S(1)}, u32[]{:S(2)}, u32[]{:S(2)}) %collective-permute-start.31) | collective-permute-done | bytes 786464 | tf_op jit(solution)/shard_map/ppermute | solution.py:350
  160.1 2.3 %collective-permute-done.33 = f32[6,256,128]{2,1,0:T(8,128)S(1)} collective-permute-done((f32[6,256,128]{2,1,0:T(8,128)S(1)}, f32[6,256,128]{2,1,0:T(8,128)S(1)}, u32[]{:S(2)}, u32[]{:S(2)}) %collective-permute-start.33) | collective-permute-done | bytes 786464 | tf_op jit(solution)/shard_map/ppermute | solution.py:350
  165.3 6.8 %collective-permute-done.34.got_ref = f32[128,512]{1,0:T(8,128)S(1)} collective-permute-done((f32[128,512]{1,0:T(8,128)S(1)}, f32[128,512]{1,0:T(8,128)S(1)}, u32[]{:S(2)}, u32[]{:S(2)}) %collective-permute-start.34) | collective-permute-done | bytes 262176 | tf_op jit(solution)/shard_map/ppermute | solution.py:350
  172.2 11.1 %all_to_all.10 = f32[8,16,512]{2,1,0:T(8,128)S(1)} all-to-all(f32[8,16,512]{2,1,0:T(8,128)S(1)} %bitcast.18), channel_id=1, replica_groups=mesh['band'=4,'grid'=8] {'grid'}, dimensions={0} | all-to-all | bytes 524288 | tf_op jit(solution)/shard_map/all_to_all | solution.py:477
  183.3 11.9 %all_to_all.11 = f32[8,16,512]{2,1,0:T(8,128)S(1)} all-to-all(f32[8,16,512]{2,1,0:T(8,128)S(1)} %broadcast_in_dim.19), channel_id=1, replica_groups=mesh['band'=4,'grid'=8] {'grid'}, dimensions={0} | all-to-all | bytes 524288 | tf_op jit(solution)/shard_map/all_to_all | solution.py:479
  (130 shorter events, 44.0 us)
Async XLA Ops:
  4.5 10.8 %collective-permute-start.3 = (f32[18,16,256]{2,1,0:T(8,128)S(1)}, f32[18,16,256]{2,1,0:T(8,128)S(1)}, u32[]{:S(2)}, u32[]{:S(2)}) collective-permute-start(f32[18,16,256]{2,1,0:T(8,128)S(1)} %get-tuple-element.52), channel_id=1, source_target_pairs={{0,1},{1,0},{2,3},{3,2},{4,5},{5,4},{6,7},{7,6},{8,9},{9,8},{10,11... | collective-permute-start | bytes 884744 | tf_op jit(solution)/shard_map/ppermute | solution.py:350
  9.4 16.0 %collective-permute-start = (f32[3,256,128]{2,1,0:T(8,128)S(1)}, f32[3,256,128]{2,1,0:T(8,128)S(1)}, u32[]{:S(2)}, u32[]{:S(2)}) collective-permute-start(f32[3,256,128]{2,1,0:T(8,128)S(1)} %shard_map.86), channel_id=1, source_target_pairs={{0,1},{1,0},{2,3},{3,2},{4,5},{5,4},{6,7},{7,6},{8,9},{9,8},{10,11... | collective-permute-start | bytes 1179656 | tf_op jit(solution)/shard_map/ppermute | solution.py:350
  9.9 24.0 %collective-permute-start.18 = (f32[3,256,128]{2,1,0:T(8,128)S(1)}, f32[3,256,128]{2,1,0:T(8,128)S(1)}, u32[]{:S(2)}, u32[]{:S(2)}) collective-permute-start(f32[3,256,128]{2,1,0:T(8,128)S(1)} %shard_map.95), channel_id=1, source_target_pairs={{0,1},{1,0},{2,3},{3,2},{4,5},{5,4},{6,7},{7,6},{8,9},{9,8},{10,11... | collective-permute-start | bytes 1179656 | tf_op jit(solution)/shard_map/ppermute | solution.py:350
  15.3 24.9 %collective-permute-start.4 = (f32[18,16,256]{2,1,0:T(8,128)S(1)}, f32[18,16,256]{2,1,0:T(8,128)S(1)}, u32[]{:S(2)}, u32[]{:S(2)}) collective-permute-start(f32[18,16,256]{2,1,0:T(8,128)S(1)} %collective-permute-done.3.part_ref), channel_id=1, source_target_pairs={{0,8},{8,0},{16,24},{24,16},{1,9},{9,1},{17,25},{25,17},{2,10},{10... | collective-permute-start | bytes 884744 | tf_op jit(solution)/shard_map/ppermute | solution.py:350
  15.3 15.2 %collective-permute-start.5 = (f32[6,16,256]{2,1,0:T(8,128)S(1)}, f32[6,16,256]{2,1,0:T(8,128)S(1)}, u32[]{:S(2)}, u32[]{:S(2)}) collective-permute-start(f32[6,16,256]{2,1,0:T(8,128)S(1)} %get-tuple-element.53), channel_id=1, source_target_pairs={{0,6},{1,3},{2,0},{3,5},{4,2},{5,7},{6,4},{7,1},{8,14},{9,11},{10,... | collective-permute-start | bytes 294920 | tf_op jit(solution)/shard_map/ppermute | solution.py:350
  19.4 11.1 %collective-permute-start.7 = (f32[6,16,256]{2,1,0:T(8,128)S(1)}, f32[6,16,256]{2,1,0:T(8,128)S(1)}, u32[]{:S(2)}, u32[]{:S(2)}) collective-permute-start(f32[6,16,256]{2,1,0:T(8,128)S(1)} %get-tuple-element.53), channel_id=1, source_target_pairs={{0,7},{1,2},{2,1},{3,4},{4,3},{5,6},{6,5},{7,0},{8,15},{9,10},{10,... | collective-permute-start | bytes 294920 | tf_op jit(solution)/shard_map/ppermute | solution.py:350
  28.0 23.4 %collective-permute-start.1 = (f32[384,128]{1,0:T(8,128)}, f32[384,128]{1,0:T(8,128)}, u32[]{:S(2)}, u32[]{:S(2)}) collective-permute-start(f32[384,128]{1,0:T(8,128)} %get-tuple-element.49), channel_id=1, source_target_pairs={{0,2},{1,3},{2,4},{3,5},{4,6},{5,7},{6,0},{7,1},{8,10},{9,11},{10,... | collective-permute-start | bytes 589832 | tf_op jit(solution)/shard_map/ppermute | solution.py:350
  31.8 28.9 %collective-permute-start.2 = (f32[384,128]{1,0:T(8,128)}, f32[384,128]{1,0:T(8,128)}, u32[]{:S(2)}, u32[]{:S(2)}) collective-permute-start(f32[384,128]{1,0:T(8,128)} %get-tuple-element.50), channel_id=1, source_target_pairs={{0,6},{1,7},{2,0},{3,1},{4,2},{5,3},{6,4},{7,5},{8,14},{9,15},{10,... | collective-permute-start | bytes 589832 | tf_op jit(solution)/shard_map/ppermute | solution.py:350
  34.0 17.4 %collective-permute-start.11 = (f32[12,256]{1,0:T(8,128)S(1)}, f32[12,256]{1,0:T(8,128)S(1)}, u32[]{:S(2)}, u32[]{:S(2)}) collective-permute-start(f32[12,256]{1,0:T(8,128)S(1)} %reshape.50), channel_id=1, source_target_pairs={{0,1},{1,0},{2,3},{3,2},{4,5},{5,4},{6,7},{7,6},{8,9},{9,8},{10,11... | collective-permute-start | bytes 36872 | tf_op jit(solution)/shard_map/ppermute | solution.py:350
  39.2 30.4 %collective-permute-start.19 = (f32[384,128]{1,0:T(8,128)}, f32[384,128]{1,0:T(8,128)}, u32[]{:S(2)}, u32[]{:S(2)}) collective-permute-start(f32[384,128]{1,0:T(8,128)} %get-tuple-element.72), channel_id=1, source_target_pairs={{0,2},{1,3},{2,4},{3,5},{4,6},{5,7},{6,0},{7,1},{8,10},{9,11},{10,... | collective-permute-start | bytes 589832 | tf_op jit(solution)/shard_map/ppermute | solution.py:350
  40.9 32.5 %collective-permute-start.20 = (f32[384,128]{1,0:T(8,128)}, f32[384,128]{1,0:T(8,128)}, u32[]{:S(2)}, u32[]{:S(2)}) collective-permute-start(f32[384,128]{1,0:T(8,128)} %get-tuple-element.73), channel_id=1, source_target_pairs={{0,6},{1,7},{2,0},{3,1},{4,2},{5,3},{6,4},{7,5},{8,14},{9,15},{10,... | collective-permute-start | bytes 589832 | tf_op jit(solution)/shard_map/ppermute | solution.py:350
  51.3 9.4 %collective-permute-start.9 = (f32[32,128]{1,0:T(8,128)S(1)}, f32[32,128]{1,0:T(8,128)S(1)}, u32[]{:S(2)}, u32[]{:S(2)}) collective-permute-start(f32[32,128]{1,0:T(8,128)S(1)} %shard_map.90.refs_5_), channel_id=1, source_target_pairs={{0,2},{1,3},{2,4},{3,5},{4,6},{5,7},{6,0},{7,1},{8,10},{9,11},{10,... | collective-permute-start | bytes 49160 | tf_op jit(solution)/shard_map/ppermute | solution.py:350
  51.4 13.2 %collective-permute-start.10 = (f32[32,128]{1,0:T(8,128)S(1)}, f32[32,128]{1,0:T(8,128)S(1)}, u32[]{:S(2)}, u32[]{:S(2)}) collective-permute-start(f32[32,128]{1,0:T(8,128)S(1)} %shard_map.90.refs_5_), channel_id=1, source_target_pairs={{0,6},{1,7},{2,0},{3,1},{4,2},{5,3},{6,4},{7,5},{8,14},{9,15},{10,... | collective-permute-start | bytes 49160 | tf_op jit(solution)/shard_map/ppermute | solution.py:350
  60.7 12.7 %collective-permute-start.21 = (f32[32,128]{1,0:T(8,128)S(1)}, f32[32,128]{1,0:T(8,128)S(1)}, u32[]{:S(2)}, u32[]{:S(2)}) collective-permute-start(f32[32,128]{1,0:T(8,128)S(1)} %shard_map.97.refs_5_), channel_id=1, source_target_pairs={{0,2},{1,3},{2,4},{3,5},{4,6},{5,7},{6,0},{7,1},{8,10},{9,11},{10,... | collective-permute-start | bytes 49160 | tf_op jit(solution)/shard_map/ppermute | solution.py:350
  60.8 12.6 %collective-permute-start.22 = (f32[32,128]{1,0:T(8,128)S(1)}, f32[32,128]{1,0:T(8,128)S(1)}, u32[]{:S(2)}, u32[]{:S(2)}) collective-permute-start(f32[32,128]{1,0:T(8,128)S(1)} %shard_map.97.refs_5_), channel_id=1, source_target_pairs={{0,6},{1,7},{2,0},{3,1},{4,2},{5,3},{6,4},{7,5},{8,14},{9,15},{10,... | collective-permute-start | bytes 49160 | tf_op jit(solution)/shard_map/ppermute | solution.py:350
  69.5 12.6 %collective-permute-start.12 = (f32[416,128]{1,0:T(8,128)S(1)}, f32[416,128]{1,0:T(8,128)S(1)}, u32[]{:S(2)}, u32[]{:S(2)}) collective-permute-start(f32[416,128]{1,0:T(8,128)S(1)} %get-tuple-element.59), channel_id=1, source_target_pairs={{0,2},{1,3},{2,4},{3,5},{4,6},{5,7},{6,0},{7,1},{8,10},{9,11},{10,... | collective-permute-start | bytes 638984 | tf_op jit(solution)/shard_map/ppermute | solution.py:350
  69.6 12.6 %collective-permute-start.13 = (f32[416,128]{1,0:T(8,128)S(1)}, f32[416,128]{1,0:T(8,128)S(1)}, u32[]{:S(2)}, u32[]{:S(2)}) collective-permute-start(f32[416,128]{1,0:T(8,128)S(1)} %get-tuple-element.60), channel_id=1, source_target_pairs={{0,6},{1,7},{2,0},{3,1},{4,2},{5,3},{6,4},{7,5},{8,14},{9,15},{10,... | collective-permute-start | bytes 638984 | tf_op jit(solution)/shard_map/ppermute | solution.py:350
  78.3 12.8 %collective-permute-start.23 = (f32[416,128]{1,0:T(8,128)S(1)}, f32[416,128]{1,0:T(8,128)S(1)}, u32[]{:S(2)}, u32[]{:S(2)}) collective-permute-start(f32[416,128]{1,0:T(8,128)S(1)} %get-tuple-element.75), channel_id=1, source_target_pairs={{0,2},{1,3},{2,4},{3,5},{4,6},{5,7},{6,0},{7,1},{8,10},{9,11},{10,... | collective-permute-start | bytes 638984 | tf_op jit(solution)/shard_map/ppermute | solution.py:350
  78.3 12.8 %collective-permute-start.24 = (f32[416,128]{1,0:T(8,128)S(1)}, f32[416,128]{1,0:T(8,128)S(1)}, u32[]{:S(2)}, u32[]{:S(2)}) collective-permute-start(f32[416,128]{1,0:T(8,128)S(1)} %get-tuple-element.76), channel_id=1, source_target_pairs={{0,6},{1,7},{2,0},{3,1},{4,2},{5,3},{6,4},{7,5},{8,14},{9,15},{10,... | collective-permute-start | bytes 638984 | tf_op jit(solution)/shard_map/ppermute | solution.py:350
  87.2 12.8 %collective-permute-start.14 = (f32[416,128]{1,0:T(8,128)S(1)}, f32[416,128]{1,0:T(8,128)S(1)}, u32[]{:S(2)}, u32[]{:S(2)}) collective-permute-start(f32[416,128]{1,0:T(8,128)S(1)} %get-tuple-element.63), channel_id=1, source_target_pairs={{0,2},{1,3},{2,4},{3,5},{4,6},{5,7},{6,0},{7,1},{8,10},{9,11},{10,... | collective-permute-start | bytes 638984 | tf_op jit(solution)/shard_map/ppermute | solution.py:350
  87.3 13.7 %collective-permute-start.15 = (f32[416,128]{1,0:T(8,128)S(1)}, f32[416,128]{1,0:T(8,128)S(1)}, u32[]{:S(2)}, u32[]{:S(2)}) collective-permute-start(f32[416,128]{1,0:T(8,128)S(1)} %get-tuple-element.64), channel_id=1, source_target_pairs={{0,6},{1,7},{2,0},{3,1},{4,2},{5,3},{6,4},{7,5},{8,14},{9,15},{10,... | collective-permute-start | bytes 638984 | tf_op jit(solution)/shard_map/ppermute | solution.py:350
  96.1 13.7 %collective-permute-start.25 = (f32[416,128]{1,0:T(8,128)S(1)}, f32[416,128]{1,0:T(8,128)S(1)}, u32[]{:S(2)}, u32[]{:S(2)}) collective-permute-start(f32[416,128]{1,0:T(8,128)S(1)} %get-tuple-element.79), channel_id=1, source_target_pairs={{0,2},{1,3},{2,4},{3,5},{4,6},{5,7},{6,0},{7,1},{8,10},{9,11},{10,... | collective-permute-start | bytes 638984 | tf_op jit(solution)/shard_map/ppermute | solution.py:350
  96.2 13.9 %collective-permute-start.26 = (f32[416,128]{1,0:T(8,128)S(1)}, f32[416,128]{1,0:T(8,128)S(1)}, u32[]{:S(2)}, u32[]{:S(2)}) collective-permute-start(f32[416,128]{1,0:T(8,128)S(1)} %get-tuple-element.80), channel_id=1, source_target_pairs={{0,6},{1,7},{2,0},{3,1},{4,2},{5,3},{6,4},{7,5},{8,14},{9,15},{10,... | collective-permute-start | bytes 638984 | tf_op jit(solution)/shard_map/ppermute | solution.py:350
  106.0 13.0 %collective-permute-start.16 = (f32[416,128]{1,0:T(8,128)S(1)}, f32[416,128]{1,0:T(8,128)S(1)}, u32[]{:S(2)}, u32[]{:S(2)}) collective-permute-start(f32[416,128]{1,0:T(8,128)S(1)} %get-tuple-element.67), channel_id=1, source_target_pairs={{0,2},{1,3},{2,4},{3,5},{4,6},{5,7},{6,0},{7,1},{8,10},{9,11},{10,... | collective-permute-start | bytes 638984 | tf_op jit(solution)/shard_map/ppermute | solution.py:350
  106.1 13.4 %collective-permute-start.17 = (f32[416,128]{1,0:T(8,128)S(1)}, f32[416,128]{1,0:T(8,128)S(1)}, u32[]{:S(2)}, u32[]{:S(2)}) collective-permute-start(f32[416,128]{1,0:T(8,128)S(1)} %get-tuple-element.68), channel_id=1, source_target_pairs={{0,6},{1,7},{2,0},{3,1},{4,2},{5,3},{6,4},{7,5},{8,14},{9,15},{10,... | collective-permute-start | bytes 638984 | tf_op jit(solution)/shard_map/ppermute | solution.py:350
  115.1 9.6 %collective-permute-start.27 = (f32[416,128]{1,0:T(8,128)S(1)}, f32[416,128]{1,0:T(8,128)S(1)}, u32[]{:S(2)}, u32[]{:S(2)}) collective-permute-start(f32[416,128]{1,0:T(8,128)S(1)} %get-tuple-element.83), channel_id=1, source_target_pairs={{0,2},{1,3},{2,4},{3,5},{4,6},{5,7},{6,0},{7,1},{8,10},{9,11},{10,... | collective-permute-start | bytes 638984 | tf_op jit(solution)/shard_map/ppermute | solution.py:350
  115.2 9.9 %collective-permute-start.28 = (f32[416,128]{1,0:T(8,128)S(1)}, f32[416,128]{1,0:T(8,128)S(1)}, u32[]{:S(2)}, u32[]{:S(2)}) collective-permute-start(f32[416,128]{1,0:T(8,128)S(1)} %get-tuple-element.84), channel_id=1, source_target_pairs={{0,6},{1,7},{2,0},{3,1},{4,2},{5,3},{6,4},{7,5},{8,14},{9,15},{10,... | collective-permute-start | bytes 638984 | tf_op jit(solution)/shard_map/ppermute | solution.py:350
  122.4 9.0 %collective-permute-start.29 = (f32[3,256,128]{2,1,0:T(8,128)}, f32[3,256,128]{2,1,0:T(8,128)S(1)}, u32[]{:S(2)}, u32[]{:S(2)}) collective-permute-start(f32[3,256,128]{2,1,0:T(8,128)} %get-tuple-element.87), channel_id=1, source_target_pairs={{0,1},{1,0},{2,3},{3,2},{4,5},{5,4},{6,7},{7,6},{8,9},{9,8},{10,11... | collective-permute-start | bytes 1179656 | tf_op jit(solution)/shard_map/ppermute | solution.py:350
  128.9 9.9 %collective-permute-start.30 = (f32[3,256,128]{2,1,0:T(8,128)}, f32[3,256,128]{2,1,0:T(8,128)S(1)}, u32[]{:S(2)}, u32[]{:S(2)}) collective-permute-start(f32[3,256,128]{2,1,0:T(8,128)} %get-tuple-element.88), channel_id=1, source_target_pairs={{0,1},{1,0},{2,3},{3,2},{4,5},{5,4},{6,7},{7,6},{8,9},{9,8},{10,11... | collective-permute-start | bytes 1179656 | tf_op jit(solution)/shard_map/ppermute | solution.py:350
  142.9 17.2 %collective-permute-start.31 = (f32[6,256,128]{2,1,0:T(8,128)S(1)}, f32[6,256,128]{2,1,0:T(8,128)S(1)}, u32[]{:S(2)}, u32[]{:S(2)}) collective-permute-start(f32[6,256,128]{2,1,0:T(8,128)S(1)} %get-tuple-element.91), channel_id=1, source_target_pairs={{0,16},{8,24},{16,0},{24,8},{1,17},{9,25},{17,1},{25,9},{2,18},{10... | collective-permute-start | bytes 2359304 | tf_op jit(solution)/shard_map/ppermute | solution.py:350
  144.4 15.7 %collective-permute-start.32 = (f32[6,256,128]{2,1,0:T(8,128)S(1)}, f32[6,256,128]{2,1,0:T(8,128)S(1)}, u32[]{:S(2)}, u32[]{:S(2)}) collective-permute-start(f32[6,256,128]{2,1,0:T(8,128)S(1)} %get-tuple-element.90), channel_id=1, source_target_pairs={{0,8},{8,0},{16,24},{24,16},{1,9},{9,1},{17,25},{25,17},{2,10},{10... | collective-permute-start | bytes 2359304 | tf_op jit(solution)/shard_map/ppermute | solution.py:350
  163.8 8.4 %collective-permute-start.34 = (f32[128,512]{1,0:T(8,128)S(1)}, f32[128,512]{1,0:T(8,128)S(1)}, u32[]{:S(2)}, u32[]{:S(2)}) collective-permute-start(f32[128,512]{1,0:T(8,128)S(1)} %get-tuple-element.93), channel_id=1, source_target_pairs={{0,16},{8,24},{16,0},{24,8},{1,17},{9,25},{17,1},{25,9},{2,18},{10... | collective-permute-start | bytes 786440 | tf_op jit(solution)/shard_map/ppermute | solution.py:350
  (31 other events, 191.3 us)

commit v2 on v1

v2 whole, which is shorter than its diff:
```python
import functools

import jax
import jax.numpy as jnp
import ml_dtypes
import numpy as np
from jax import lax
from jax.experimental import pallas as pl
from jax.experimental.pallas import tpu as pltpu
from jax.sharding import PartitionSpec as P

DEGREE = 4
REACH = 6
LANES = 128
QUARTER = 32

WEIGHTS = (
    -5369.0 / 1800.0,
    12.0 / 7.0,
    -15.0 / 56.0,
    10.0 / 189.0,
    -1.0 / 112.0,
    2.0 / 1925.0,
    -1.0 / 16632.0,
)
LOWER = -4.0
CUTOFF = 1.0
UPPER = 16.0
F32 = jnp.float32
BF16 = jnp.bfloat16


def filter_terms(degree):
    half_span = (UPPER - CUTOFF) / 2.0
    middle = (UPPER + CUTOFF) / 2.0
    sigma_now = half_span / (LOWER - middle)
    sigma_first = sigma_now
    scales = [sigma_now / half_span]
    recall = [0.0]
    for level in range(1, degree):
        sigma_next = 1.0 / (2.0 / sigma_first - sigma_now)
        scales.append(2.0 * sigma_next / half_span)
        recall.append(sigma_now * sigma_next)
        sigma_now = sigma_next
    return (middle, scales, recall)


def plane_matrix(ny, nz):
    def ring(n):
        m = np.zeros((n, n))
        for i in range(n):
            m[i, i] += WEIGHTS[0]
            for r in range(1, REACH + 1):
                m[i, (i + r) % n] += WEIGHTS[r]
                m[i, (i - r) % n] += WEIGHTS[r]
        return m

    full = -0.5 * (np.kron(ring(ny), np.eye(nz)) + np.kron(np.eye(ny), ring(nz)))
    high = full.astype(ml_dtypes.bfloat16)
    low = (full - high.astype(np.float64)).astype(ml_dtypes.bfloat16)
    return high, low


def halves(value):
    high = value.astype(BF16)
    return high, (value - high.astype(F32)).astype(BF16)


def dot3(*pairs):
    left, right = [], []
    for (a_high, a_low), (b_high, b_low) in pairs:
        left += [a_high, a_high, a_low]
        right += [b_high, b_low, b_high]
    return lax.dot_general(
        jnp.concatenate(left, axis=1),
        jnp.concatenate(right, axis=0),
        (((1,), (0,)), ((), ())),
        preferred_element_type=F32,
    )


def lane_ids(shape):
    return lax.broadcasted_iota(jnp.int32, shape, len(shape) - 1)


def turn(value, shift):
    if isinstance(shift, int):
        shift = shift % LANES
        if shift == 0:
            return value
    else:
        shift = lax.rem(shift + 8 * LANES, LANES)
    return pltpu.roll(value, shift, axis=value.ndim - 1)


def pack_kernel(chunk, y_ref, x_ref, *refs):
    y = y_ref[0]
    out_ref = refs[-1]
    cells = x_ref.shape[1]
    group = lane_ids((cells, LANES)) // QUARTER
    if chunk:
        out_ref[3 * cells :] = refs[0][...]
    for r in range(3):
        row = None
        for slot, plane in enumerate((r, r + 6, r + 3, r + 9)):
            piece = turn(x_ref[plane], QUARTER * slot - 64 - QUARTER * chunk + 64 * y)
            row = piece if row is None else jnp.where(group == slot, piece, row)
        out_ref[r * cells : (r + 1) * cells] = row


def rim_pack(row, out_ref, r, source):
    part = row.shape[0] // 4
    group = lane_ids((part, LANES)) // QUARTER
    packed = None
    for j in range(4):
        piece = turn(row[j * part : (j + 1) * part], QUARTER * (j - source))
        packed = piece if packed is None else jnp.where(group == j, piece, packed)
    out_ref[pl.ds(r * part, part), :] = packed


def assemble_kernel(chunk, y_ref, x_ref, got_ref, *refs):
    y = y_ref[0]
    if chunk == 0:
        v_ref, up_ref, down_ref = refs
    else:
        mh_ref, ml_ref, v_ref, up_ref, down_ref, coef_ref = refs
    cells = x_ref.shape[1]
    group = lane_ids((cells, LANES)) // QUARTER
    coef = None
    for r in range(6):
        first = turn(x_ref[r], -QUARTER * chunk)
        second = turn(x_ref[r + 6], QUARTER - QUARTER * chunk)
        other = turn(
            got_ref[cells * (r % 3) : cells * (r % 3 + 1)], 64 * (1 - y) if r < 3 else 64 * y
        )
        row = jnp.where(group == 2 * y, first, jnp.where(group == 2 * y + 1, second, other))
        v_ref[r] = row
        rim_pack(row, up_ref, r, 3)
        rim_pack(row, down_ref, r, 0)
        if chunk:
            term = dot3(((mh_ref[r], ml_ref[r]), halves(row)))
            coef = term if coef is None else coef + term
    if chunk:
        share_coef(coef, coef_ref, up_ref, down_ref)


def share_coef(coef, coef_ref, up_ref, down_ref):
    packed = collapse(coef)
    coef_ref[...] = packed
    rim = up_ref.shape[0] - 32
    up_ref[pl.ds(rim, 32), :] = packed
    down_ref[pl.ds(rim, 32), :] = packed


def collapse(blocks):
    group = lane_ids((32, LANES)) // QUARTER

    def block(i, s, target):
        b = 2 * i + s
        return turn(blocks[32 * b : 32 * b + 32], QUARTER * (target - i))

    low = block(0, 0, 0) + block(1, 0, 0) + block(2, 0, 0)
    high = block(1, 1, 1) + block(2, 1, 1) + block(3, 1, 1)
    below, above = block(0, 1, 2), block(3, 0, 3)
    return jnp.where(
        group == 0, low, jnp.where(group == 1, high, jnp.where(group == 2, below, above))
    )


def coef_kernel(v_ref, mh_ref, ml_ref, out_ref):
    total = None
    for r in range(6):
        term = dot3(((mh_ref[r], ml_ref[r]), halves(v_ref[r])))
        total = term if total is None else total + term
    out_ref[...] = collapse(total)


def level_kernel(scale, recall, first, apart, last, joined, *refs):
    refs = list(refs)
    if last:
        yx_ref = refs.pop(0)
    v_ref = refs.pop(0)
    prev_ref = None if first else refs.pop(0)
    below_ref, above_ref = refs.pop(0), refs.pop(0)
    if apart:
        below_coef, above_coef = refs.pop(0), refs.pop(0)
    own_ref, kb_ref, ch_ref, cl_ref, th_ref, tl_ref, pot_ref = refs[:7]
    refs = refs[7:]
    if last:
        out_ref, own_piece, y_piece, x_piece, d_piece, ext = refs
    else:
        mh_ref, ml_ref, out_ref, up_ref, down_ref, coef_ref, ext = refs
    cells = v_ref.shape[1]
    part = cells // 4
    rim = 6 * part
    part_group = lane_ids((part, LANES)) // QUARTER
    cg = lane_ids((32, LANES)) // QUARTER
    from_below = below_coef[...] if apart else below_ref[pl.ds(rim, 32), :]
    from_above = above_coef[...] if apart else above_ref[pl.ds(rim, 32), :]
    total = own_ref[...] + jnp.where(cg % 2 == 0, turn(from_below, 32), turn(from_above, -32))
    total = total * kb_ref[...]
    rows = []
    for i, s, source in (
        (0, 0, 0), (0, 1, 2), (1, 0, 0), (1, 1, 1), (2, 0, 0), (2, 1, 1), (3, 0, 3), (3, 1, 1),
    ):
        rows.append(jnp.where(cg == i, turn(total, QUARTER * (i - source)), 0.0))
    spread = halves(jnp.concatenate(rows, axis=0))
    for r in range(6):
        row = v_ref[r]
        ext[6 + r] = row
        before, after = turn(row, QUARTER), turn(row, -QUARTER)
        low, high = below_ref[pl.ds(r * part, part), :], above_ref[pl.ds(r * part, part), :]
        for j in range(4):
            cut = slice(j * part, (j + 1) * part)
            ext[r, cut] = jnp.where(part_group == 0, turn(low, -QUARTER * j), before[cut])
            ext[12 + r, cut] = jnp.where(part_group == 3, turn(high, 96 - QUARTER * j), after[cut])
    coef = None
    if last:
        mine = 2 * yx_ref[0] + yx_ref[1]
    for r in range(6):
        row = ext[6 + r]
        value = dot3(
            ((ch_ref[...], cl_ref[...]), halves(row)), ((th_ref[r], tl_ref[r]), spread)
        )
        value = value + pot_ref[r] * row
        for k in range(1, REACH + 1):
            value = value + (-0.5 * WEIGHTS[k]) * (ext[6 + r + k] + ext[6 + r - k])
        value = scale * value
        if not first:
            value = value - recall * prev_ref[r]
        out_ref[r] = value
        if last:
            for flip, piece in enumerate((own_piece, x_piece, y_piece, d_piece)):
                rim_pack(value, piece, r, lax.bitwise_xor(mine, flip))
            if joined:
                y_piece[pl.ds(rim + r * part, part), :] = d_piece[pl.ds(r * part, part), :]
        else:
            rim_pack(value, up_ref, r, 3)
            rim_pack(value, down_ref, r, 0)
            term = dot3(((mh_ref[r], ml_ref[r]), halves(value)))
            coef = term if coef is None else coef + term
    if not last:
        share_coef(coef, coef_ref, up_ref, down_ref)


def unpack_kernel(yx_ref, v0_ref, v1_ref, y0_ref, y1_ref, rest_ref, out_ref):
    y, x = yx_ref[0], yx_ref[1]
    cells = v0_ref.shape[1]
    part = cells // 4
    group = lane_ids((part, LANES)) // QUARTER
    rim = 6 * part
    rest0_ref = y0_ref.at[pl.ds(rim, rim)]
    for half, pieces in ((x, (y0_ref, y1_ref)), (1 - x, (rest0_ref, rest_ref))):
        for r in range(6):
            own = [turn(v_ref[r], QUARTER * (k - half)) for k, v_ref in enumerate((v0_ref, v1_ref))]
            for j in range(4):
                rows = slice(j * part, (j + 1) * part)
                block = None
                for k in range(2):
                    got = turn(
                        pieces[k][pl.ds(r * part, part), :],
                        64 * (1 - y) + QUARTER * (k - j),
                    )
                    mine = jnp.where(group == 2 * y + k, own[k][rows], got)
                    block = mine if k == 0 else jnp.where(group % 2 == 1, mine, block)
                out_ref[6 * half + r, rows] = block


def tile_kernel(y_ref, own_ref, x_ref, y_piece_ref, d_ref, out_ref):
    y = y_ref[0]
    rows = own_ref.shape[0]
    pieces = [own_ref[...], y_piece_ref[pl.ds(0, rows)], x_ref[...], d_ref[...]]
    group = lane_ids((rows, LANES)) // QUARTER
    for j in range(4):
        block = None
        for s, piece in enumerate(pieces):
            target = 2 * (s // 2) + lax.bitwise_xor(y, s % 2)
            turned = turn(piece, QUARTER * (target - j))
            block = turned if block is None else jnp.where(group == target, turned, block)
        out_ref[pl.ds(j * rows, rows), :] = block


def gram_kernel(a0_ref, a1_ref, s0_ref, s1_ref, keep_ref, send_ref):
    def dot(p, q):
        return lax.dot_general(p, q, (((0,), (0,)), ((), ())), preferred_element_type=F32)

    parts = [halves(ref[...]) for ref in (a0_ref, a1_ref, s0_ref, s1_ref)]
    high = jnp.concatenate([p[0] for p in parts], axis=1)
    low = jnp.concatenate([p[1] for p in parts], axis=1)
    left_high, left_low = high[:, :256], low[:, :256]
    total = dot(left_high, high) + (dot(left_high, low) + dot(left_low, high))
    group = lane_ids((32, LANES)) // QUARTER
    for x_row, out_ref in ((0, keep_ref), (1, send_ref)):
        for h_row in range(2):
            for k_row in range(2):
                at = 128 * k_row + 64 * x_row + 32 * h_row
                for flip in range(4):
                    x_col, core = flip // 2, flip % 2
                    block = None
                    for h in range(2):
                        for k in range(2):
                            start = 256 * core + 128 * k
                            tile = total[at : at + 32, start : start + 128]
                            piece = turn(tile, QUARTER * (2 * h + k - 2 * x_col - h))
                            block = (
                                piece
                                if block is None
                                else jnp.where(group == 2 * h + k, piece, block)
                            )
                    to = 2 * (x_col ^ x_row) + core
                    out_ref[
                        pl.ds(64 * h_row + 32 * k_row, 32), 128 * to : 128 * to + 128
                    ] = block


def order_kernel(factor, b_ref, keep_ref, got_ref, out_ref):
    b = b_ref[0]
    for j, flip in enumerate((0, 1, 2, 3)):
        cut = slice(j * 128, (j + 1) * 128)
        block = (keep_ref[:, cut] + got_ref[:, cut]) * factor
        target = pl.multiple_of(lax.bitwise_xor(b, flip) * 128, 128)
        out_ref[:, pl.ds(target, 128)] = block


def dense_kernel(yc_ref, planes_ref, proj_ref, e_ref, part_ref, rim_ref):
    y, c = yc_ref[0], yc_ref[1]
    e_ref[...] = jnp.zeros_like(e_ref)
    atoms, span, count, _ = proj_ref.shape
    for a in range(atoms):
        for b in range(span):
            at = (planes_ref[a, b], slice(a * count, (a + 1) * count))
            e_ref[at] = e_ref[at] + proj_ref[a, b]
    rows = pl.ds(pl.multiple_of(16 * c, 16), 16)
    for r in range(18):
        part_ref[r] = e_ref[6 * (1 - y) + r, rows, :]
    rim_ref[...] = e_ref[pl.ds(18 * y, 6), rows, :]


def potential_kernel(offset, y_ref, own_ref, got_ref, out_ref):
    y = y_ref[0]
    cells = out_ref.shape[1]
    own = own_ref[...] + offset
    other = got_ref[3 * cells :] + offset
    first, second = jnp.where(y == 0, own, other), jnp.where(y == 0, other, own)
    whole = jnp.concatenate([first, second], axis=0)
    fill = jnp.zeros((LANES - whole.shape[0], LANES), F32)
    columns = jnp.concatenate([whole, fill], axis=0).T
    each = cells // LANES
    group = lane_ids((LANES, LANES)) // QUARTER
    for r in range(6):
        for h in range(each):
            row = None
            for i in range(4):
                at = (6 * i + r) * each + h
                piece = jnp.broadcast_to(columns[:, at : at + 1], (LANES, LANES))
                row = piece if row is None else jnp.where(group == i, piece, row)
            out_ref[r, h * LANES : (h + 1) * LANES] = row


def maps_kernel(
    yc_ref, e_ref, part_ref, part2_ref, a_ref, a2_ref, b_ref, b2_ref,
    mh_ref, ml_ref, th_ref, tl_ref,
):
    y, c = yc_ref[0], yc_ref[1]

    def whole(mine, rest):
        first, second = jnp.where(c == 0, mine, rest), jnp.where(c == 0, rest, mine)
        return jnp.concatenate([first, second], axis=0)

    for r in range(6):
        one, two = whole(a_ref[r], a2_ref[r]), whole(b_ref[r], b2_ref[r])
        below, above = jnp.where(y == 1, one, two), jnp.where(y == 1, two, one)
        other = [whole(part_ref[6 * i + r], part2_ref[6 * i + r]) for i in range(3)]
        low = [jnp.where(y == 0, e_ref[6 + 6 * i + r], other[i]) for i in range(3)]
        high = [jnp.where(y == 1, e_ref[6 * i + r], other[i]) for i in range(3)]
        block = jnp.concatenate(
            [low[0], below, low[1], high[0], low[2], high[1], above, high[2]], axis=0
        )
        mh_ref[r], ml_ref[r] = halves(block)
        th_ref[r], tl_ref[r] = halves(block.T)


SMEM = pl.BlockSpec(memory_space=pltpu.SMEM)
VMEM = pl.BlockSpec(memory_space=pltpu.VMEM)
ANY = pl.BlockSpec(memory_space=pl.ANY)


def call(kernel, out, scalars, arrays, scratch=(), after=()):
    used = len(scalars) + len(arrays)

    def body(*refs):
        kernel(*refs[:used], *refs[used + len(after) :])

    return pl.pallas_call(
        body,
        out_shape=out,
        in_specs=[SMEM] * len(scalars) + [VMEM] * len(arrays) + [ANY] * len(after),
        out_specs=[VMEM] * len(out),
        scratch_shapes=list(scratch),
        compiler_params=pltpu.CompilerParams(vmem_limit_bytes=48 * 1024 * 1024),
        cost_estimate=pl.CostEstimate(flops=1 << 10, bytes_accessed=1 << 10, transcendentals=0),
    )(*scalars, *arrays, *after)


def f32(*shape):
    return jax.ShapeDtypeStruct(shape, F32)


def bf16(*shape):
    return jax.ShapeDtypeStruct(shape, BF16)


def shards(orbitals, potential, projectors, atom_planes, kb_energy):
    slab, ny, nz, orb_here = orbitals.shape
    cells = ny * nz
    peers = lax.axis_size("grid")
    bands = lax.axis_size("band")
    g, b = lax.axis_index("grid"), lax.axis_index("band")
    y, c, x = lax.rem(g, 2), lax.rem(b, 2), b // 2
    y1 = y.reshape(1).astype(jnp.int32)
    b1 = b.reshape(1).astype(jnp.int32)
    yc = jnp.stack([y, c]).astype(jnp.int32)
    yx = jnp.stack([y, x]).astype(jnp.int32)

    def move(array, axis, target):
        size = lax.axis_size(axis)
        return lax.ppermute(array, axis, [(i, target(i) % size) for i in range(size)])

    def partner(array):
        return move(array, "grid", lambda i: i ^ 1)

    def up(array):
        return move(array, "grid", lambda i: i + 2)

    def down(array):
        return move(array, "grid", lambda i: i - 2)

    def sibling(array):
        return move(array, "band", lambda i: i ^ 1)

    def across(array):
        return move(array, "band", lambda i: i ^ 2)

    field = orbitals.reshape(slab, cells, orb_here)
    rim_rows = 6 * (cells // 4)
    middle, scales, recall = filter_terms(DEGREE)

    def diagonal(array):
        size = peers * bands
        flip = 2 * peers + 1
        return lax.ppermute(array, ("band", "grid"), [(i, i ^ flip) for i in range(size)])

    pot_own = potential.reshape(slab * cells // LANES, LANES)
    pot_rows = pot_own.shape[0]
    sent0 = call(
        functools.partial(pack_kernel, 0), [f32(3 * cells, LANES)], [y1], [field]
    )[0]
    other0 = partner(sent0)
    dense, part, rim = call(
        dense_kernel,
        [f32(24, 32, cells), f32(18, 16, cells), f32(6, 16, cells)],
        [yc, atom_planes],
        [projectors.transpose(0, 2, 1, 3)],
        after=[sent0],
    )
    part = partner(part)
    rim_a = move(rim, "grid", lambda i: i + 2 if i % 2 else i - 2)
    rim_b = move(rim, "grid", lambda i: i + 1 if i % 2 else i - 1)
    sent1 = call(
        functools.partial(pack_kernel, 1),
        [f32(3 * cells + pot_rows, LANES)],
        [y1],
        [field, pot_own],
        after=[other0],
    )[0]
    other1 = partner(sent1)
    other = [other0, other1]
    first_made = call(
        functools.partial(assemble_kernel, 0),
        [f32(6, cells, LANES)] + [f32(rim_rows, LANES)] * 2,
        [y1],
        [field, other0],
    )
    part, rim_a, rim_b, v0 = lax.optimization_barrier((part, rim_a, rim_b, first_made[0]))
    mh, ml, th, tl = call(
        maps_kernel,
        [bf16(6, 256, cells)] * 2 + [bf16(6, cells, 256)] * 2,
        [yc],
        [dense, part, sibling(part), rim_a, sibling(rim_a), rim_b, sibling(rim_b)],
    )
    pot = call(
        functools.partial(potential_kernel, -(middle + 0.5 * WEIGHTS[0])),
        [f32(6, cells, LANES)],
        [y1],
        [pot_own, other1],
    )[0]
    kb = jnp.broadcast_to(jnp.tile(kb_energy, 4)[:, None], (32, LANES))
    ch, cl = (jnp.asarray(m) for m in plane_matrix(ny, nz))

    s = dict(v=v0, prev=None, below=up(first_made[1]), above=down(first_made[2]))
    s["coef"] = call(coef_kernel, [f32(32, LANES)], [], [v0, mh, ml])[0]
    s["apart"] = [up(s["coef"]), down(s["coef"])]
    made = call(
        functools.partial(assemble_kernel, 1),
        [f32(6, cells, LANES)] + [f32(rim_rows + 32, LANES)] * 2 + [f32(32, LANES)],
        [y1],
        [field, other1, mh, ml],
        after=[s["coef"]],
    )
    up1, down1, s["apart"] = lax.optimization_barrier((made[1], made[2], s["apart"]))
    chunks = [
        s,
        dict(v=made[0], prev=None, below=up(up1), above=down(down1), coef=made[3]),
    ]

    for level in range(DEGREE):
        first, last = level == 0, level == DEGREE - 1
        for k, s in enumerate(chunks):
            apart = s.pop("apart", [])
            arrays = [s["v"]] + ([] if first else [s["prev"]]) + [s["below"], s["above"]]
            arrays += apart + [s["coef"], kb, ch, cl, th, tl, pot]
            out = [f32(6, cells, LANES)]
            if last:
                out += [f32(rim_rows * n, LANES) for n in (1, 2 - k, 1, 1)]
            else:
                arrays += [mh, ml]
                out += [f32(rim_rows + 32, LANES)] * 2 + [f32(32, LANES)]
            made = call(
                functools.partial(
                    level_kernel, scales[level], recall[level], first, bool(apart), last, k == 0
                ),
                out,
                [yx] if last else [],
                arrays,
                [pltpu.VMEM((18, cells, LANES), F32)],
            )
            s["prev"], s["v"] = s["v"], made[0]
            if last:
                s["pieces"] = [made[1], across(made[3]), partner(made[2]), diagonal(made[4])]
                rest = made[4]
            else:
                s["coef"], s["below"], s["above"] = made[3], up(made[1]), down(made[2])

    tiles = [
        call(tile_kernel, [f32(4 * rim_rows, LANES)], [y1], s["pieces"])[0] for s in chunks
    ]
    mine, theirs = call(
        gram_kernel,
        [f32(128, bands * 128)] * 2,
        [],
        tiles + [sibling(t) for t in tiles],
    )
    rest = partner(rest)
    filtered = call(
        unpack_kernel,
        [f32(slab, cells, LANES)],
        [yx],
        [s["v"] for s in chunks] + [s["pieces"][2] for s in chunks] + [rest],
    )[0]
    total = call(
        functools.partial(order_kernel, 1.0 / (slab * cells * peers)),
        [f32(128, bands * 128)],
        [b1],
        [mine, across(theirs)],
        after=[rest],
    )[0]
    pieces = total.reshape(peers, 128 // peers, bands * 128)
    pieces = lax.all_to_all(pieces, "grid", 0, 0)
    piece = jnp.broadcast_to(jnp.sum(pieces, axis=0, keepdims=True), pieces.shape)
    gram = lax.all_to_all(piece, "grid", 0, 0).reshape(128, bands * 128)
    return (filtered.reshape(orbitals.shape), gram)


def solution(mesh):
    return jax.shard_map(
        shards,
        mesh=mesh,
        in_specs=(
            P("grid", None, None, "band"),
            P("grid", None, None),
            P("grid", None, None, None),
            P("grid", None),
            P(),
        ),
        out_specs=(P("grid", None, None, "band"), P("band", None)),
        check_vma=False,
    )
```

time: 197 us -> 164 us (0.83)
  waiting for transfers between devices: 47.4 us -> 27.2 us
  blocking collectives: 23 us -> 11.1 us
  local copies, waits for them, and re-layouts: 20.6 us -> 11.5 us
  starting transfers between devices: 55.7 us -> 60.6 us
  Pallas kernels: 48.1 us -> 51.9 us
    ppermute x35 -> x34, waiting for transfers between devices: 47.4 us -> 21.5 us  [move(): lax.ppermute(array, axis, [(i, target(i) % size) for i in range(size)])]
    all_to_all x1 -> x0, blocking collectives: 11.9 us -> none  [shards(): gram = lax.all_to_all(piece, 'grid', 0, 0).reshape(128, bands * 128)]
    unnamed x58 -> x65, local copies, waits for them, and re-layouts: 18 us -> 10.5 us
    all_to_all x0 -> x1, waiting for transfers between devices: none -> 5.14 us  [shards(): gram = lax.all_to_all(piece, 'grid', 0, 0).reshape(128, bands * 128)]
    pallas_call x19 -> x21, Pallas kernels: 48.1 us -> 51.9 us  [call(): pl.pallas_call(body, out_shape=out, in_specs=[SMEM] * len(scalars) + [VME...]
    all_to_all x0 -> x1, starting transfers between devices: none -> 3.57 us  [shards(): gram = lax.all_to_all(piece, 'grid', 0, 0).reshape(128, bands * 128)]
    ppermute x35 -> x34, starting transfers between devices: 55.7 us -> 56.4 us  [move(): lax.ppermute(array, axis, [(i, target(i) % size) for i in range(size)])]
  transfers between devices with their start and end apart: 35 -> 37, of which waited for: 13 -> 12; matrix products, arithmetic and copies ran while one was open for 1% -> 0% of each run, Pallas kernels for 22% -> 30%
where the time goes in v2:
time: 164 us
  starting transfers between devices  60.6 us (37%)
  Pallas kernels  51.9 us (32%)
  waiting for transfers between devices  27.2 us (17%)
  local copies, waits for them, and re-layouts  11.5 us (7%)
  blocking collectives  11.1 us (7%)
    ppermute x34, starting transfers between devices, move(): lax.ppermute(array, axis, [(i, target(i) % size) for i in range(size)])  56.4 us
    pallas_call x21, Pallas kernels, call(): pl.pallas_call(body, out_shape=out, in_specs=[SMEM] * len(scalars) + [VME...  51.9 us
    ppermute x34, waiting for transfers between devices, move(): lax.ppermute(array, axis, [(i, target(i) % size) for i in range(size)])  21.5 us
    all_to_all x1, blocking collectives, shards(): pieces = lax.all_to_all(pieces, 'grid', 0, 0)  11.1 us
    unnamed x65, local copies, waits for them, and re-layouts  10.5 us
    all_to_all x1, waiting for transfers between devices, shards(): gram = lax.all_to_all(piece, 'grid', 0, 0).reshape(128, bands * 128)  5.14 us
    all_to_all x1, starting transfers between devices, shards(): gram = lax.all_to_all(piece, 'grid', 0, 0).reshape(128, bands * 128)  3.57 us
  transfers between devices with their start and end apart: 37, of which 12 were waited for; matrix products, arithmetic and copies ran while one was open for 0% of the time, Pallas kernels for 30%

profile of v2, /device:TPU:0, one launch (start us, length us, event | category | flops | bytes accessed | tf_op | source)
XLA Modules:
  0.0 163.5 jit_solution(17426309719660976736)
XLA Ops:
  2.5 3.0 %collective-permute-start.3 = (f32[768,128]{1,0:T(8,128)S(1)}, f32[768,128]{1,0:T(8,128)S(1)}, u32[]{:S(2)}, u32[]{:S(2)}) collective-permute-start(f32[768,128]{1,0:T(8,128)S(1)} %shard_map.86.refs_3_), channel_id=1, source_target_pairs={{0,1},{1,0},{2,3},{3,2},{4,5},{5,4},{6,7},{7,6},{8,9},{9,8},{10,11... | collective-permute-start | bytes 1179656 | tf_op jit(solution)/shard_map/ppermute | solution.py:427
  8.4 4.1 %collective-permute-start.1 = (f32[6,16,256]{2,1,0:T(8,128)S(1)}, f32[6,16,256]{2,1,0:T(8,128)S(1)}, u32[]{:S(2)}, u32[]{:S(2)}) collective-permute-start(f32[6,16,256]{2,1,0:T(8,128)S(1)} %get-tuple-element.61), channel_id=1, source_target_pairs={{0,6},{1,3},{2,0},{3,5},{4,2},{5,7},{6,4},{7,1},{8,14},{9,11},{10,... | collective-permute-start | bytes 294920 | tf_op jit(solution)/shard_map/ppermute | solution.py:427
  13.7 3.5 %collective-permute-done.3.refs_2_.refs_3_ = f32[768,128]{1,0:T(8,128)S(1)} collective-permute-done((f32[768,128]{1,0:T(8,128)S(1)}, f32[768,128]{1,0:T(8,128)S(1)}, u32[]{:S(2)}, u32[]{:S(2)}) %collective-permute-start.3) | collective-permute-done | bytes 393248 | tf_op jit(solution)/shard_map/ppermute | solution.py:427
  17.7 2.5 %collective-permute-start.6 = (f32[792,128]{1,0:T(8,128)S(1)}, f32[792,128]{1,0:T(8,128)S(1)}, u32[]{:S(2)}, u32[]{:S(2)}) collective-permute-start(f32[792,128]{1,0:T(8,128)S(1)} %shard_map.89), channel_id=1, source_target_pairs={{0,1},{1,0},{2,3},{3,2},{4,5},{5,4},{6,7},{7,6},{8,9},{9,8},{10,11... | collective-permute-start | bytes 1216520 | tf_op jit(solution)/shard_map/ppermute | solution.py:427
  22.0 2.0 %collective-permute-done.refs_2_ = f32[18,16,256]{2,1,0:T(8,128)S(1)} collective-permute-done((f32[18,16,256]{2,1,0:T(8,128)S(1)}, f32[18,16,256]{2,1,0:T(8,128)S(1)}, u32[]{:S(2)}, u32[]{:S(2)}) %collective-permute-start) | collective-permute-done | bytes 294944 | tf_op jit(solution)/shard_map/ppermute | solution.py:427
  25.1 2.1 %collective-permute-start.4 = (f32[384,128]{1,0:T(8,128)}, f32[384,128]{1,0:T(8,128)}, u32[]{:S(2)}, u32[]{:S(2)}) collective-permute-start(f32[384,128]{1,0:T(8,128)} %get-tuple-element.64), channel_id=1, source_target_pairs={{0,2},{1,3},{2,4},{3,5},{4,6},{5,7},{6,0},{7,1},{8,10},{9,11},{10,... | collective-permute-start | bytes 589832 | tf_op jit(solution)/shard_map/ppermute | solution.py:427
  27.2 2.6 %collective-permute-start.5 = (f32[384,128]{1,0:T(8,128)}, f32[384,128]{1,0:T(8,128)}, u32[]{:S(2)}, u32[]{:S(2)}) collective-permute-start(f32[384,128]{1,0:T(8,128)} %get-tuple-element.65), channel_id=1, source_target_pairs={{0,6},{1,7},{2,0},{3,1},{4,2},{5,3},{6,4},{7,5},{8,14},{9,15},{10,... | collective-permute-start | bytes 589832 | tf_op jit(solution)/shard_map/ppermute | solution.py:427
  32.8 3.8 %collective-permute-start.11 = (f32[32,128]{1,0:T(8,128)S(1)}, f32[32,128]{1,0:T(8,128)S(1)}, u32[]{:S(2)}, u32[]{:S(2)}) collective-permute-start(f32[32,128]{1,0:T(8,128)S(1)} %shard_map.91.refs_5_), channel_id=1, source_target_pairs={{0,6},{1,7},{2,0},{3,1},{4,2},{5,3},{6,4},{7,5},{8,14},{9,15},{10,... | collective-permute-start | bytes 49160 | tf_op jit(solution)/shard_map/ppermute | solution.py:427
  40.5 3.1 %collective-permute-start.19 = (f32[416,128]{1,0:T(8,128)}, f32[416,128]{1,0:T(8,128)}, u32[]{:S(2)}, u32[]{:S(2)}) collective-permute-start(f32[416,128]{1,0:T(8,128)} %get-tuple-element.93), channel_id=1, source_target_pairs={{0,6},{1,7},{2,0},{3,1},{4,2},{5,3},{6,4},{7,5},{8,14},{9,15},{10,... | collective-permute-start | bytes 638984 | tf_op jit(solution)/shard_map/ppermute | solution.py:427
  45.9 4.7 %shard_map.94 = (f32[6,256,128]{2,1,0:T(8,128)S(1)}, f32[416,128]{1,0:T(8,128)S(1)}, f32[416,128]{1,0:T(8,128)S(1)}, f32[32,128]{1,0:T(8,128)S(1)}) custom-call(f32[6,256,128]{2,1,0:T(8,128)S(1)} %copy-done.9, f32[384,128]{1,0:T(8,128)} %collective-permute-done.4.refs_1_, f32[384,128]{1,0:T(8,128)} %collective-permute-done.5.refs_2_, ...), custom_call_target="tpu_custom_call" | custom-call | flops 1024 | bytes 1024 | tf_op jit(solution)/shard_map/pallas_call | solution.py:394
  50.7 3.8 %collective-permute-start.13 = (f32[416,128]{1,0:T(8,128)S(1)}, f32[416,128]{1,0:T(8,128)S(1)}, u32[]{:S(2)}, u32[]{:S(2)}) collective-permute-start(f32[416,128]{1,0:T(8,128)S(1)} %get-tuple-element.80), channel_id=1, source_target_pairs={{0,6},{1,7},{2,0},{3,1},{4,2},{5,3},{6,4},{7,5},{8,14},{9,15},{10,... | collective-permute-start | bytes 638984 | tf_op jit(solution)/shard_map/ppermute | solution.py:427
  54.5 4.6 %shard_map.98 = (f32[6,256,128]{2,1,0:T(8,128)S(1)}, f32[416,128]{1,0:T(8,128)S(1)}, f32[416,128]{1,0:T(8,128)S(1)}, f32[32,128]{1,0:T(8,128)S(1)}) custom-call(f32[6,256,128]{2,1,0:T(8,128)S(1)} %copy-done.15, f32[416,128]{1,0:T(8,128)} %collective-permute-done.18.refs_1_, f32[416,128]{1,0:T(8,128)} %collective-permute-done.19.refs_2_, ...), custom_call_target="tpu_custom_call" | custom-call | flops 1024 | bytes 1024 | tf_op jit(solution)/shard_map/pallas_call | solution.py:394
  59.2 3.8 %collective-permute-start.21 = (f32[416,128]{1,0:T(8,128)S(1)}, f32[416,128]{1,0:T(8,128)S(1)}, u32[]{:S(2)}, u32[]{:S(2)}) collective-permute-start(f32[416,128]{1,0:T(8,128)S(1)} %get-tuple-element.97), channel_id=1, source_target_pairs={{0,6},{1,7},{2,0},{3,1},{4,2},{5,3},{6,4},{7,5},{8,14},{9,15},{10,... | collective-permute-start | bytes 638984 | tf_op jit(solution)/shard_map/ppermute | solution.py:427
  63.2 4.6 %shard_map.95 = (f32[6,256,128]{2,1,0:T(8,128)S(1)}, f32[416,128]{1,0:T(8,128)S(1)}, f32[416,128]{1,0:T(8,128)S(1)}, f32[32,128]{1,0:T(8,128)S(1)}) custom-call(f32[6,256,128]{2,1,0:T(8,128)S(1)} %get-tuple-element.78.refs_0_.refs_1_, f32[6,256,128]{2,1,0:T(8,128)S(1)} %copy-done.9, f32[416,128]{1,0:T(8,128)S(1)} %collective-permute-done.12.refs_2_, ...), custom_call_target="tpu_custom_call" | custom-call | flops 1024 | bytes 1024 | tf_op jit(solution)/shard_map/pallas_call | solution.py:394
  68.3 3.3 %collective-permute-start.15 = (f32[416,128]{1,0:T(8,128)S(1)}, f32[416,128]{1,0:T(8,128)S(1)}, u32[]{:S(2)}, u32[]{:S(2)}) collective-permute-start(f32[416,128]{1,0:T(8,128)S(1)} %get-tuple-element.84), channel_id=1, source_target_pairs={{0,6},{1,7},{2,0},{3,1},{4,2},{5,3},{6,4},{7,5},{8,14},{9,15},{10,... | collective-permute-start | bytes 638984 | tf_op jit(solution)/shard_map/ppermute | solution.py:427
  72.6 5.4 %shard_map.99 = (f32[6,256,128]{2,1,0:T(8,128)S(1)}, f32[416,128]{1,0:T(8,128)}, f32[416,128]{1,0:T(8,128)}, f32[32,128]{1,0:T(8,128)S(1)}) custom-call(f32[6,256,128]{2,1,0:T(8,128)S(1)} %get-tuple-element.95.refs_0_.refs_1_, f32[6,256,128]{2,1,0:T(8,128)S(1)} %copy-done.15, f32[416,128]{1,0:T(8,128)S(1)} %collective-permute-done.20.refs_2_, ...), custom_call_target="tpu_custom_call" | custom-call | flops 1024 | bytes 1024 | tf_op jit(solution)/shard_map/pallas_call | solution.py:394
  78.5 3.4 %collective-permute-start.23 = (f32[416,128]{1,0:T(8,128)}, f32[416,128]{1,0:T(8,128)}, u32[]{:S(2)}, u32[]{:S(2)}) collective-permute-start(f32[416,128]{1,0:T(8,128)} %get-tuple-element.101), channel_id=1, source_target_pairs={{0,6},{1,7},{2,0},{3,1},{4,2},{5,3},{6,4},{7,5},{8,14},{9,15},{10,... | collective-permute-start | bytes 638984 | tf_op jit(solution)/shard_map/ppermute | solution.py:427
  81.9 5.4 %shard_map.96 = (f32[6,256,128]{2,1,0:T(8,128)S(1)}, f32[416,128]{1,0:T(8,128)}, f32[416,128]{1,0:T(8,128)}, f32[32,128]{1,0:T(8,128)S(1)}) custom-call(f32[6,256,128]{2,1,0:T(8,128)S(1)} %get-tuple-element.82.refs_0_.refs_2_, f32[6,256,128]{2,1,0:T(8,128)S(1)} %get-tuple-element.78.refs_0_.refs_1_, f32[416,128]{1,0:T(8,128)S(1)} %collective-permute-done.14.refs_2_, ...), custom_call_target="tpu_custom_call" | custom-call | flops 1024 | bytes 1024 | tf_op jit(solution)/shard_map/pallas_call | solution.py:394
  88.2 3.8 %collective-permute-start.17 = (f32[416,128]{1,0:T(8,128)}, f32[416,128]{1,0:T(8,128)}, u32[]{:S(2)}, u32[]{:S(2)}) collective-permute-start(f32[416,128]{1,0:T(8,128)} %get-tuple-element.88), channel_id=1, source_target_pairs={{0,6},{1,7},{2,0},{3,1},{4,2},{5,3},{6,4},{7,5},{8,14},{9,15},{10,... | collective-permute-start | bytes 638984 | tf_op jit(solution)/shard_map/ppermute | solution.py:427
  93.1 5.0 %shard_map.100 = (f32[6,256,128]{2,1,0:T(8,128)S(1)}, f32[416,128]{1,0:T(8,128)S(1)}, f32[416,128]{1,0:T(8,128)S(1)}, f32[32,128]{1,0:T(8,128)S(1)}) custom-call(f32[6,256,128]{2,1,0:T(8,128)S(1)} %get-tuple-element.99.refs_0_.refs_2_, f32[6,256,128]{2,1,0:T(8,128)S(1)} %copy-done.13, f32[416,128]{1,0:T(8,128)} %collective-permute-done.22.refs_2_, ...), custom_call_target="tpu_custom_call" | custom-call | flops 1024 | bytes 1024 | tf_op jit(solution)/shard_map/pallas_call | solution.py:394
  98.2 3.8 %collective-permute-start.25 = (f32[416,128]{1,0:T(8,128)S(1)}, f32[416,128]{1,0:T(8,128)S(1)}, u32[]{:S(2)}, u32[]{:S(2)}) collective-permute-start(f32[416,128]{1,0:T(8,128)S(1)} %get-tuple-element.105), channel_id=1, source_target_pairs={{0,6},{1,7},{2,0},{3,1},{4,2},{5,3},{6,4},{7,5},{8,14},{9,15},{10,... | collective-permute-start | bytes 638984 | tf_op jit(solution)/shard_map/ppermute | solution.py:427
  102.1 3.6 %shard_map.97 = (f32[6,256,128]{2,1,0:T(8,128)S(1)}, f32[384,128]{1,0:T(8,128)S(1)}, f32[768,128]{1,0:T(8,128)S(1)}, f32[384,128]{1,0:T(8,128)S(1)}, f32[384,128]{1,0:T(8,128)S(1)}) custom-call(s32[2]{0:T(128)S(1)} %pad_add_fusion.refs_0_, f32[6,256,128]{2,1,0:T(8,128)S(1)} %copy-done.19, f32[6,256,128]{2,1,0:T(8,128)S(1)} %copy-done.11, ...), custom_call_target="tpu_custom_call" | custom-call | flops 1024 | bytes 1024 | tf_op jit(solution)/shard_map/pallas_call | solution.py:394
  109.3 3.4 %shard_map.101 = (f32[6,256,128]{2,1,0:T(8,128)S(1)}, f32[384,128]{1,0:T(8,128)S(1)}, f32[384,128]{1,0:T(8,128)S(1)}, f32[384,128]{1,0:T(8,128)S(1)}, f32[384,128]{1,0:T(8,128)S(1)}) custom-call(s32[2]{0:T(128)S(1)} %pad_add_fusion.refs_0_, f32[6,256,128]{2,1,0:T(8,128)S(1)} %get-tuple-element.103.refs_1_, ...), custom_call_target="tpu_custom_call" | custom-call | flops 1024 | bytes 1024 | tf_op jit(solution)/shard_map/pallas_call | solution.py:394
  117.6 3.5 %collective-permute-done.26.refs_3_ = f32[768,128]{1,0:T(8,128)S(1)} collective-permute-done((f32[768,128]{1,0:T(8,128)S(1)}, f32[768,128]{1,0:T(8,128)S(1)}, u32[]{:S(2)}, u32[]{:S(2)}) %collective-permute-start.26) | collective-permute-done | bytes 393248 | tf_op jit(solution)/shard_map/ppermute | solution.py:427
  122.1 3.2 %collective-permute-done.27.refs_4_.refs_3_ = f32[384,128]{1,0:T(8,128)S(1)} collective-permute-done((f32[384,128]{1,0:T(8,128)S(1)}, f32[384,128]{1,0:T(8,128)S(1)}, u32[]{:S(2)}, u32[]{:S(2)}) %collective-permute-start.27) | collective-permute-done | bytes 196640 | tf_op jit(solution)/shard_map/ppermute | solution.py:427
  126.3 2.3 %collective-permute-done.34.refs_3_ = f32[1536,128]{1,0:T(8,128)S(1)} collective-permute-done((f32[1536,128]{1,0:T(8,128)S(1)}, f32[1536,128]{1,0:T(8,128)S(1)}, u32[]{:S(2)}, u32[]{:S(2)}) %collective-permute-start.34) | collective-permute-done | bytes 786464 | tf_op jit(solution)/shard_map/ppermute | solution.py:427
  128.6 1.8 %shard_map.105 = (f32[128,512]{1,0:T(8,128)S(1)}, f32[128,512]{1,0:T(8,128)S(1)}) custom-call(f32[1536,128]{1,0:T(8,128)S(1)} %shard_map.103.refs_0_, f32[1536,128]{1,0:T(8,128)S(1)} %shard_map.104.refs_1_, f32[1536,128]{1,0:T(8,128)S(1)} %collective-permute-done.33.refs_2_, f32[1536,128]{1,0:T(8,128)S(1)} %collective-permute-done.34.refs_3_), custom_call_target="tpu_custom_call" | custom-call | flops 1024 | bytes 1024 | tf_op jit(solution)/shard_map/pallas_call | solution.py:394
  133.4 5.2 %collective-permute-done.28.refs_5_.refs_3_ = f32[384,128]{1,0:T(8,128)S(1)} collective-permute-done((f32[384,128]{1,0:T(8,128)S(1)}, f32[384,128]{1,0:T(8,128)S(1)}, u32[]{:S(2)}, u32[]{:S(2)}) %collective-permute-start.28) | collective-permute-done | bytes 196640 | tf_op jit(solution)/shard_map/ppermute | solution.py:427
  138.9 11.1 %all_to_all.10 = f32[8,16,512]{2,1,0:T(8,128)S(1)} all-to-all(f32[8,16,512]{2,1,0:T(8,128)S(1)} %bitcast.13), channel_id=1, replica_groups=mesh['band'=4,'grid'=8] {'grid'}, dimensions={0} | all-to-all | bytes 524288 | tf_op jit(solution)/shard_map/all_to_all | solution.py:568
  150.7 3.6 %all-to-all-start.1 = ((f32[8,16,512]{2,1,0:T(8,128)}), f32[8,16,512]{2,1,0:T(8,128)S(1)}, u32[]{:S(2)}, u32[]{:S(2)}) async-start(f32[8,16,512]{2,1,0:T(8,128)} %broadcast_in_dim.15), calls=%async_computation.1 | async-start | bytes 524288 | tf_op jit(solution)/shard_map/all_to_all | solution.py:570
  154.3 3.4 %shard_map.102 = f32[12,256,128]{2,1,0:T(8,128)} custom-call(s32[2]{0:T(128)S(1)} %pad_add_fusion.refs_0_, f32[6,256,128]{2,1,0:T(8,128)S(1)} %copy-done.21, f32[6,256,128]{2,1,0:T(8,128)S(1)} %copy-done.23, f32[768,128]{1,0:T(8,128)S(1)} %collective-permute-done.26.refs_3_, f32[384,128]{1,0:T(8,128)S(1)} %collective-permute-done.27.refs_4_.refs_3_, ...), custom_call_target="tpu_custom_call" | custom-call | flops 1024 | bytes 1024 | tf_op jit(solution)/shard_map/pallas_call | solution.py:394
  157.7 5.1 %all-to-all-done.1 = f32[8,16,512]{2,1,0:T(8,128)S(1)} async-done(((f32[8,16,512]{2,1,0:T(8,128)}), f32[8,16,512]{2,1,0:T(8,128)S(1)}, u32[]{:S(2)}, u32[]{:S(2)}) %all-to-all-start.1) | async-done | bytes 262176 | tf_op jit(solution)/shard_map/all_to_all | solution.py:570
  (137 shorter events, 37.9 us)
Async XLA Ops:
  2.5 14.7 %collective-permute-start.3 = (f32[768,128]{1,0:T(8,128)S(1)}, f32[768,128]{1,0:T(8,128)S(1)}, u32[]{:S(2)}, u32[]{:S(2)}) collective-permute-start(f32[768,128]{1,0:T(8,128)S(1)} %shard_map.86.refs_3_), channel_id=1, source_target_pairs={{0,1},{1,0},{2,3},{3,2},{4,5},{5,4},{6,7},{7,6},{8,9},{9,8},{10,11... | collective-permute-start | bytes 1179656 | tf_op jit(solution)/shard_map/ppermute | solution.py:427
  8.4 15.6 %collective-permute-start = (f32[18,16,256]{2,1,0:T(8,128)S(1)}, f32[18,16,256]{2,1,0:T(8,128)S(1)}, u32[]{:S(2)}, u32[]{:S(2)}) collective-permute-start(f32[18,16,256]{2,1,0:T(8,128)S(1)} %get-tuple-element.60), channel_id=1, source_target_pairs={{0,1},{1,0},{2,3},{3,2},{4,5},{5,4},{6,7},{7,6},{8,9},{9,8},{10,11... | collective-permute-start | bytes 884744 | tf_op jit(solution)/shard_map/ppermute | solution.py:427
  8.4 13.6 %collective-permute-start.1 = (f32[6,16,256]{2,1,0:T(8,128)S(1)}, f32[6,16,256]{2,1,0:T(8,128)S(1)}, u32[]{:S(2)}, u32[]{:S(2)}) collective-permute-start(f32[6,16,256]{2,1,0:T(8,128)S(1)} %get-tuple-element.61), channel_id=1, source_target_pairs={{0,6},{1,3},{2,0},{3,5},{4,2},{5,7},{6,4},{7,1},{8,14},{9,11},{10,... | collective-permute-start | bytes 294920 | tf_op jit(solution)/shard_map/ppermute | solution.py:427
  12.5 9.5 %collective-permute-start.2 = (f32[6,16,256]{2,1,0:T(8,128)S(1)}, f32[6,16,256]{2,1,0:T(8,128)S(1)}, u32[]{:S(2)}, u32[]{:S(2)}) collective-permute-start(f32[6,16,256]{2,1,0:T(8,128)S(1)} %get-tuple-element.61), channel_id=1, source_target_pairs={{0,7},{1,2},{2,1},{3,4},{4,3},{5,6},{6,5},{7,0},{8,15},{9,10},{10,... | collective-permute-start | bytes 294920 | tf_op jit(solution)/shard_map/ppermute | solution.py:427
  17.7 18.9 %collective-permute-start.6 = (f32[792,128]{1,0:T(8,128)S(1)}, f32[792,128]{1,0:T(8,128)S(1)}, u32[]{:S(2)}, u32[]{:S(2)}) collective-permute-start(f32[792,128]{1,0:T(8,128)S(1)} %shard_map.89), channel_id=1, source_target_pairs={{0,1},{1,0},{2,3},{3,2},{4,5},{5,4},{6,7},{7,6},{8,9},{9,8},{10,11... | collective-permute-start | bytes 1216520 | tf_op jit(solution)/shard_map/ppermute | solution.py:427
  25.1 20.7 %collective-permute-start.4 = (f32[384,128]{1,0:T(8,128)}, f32[384,128]{1,0:T(8,128)}, u32[]{:S(2)}, u32[]{:S(2)}) collective-permute-start(f32[384,128]{1,0:T(8,128)} %get-tuple-element.64), channel_id=1, source_target_pairs={{0,2},{1,3},{2,4},{3,5},{4,6},{5,7},{6,0},{7,1},{8,10},{9,11},{10,... | collective-permute-start | bytes 589832 | tf_op jit(solution)/shard_map/ppermute | solution.py:427
  27.2 18.6 %collective-permute-start.5 = (f32[384,128]{1,0:T(8,128)}, f32[384,128]{1,0:T(8,128)}, u32[]{:S(2)}, u32[]{:S(2)}) collective-permute-start(f32[384,128]{1,0:T(8,128)} %get-tuple-element.65), channel_id=1, source_target_pairs={{0,6},{1,7},{2,0},{3,1},{4,2},{5,3},{6,4},{7,5},{8,14},{9,15},{10,... | collective-permute-start | bytes 589832 | tf_op jit(solution)/shard_map/ppermute | solution.py:427
  32.7 7.1 %collective-permute-start.10 = (f32[32,128]{1,0:T(8,128)S(1)}, f32[32,128]{1,0:T(8,128)S(1)}, u32[]{:S(2)}, u32[]{:S(2)}) collective-permute-start(f32[32,128]{1,0:T(8,128)S(1)} %shard_map.91.refs_5_), channel_id=1, source_target_pairs={{0,2},{1,3},{2,4},{3,5},{4,6},{5,7},{6,0},{7,1},{8,10},{9,11},{10,... | collective-permute-start | bytes 49160 | tf_op jit(solution)/shard_map/ppermute | solution.py:427
  32.8 7.0 %collective-permute-start.11 = (f32[32,128]{1,0:T(8,128)S(1)}, f32[32,128]{1,0:T(8,128)S(1)}, u32[]{:S(2)}, u32[]{:S(2)}) collective-permute-start(f32[32,128]{1,0:T(8,128)S(1)} %shard_map.91.refs_5_), channel_id=1, source_target_pairs={{0,6},{1,7},{2,0},{3,1},{4,2},{5,3},{6,4},{7,5},{8,14},{9,15},{10,... | collective-permute-start | bytes 49160 | tf_op jit(solution)/shard_map/ppermute | solution.py:427
  39.8 14.7 %collective-permute-start.18 = (f32[416,128]{1,0:T(8,128)}, f32[416,128]{1,0:T(8,128)}, u32[]{:S(2)}, u32[]{:S(2)}) collective-permute-start(f32[416,128]{1,0:T(8,128)} %get-tuple-element.92), channel_id=1, source_target_pairs={{0,2},{1,3},{2,4},{3,5},{4,6},{5,7},{6,0},{7,1},{8,10},{9,11},{10,... | collective-permute-start | bytes 638984 | tf_op jit(solution)/shard_map/ppermute | solution.py:427
  40.5 14.0 %collective-permute-start.19 = (f32[416,128]{1,0:T(8,128)}, f32[416,128]{1,0:T(8,128)}, u32[]{:S(2)}, u32[]{:S(2)}) collective-permute-start(f32[416,128]{1,0:T(8,128)} %get-tuple-element.93), channel_id=1, source_target_pairs={{0,6},{1,7},{2,0},{3,1},{4,2},{5,3},{6,4},{7,5},{8,14},{9,15},{10,... | collective-permute-start | bytes 638984 | tf_op jit(solution)/shard_map/ppermute | solution.py:427
  50.6 12.4 %collective-permute-start.12 = (f32[416,128]{1,0:T(8,128)S(1)}, f32[416,128]{1,0:T(8,128)S(1)}, u32[]{:S(2)}, u32[]{:S(2)}) collective-permute-start(f32[416,128]{1,0:T(8,128)S(1)} %get-tuple-element.79), channel_id=1, source_target_pairs={{0,2},{1,3},{2,4},{3,5},{4,6},{5,7},{6,0},{7,1},{8,10},{9,11},{10,... | collective-permute-start | bytes 638984 | tf_op jit(solution)/shard_map/ppermute | solution.py:427
  50.7 12.4 %collective-permute-start.13 = (f32[416,128]{1,0:T(8,128)S(1)}, f32[416,128]{1,0:T(8,128)S(1)}, u32[]{:S(2)}, u32[]{:S(2)}) collective-permute-start(f32[416,128]{1,0:T(8,128)S(1)} %get-tuple-element.80), channel_id=1, source_target_pairs={{0,6},{1,7},{2,0},{3,1},{4,2},{5,3},{6,4},{7,5},{8,14},{9,15},{10,... | collective-permute-start | bytes 638984 | tf_op jit(solution)/shard_map/ppermute | solution.py:427
  59.2 12.5 %collective-permute-start.20 = (f32[416,128]{1,0:T(8,128)S(1)}, f32[416,128]{1,0:T(8,128)S(1)}, u32[]{:S(2)}, u32[]{:S(2)}) collective-permute-start(f32[416,128]{1,0:T(8,128)S(1)} %get-tuple-element.96), channel_id=1, source_target_pairs={{0,2},{1,3},{2,4},{3,5},{4,6},{5,7},{6,0},{7,1},{8,10},{9,11},{10,... | collective-permute-start | bytes 638984 | tf_op jit(solution)/shard_map/ppermute | solution.py:427
  59.2 13.4 %collective-permute-start.21 = (f32[416,128]{1,0:T(8,128)S(1)}, f32[416,128]{1,0:T(8,128)S(1)}, u32[]{:S(2)}, u32[]{:S(2)}) collective-permute-start(f32[416,128]{1,0:T(8,128)S(1)} %get-tuple-element.97), channel_id=1, source_target_pairs={{0,6},{1,7},{2,0},{3,1},{4,2},{5,3},{6,4},{7,5},{8,14},{9,15},{10,... | collective-permute-start | bytes 638984 | tf_op jit(solution)/shard_map/ppermute | solution.py:427
  67.8 14.0 %collective-permute-start.14 = (f32[416,128]{1,0:T(8,128)S(1)}, f32[416,128]{1,0:T(8,128)S(1)}, u32[]{:S(2)}, u32[]{:S(2)}) collective-permute-start(f32[416,128]{1,0:T(8,128)S(1)} %get-tuple-element.83), channel_id=1, source_target_pairs={{0,2},{1,3},{2,4},{3,5},{4,6},{5,7},{6,0},{7,1},{8,10},{9,11},{10,... | collective-permute-start | bytes 638984 | tf_op jit(solution)/shard_map/ppermute | solution.py:427
  68.3 13.5 %collective-permute-start.15 = (f32[416,128]{1,0:T(8,128)S(1)}, f32[416,128]{1,0:T(8,128)S(1)}, u32[]{:S(2)}, u32[]{:S(2)}) collective-permute-start(f32[416,128]{1,0:T(8,128)S(1)} %get-tuple-element.84), channel_id=1, source_target_pairs={{0,6},{1,7},{2,0},{3,1},{4,2},{5,3},{6,4},{7,5},{8,14},{9,15},{10,... | collective-permute-start | bytes 638984 | tf_op jit(solution)/shard_map/ppermute | solution.py:427
  78.0 13.9 %collective-permute-start.22 = (f32[416,128]{1,0:T(8,128)}, f32[416,128]{1,0:T(8,128)}, u32[]{:S(2)}, u32[]{:S(2)}) collective-permute-start(f32[416,128]{1,0:T(8,128)} %get-tuple-element.100), channel_id=1, source_target_pairs={{0,2},{1,3},{2,4},{3,5},{4,6},{5,7},{6,0},{7,1},{8,10},{9,11},{10,... | collective-permute-start | bytes 638984 | tf_op jit(solution)/shard_map/ppermute | solution.py:427
  78.5 13.5 %collective-permute-start.23 = (f32[416,128]{1,0:T(8,128)}, f32[416,128]{1,0:T(8,128)}, u32[]{:S(2)}, u32[]{:S(2)}) collective-permute-start(f32[416,128]{1,0:T(8,128)} %get-tuple-element.101), channel_id=1, source_target_pairs={{0,6},{1,7},{2,0},{3,1},{4,2},{5,3},{6,4},{7,5},{8,14},{9,15},{10,... | collective-permute-start | bytes 638984 | tf_op jit(solution)/shard_map/ppermute | solution.py:427
  88.2 13.9 %collective-permute-start.16 = (f32[416,128]{1,0:T(8,128)}, f32[416,128]{1,0:T(8,128)}, u32[]{:S(2)}, u32[]{:S(2)}) collective-permute-start(f32[416,128]{1,0:T(8,128)} %get-tuple-element.87), channel_id=1, source_target_pairs={{0,2},{1,3},{2,4},{3,5},{4,6},{5,7},{6,0},{7,1},{8,10},{9,11},{10,... | collective-permute-start | bytes 638984 | tf_op jit(solution)/shard_map/ppermute | solution.py:427
  88.2 13.9 %collective-permute-start.17 = (f32[416,128]{1,0:T(8,128)}, f32[416,128]{1,0:T(8,128)}, u32[]{:S(2)}, u32[]{:S(2)}) collective-permute-start(f32[416,128]{1,0:T(8,128)} %get-tuple-element.88), channel_id=1, source_target_pairs={{0,6},{1,7},{2,0},{3,1},{4,2},{5,3},{6,4},{7,5},{8,14},{9,15},{10,... | collective-permute-start | bytes 638984 | tf_op jit(solution)/shard_map/ppermute | solution.py:427
  98.1 11.1 %collective-permute-start.24 = (f32[416,128]{1,0:T(8,128)S(1)}, f32[416,128]{1,0:T(8,128)S(1)}, u32[]{:S(2)}, u32[]{:S(2)}) collective-permute-start(f32[416,128]{1,0:T(8,128)S(1)} %get-tuple-element.104), channel_id=1, source_target_pairs={{0,2},{1,3},{2,4},{3,5},{4,6},{5,7},{6,0},{7,1},{8,10},{9,11},{10,... | collective-permute-start | bytes 638984 | tf_op jit(solution)/shard_map/ppermute | solution.py:427
  98.2 11.1 %collective-permute-start.25 = (f32[416,128]{1,0:T(8,128)S(1)}, f32[416,128]{1,0:T(8,128)S(1)}, u32[]{:S(2)}, u32[]{:S(2)}) collective-permute-start(f32[416,128]{1,0:T(8,128)S(1)} %get-tuple-element.105), channel_id=1, source_target_pairs={{0,6},{1,7},{2,0},{3,1},{4,2},{5,3},{6,4},{7,5},{8,14},{9,15},{10,... | collective-permute-start | bytes 638984 | tf_op jit(solution)/shard_map/ppermute | solution.py:427
  105.7 15.4 %collective-permute-start.26 = (f32[768,128]{1,0:T(8,128)S(1)}, f32[768,128]{1,0:T(8,128)S(1)}, u32[]{:S(2)}, u32[]{:S(2)}) collective-permute-start(f32[768,128]{1,0:T(8,128)S(1)} %get-tuple-element.108), channel_id=1, source_target_pairs={{0,1},{1,0},{2,3},{3,2},{4,5},{5,4},{6,7},{7,6},{8,9},{9,8},{10,11... | collective-permute-start | bytes 1179656 | tf_op jit(solution)/shard_map/ppermute | solution.py:427
  107.5 9.3 %collective-permute-start.29 = (f32[384,128]{1,0:T(8,128)S(1)}, f32[384,128]{1,0:T(8,128)S(1)}, u32[]{:S(2)}, u32[]{:S(2)}) collective-permute-start(f32[384,128]{1,0:T(8,128)S(1)} %get-tuple-element.112), channel_id=1, source_target_pairs={{0,16},{8,24},{16,0},{24,8},{1,17},{9,25},{17,1},{25,9},{2,18},{10... | collective-permute-start | bytes 589832 | tf_op jit(solution)/shard_map/ppermute | solution.py:427
  108.9 8.7 %collective-permute-start.30 = (f32[384,128]{1,0:T(8,128)S(1)}, f32[384,128]{1,0:T(8,128)S(1)}, u32[]{:S(2)}, u32[]{:S(2)}) collective-permute-start(f32[384,128]{1,0:T(8,128)S(1)} %get-tuple-element.113), channel_id=1, source_target_pairs={{0,17},{1,16},{2,19},{3,18},{4,21},{5,20},{6,23},{7,22},{8,25},{9,... | collective-permute-start | bytes 589832 | tf_op jit(solution)/shard_map/ppermute | solution.py:451
  113.6 11.7 %collective-permute-start.27 = (f32[384,128]{1,0:T(8,128)S(1)}, f32[384,128]{1,0:T(8,128)S(1)}, u32[]{:S(2)}, u32[]{:S(2)}) collective-permute-start(f32[384,128]{1,0:T(8,128)S(1)} %get-tuple-element.109), channel_id=1, source_target_pairs={{0,1},{1,0},{2,3},{3,2},{4,5},{5,4},{6,7},{7,6},{8,9},{9,8},{10,11... | collective-permute-start | bytes 589832 | tf_op jit(solution)/shard_map/ppermute | solution.py:427
  115.3 10.0 %collective-permute-start.31 = (f32[384,128]{1,0:T(8,128)S(1)}, f32[384,128]{1,0:T(8,128)S(1)}, u32[]{:S(2)}, u32[]{:S(2)}) collective-permute-start(f32[384,128]{1,0:T(8,128)S(1)} %get-tuple-element.115), channel_id=1, source_target_pairs={{0,16},{8,24},{16,0},{24,8},{1,17},{9,25},{17,1},{25,9},{2,18},{10... | collective-permute-start | bytes 589832 | tf_op jit(solution)/shard_map/ppermute | solution.py:427
  116.7 8.6 %collective-permute-start.32 = (f32[384,128]{1,0:T(8,128)S(1)}, f32[384,128]{1,0:T(8,128)S(1)}, u32[]{:S(2)}, u32[]{:S(2)}) collective-permute-start(f32[384,128]{1,0:T(8,128)S(1)} %get-tuple-element.110), channel_id=1, source_target_pairs={{0,17},{1,16},{2,19},{3,18},{4,21},{5,20},{6,23},{7,22},{8,25},{9,... | collective-permute-start | bytes 589832 | tf_op jit(solution)/shard_map/ppermute | solution.py:451
  130.4 8.4 %collective-permute-start.35 = (f32[128,512]{1,0:T(8,128)S(1)}, f32[128,512]{1,0:T(8,128)S(1)}, u32[]{:S(2)}, u32[]{:S(2)}) collective-permute-start(f32[128,512]{1,0:T(8,128)S(1)} %get-tuple-element.117), channel_id=1, source_target_pairs={{0,16},{8,24},{16,0},{24,8},{1,17},{9,25},{17,1},{25,9},{2,18},{10... | collective-permute-start | bytes 786440 | tf_op jit(solution)/shard_map/ppermute | solution.py:427
  131.9 6.7 %collective-permute-start.28 = (f32[384,128]{1,0:T(8,128)S(1)}, f32[384,128]{1,0:T(8,128)S(1)}, u32[]{:S(2)}, u32[]{:S(2)}) collective-permute-start(f32[384,128]{1,0:T(8,128)S(1)} %get-tuple-element.110), channel_id=1, source_target_pairs={{0,1},{1,0},{2,3},{3,2},{4,5},{5,4},{6,7},{7,6},{8,9},{9,8},{10,11... | collective-permute-start | bytes 589832 | tf_op jit(solution)/shard_map/ppermute | solution.py:427
  150.7 12.1 %all-to-all-start.1 = ((f32[8,16,512]{2,1,0:T(8,128)}), f32[8,16,512]{2,1,0:T(8,128)S(1)}, u32[]{:S(2)}, u32[]{:S(2)}) async-start(f32[8,16,512]{2,1,0:T(8,128)} %broadcast_in_dim.15), calls=%async_computation.1 | async-start | bytes 524288 | tf_op jit(solution)/shard_map/all_to_all | solution.py:570
  (37 other events, 314.7 us)

commit v3 on v2

--- a/solution.py
+++ b/solution.py
@@ -98,7 +98,7 @@
     out_ref = refs[-1]
     cells = x_ref.shape[1]
     group = lane_ids((cells, LANES)) // QUARTER
-    if chunk:
+    if len(refs) > 1:
         out_ref[3 * cells :] = refs[0][...]
     for r in range(3):
         row = None
@@ -120,10 +120,7 @@
 
 def assemble_kernel(chunk, y_ref, x_ref, got_ref, *refs):
     y = y_ref[0]
-    if chunk == 0:
-        v_ref, up_ref, down_ref = refs
-    else:
-        mh_ref, ml_ref, v_ref, up_ref, down_ref, coef_ref = refs
+    mh_ref, ml_ref, v_ref, up_ref, down_ref, coef_ref = refs
     cells = x_ref.shape[1]
     group = lane_ids((cells, LANES)) // QUARTER
     coef = None
@@ -137,11 +134,9 @@
         v_ref[r] = row
         rim_pack(row, up_ref, r, 3)
         rim_pack(row, down_ref, r, 0)
-        if chunk:
-            term = dot3(((mh_ref[r], ml_ref[r]), halves(row)))
-            coef = term if coef is None else coef + term
-    if chunk:
-        share_coef(coef, coef_ref, up_ref, down_ref)
+        term = dot3(((mh_ref[r], ml_ref[r]), halves(row)))
+        coef = term if coef is None else coef + term
+    share_coef(coef, coef_ref, up_ref, down_ref)
 
 
 def share_coef(coef, coef_ref, up_ref, down_ref):
@@ -167,23 +162,13 @@
     )
 
 
-def coef_kernel(v_ref, mh_ref, ml_ref, out_ref):
-    total = None
-    for r in range(6):
-        term = dot3(((mh_ref[r], ml_ref[r]), halves(v_ref[r])))
-        total = term if total is None else total + term
-    out_ref[...] = collapse(total)
-
-
-def level_kernel(scale, recall, first, apart, last, joined, *refs):
+def level_kernel(scale, recall, first, last, *refs):
     refs = list(refs)
     if last:
         yx_ref = refs.pop(0)
     v_ref = refs.pop(0)
     prev_ref = None if first else refs.pop(0)
     below_ref, above_ref = refs.pop(0), refs.pop(0)
-    if apart:
-        below_coef, above_coef = refs.pop(0), refs.pop(0)
     own_ref, kb_ref, ch_ref, cl_ref, th_ref, tl_ref, pot_ref = refs[:7]
     refs = refs[7:]
     if last:
@@ -195,8 +180,8 @@
     rim = 6 * part
     part_group = lane_ids((part, LANES)) // QUARTER
     cg = lane_ids((32, LANES)) // QUARTER
-    from_below = below_coef[...] if apart else below_ref[pl.ds(rim, 32), :]
-    from_above = above_coef[...] if apart else above_ref[pl.ds(rim, 32), :]
+    from_below = below_ref[pl.ds(rim, 32), :]
+    from_above = above_ref[pl.ds(rim, 32), :]
     total = own_ref[...] + jnp.where(cg % 2 == 0, turn(from_below, 32), turn(from_above, -32))
     total = total * kb_ref[...]
     rows = []
@@ -232,8 +217,6 @@
         if last:
             for flip, piece in enumerate((own_piece, x_piece, y_piece, d_piece)):
                 rim_pack(value, piece, r, lax.bitwise_xor(mine, flip))
-            if joined:
-                y_piece[pl.ds(rim + r * part, part), :] = d_piece[pl.ds(r * part, part), :]
         else:
             rim_pack(value, up_ref, r, 3)
             rim_pack(value, down_ref, r, 0)
@@ -243,14 +226,12 @@
         share_coef(coef, coef_ref, up_ref, down_ref)
 
 
-def unpack_kernel(yx_ref, v0_ref, v1_ref, y0_ref, y1_ref, rest_ref, out_ref):
+def unpack_kernel(yx_ref, v0_ref, v1_ref, y0_ref, y1_ref, o0_ref, o1_ref, out_ref):
     y, x = yx_ref[0], yx_ref[1]
     cells = v0_ref.shape[1]
     part = cells // 4
     group = lane_ids((part, LANES)) // QUARTER
-    rim = 6 * part
-    rest0_ref = y0_ref.at[pl.ds(rim, rim)]
-    for half, pieces in ((x, (y0_ref, y1_ref)), (1 - x, (rest0_ref, rest_ref))):
+    for half, pieces in ((x, (y0_ref, y1_ref)), (1 - x, (o0_ref, o1_ref))):
         for r in range(6):
             own = [turn(v_ref[r], QUARTER * (k - half)) for k, v_ref in enumerate((v0_ref, v1_ref))]
             for j in range(4):
@@ -269,7 +250,7 @@
 def tile_kernel(y_ref, own_ref, x_ref, y_piece_ref, d_ref, out_ref):
     y = y_ref[0]
     rows = own_ref.shape[0]
-    pieces = [own_ref[...], y_piece_ref[pl.ds(0, rows)], x_ref[...], d_ref[...]]
+    pieces = [own_ref[...], y_piece_ref[...], x_ref[...], d_ref[...]]
     group = lane_ids((rows, LANES)) // QUARTER
     for j in range(4):
         block = None
@@ -280,7 +261,9 @@
         out_ref[pl.ds(j * rows, rows), :] = block
 
 
-def gram_kernel(a0_ref, a1_ref, s0_ref, s1_ref, keep_ref, send_ref):
+def gram_kernel(
+    y_ref, a0_ref, a1_ref, s0_ref, s1_ref, own_ref, to_y_ref, to_x_ref, to_d_ref, parts_ref
+):
     def dot(p, q):
         return lax.dot_general(p, q, (((0,), (0,)), ((), ())), preferred_element_type=F32)
 
@@ -290,7 +273,7 @@
     left_high, left_low = high[:, :256], low[:, :256]
     total = dot(left_high, high) + (dot(left_high, low) + dot(left_low, high))
     group = lane_ids((32, LANES)) // QUARTER
-    for x_row, out_ref in ((0, keep_ref), (1, send_ref)):
+    for x_row in range(2):
         for h_row in range(2):
             for k_row in range(2):
                 at = 128 * k_row + 64 * x_row + 32 * h_row
@@ -308,18 +291,43 @@
                                 else jnp.where(group == 2 * h + k, piece, block)
                             )
                     to = 2 * (x_col ^ x_row) + core
-                    out_ref[
-                        pl.ds(64 * h_row + 32 * k_row, 32), 128 * to : 128 * to + 128
-                    ] = block
-
-
-def order_kernel(factor, b_ref, keep_ref, got_ref, out_ref):
-    b = b_ref[0]
-    for j, flip in enumerate((0, 1, 2, 3)):
-        cut = slice(j * 128, (j + 1) * 128)
-        block = (keep_ref[:, cut] + got_ref[:, cut]) * factor
-        target = pl.multiple_of(lax.bitwise_xor(b, flip) * 128, 128)
-        out_ref[:, pl.ds(target, 128)] = block
+                    rows = slice(32 * k_row, 32 * k_row + 32)
+                    parts_ref[2 * x_row + h_row, rows, 128 * to : 128 * to + 128] = block
+    y = y_ref[0]
+    own_ref[...] = parts_ref[y]
+    to_y_ref[...] = parts_ref[1 - y]
+    to_x_ref[...] = parts_ref[2 + y]
+    to_d_ref[...] = parts_ref[3 - y]
+
+
+def add_kernel(*refs):
+    *terms, out_ref = refs
+    out_ref[...] = (terms[0][...] + terms[1][...]) + (terms[2][...] + terms[3][...])
+
+
+def ring_add_kernel(factor, z_ref, *refs):
+    *terms, out_ref, slots = refs
+    count = len(terms)
+    for k, term in enumerate(terms):
+        slots[lax.rem(z_ref[0] - k + count, count)] = term[...]
+    total = slots[0]
+    for k in range(1, count):
+        total = total + slots[k]
+    out_ref[...] = total * factor
+
+
+def scale_kernel(factor, in_ref, out_ref):
+    out_ref[...] = in_ref[...] * factor
+
+
+def order_kernel(yb_ref, mine_ref, got_ref, out_ref):
+    y, b = yb_ref[0], yb_ref[1]
+    half = mine_ref.shape[0]
+    for ref, h in ((mine_ref, y), (got_ref, 1 - y)):
+        rows = pl.ds(pl.multiple_of(half * h, half), half)
+        for j in range(4):
+            to = pl.multiple_of(lax.bitwise_xor(b, j) * 128, 128)
+            out_ref[rows, pl.ds(to, 128)] = ref[:, j * 128 : (j + 1) * 128]
 
 
 def dense_kernel(yc_ref, planes_ref, proj_ref, e_ref, part_ref, rim_ref):
@@ -357,20 +365,26 @@
             out_ref[r, h * LANES : (h + 1) * LANES] = row
 
 
-def maps_kernel(
-    yc_ref, e_ref, part_ref, part2_ref, a_ref, a2_ref, b_ref, b2_ref,
-    mh_ref, ml_ref, th_ref, tl_ref,
-):
+def gather_kernel(y_ref, part_ref, a_ref, b_ref, out_ref):
+    y = y_ref[0]
+    out_ref[:18] = part_ref[...]
+    for r in range(6):
+        one, two = a_ref[r], b_ref[r]
+        out_ref[18 + r] = jnp.where(y == 1, one, two)
+        out_ref[24 + r] = jnp.where(y == 1, two, one)
+
+
+def maps_kernel(yc_ref, e_ref, part_ref, part2_ref, mh_ref, ml_ref, th_ref, tl_ref):
     y, c = yc_ref[0], yc_ref[1]
 
-    def whole(mine, rest):
+    def whole(plane):
+        mine, rest = part_ref[plane], part2_ref[plane]
         first, second = jnp.where(c == 0, mine, rest), jnp.where(c == 0, rest, mine)
         return jnp.concatenate([first, second], axis=0)
 
     for r in range(6):
-        one, two = whole(a_ref[r], a2_ref[r]), whole(b_ref[r], b2_ref[r])
-        below, above = jnp.where(y == 1, one, two), jnp.where(y == 1, two, one)
-        other = [whole(part_ref[6 * i + r], part2_ref[6 * i + r]) for i in range(3)]
+        below, above = whole(18 + r), whole(24 + r)
+        other = [whole(6 * i + r) for i in range(3)]
         low = [jnp.where(y == 0, e_ref[6 + 6 * i + r], other[i]) for i in range(3)]
         high = [jnp.where(y == 1, e_ref[6 * i + r], other[i]) for i in range(3)]
         block = jnp.concatenate(
@@ -397,17 +411,17 @@
         in_specs=[SMEM] * len(scalars) + [VMEM] * len(arrays) + [ANY] * len(after),
         out_specs=[VMEM] * len(out),
         scratch_shapes=list(scratch),
-        compiler_params=pltpu.CompilerParams(vmem_limit_bytes=48 * 1024 * 1024),
+        compiler_params=pltpu.CompilerParams(vmem_limit_bytes=16 * 1024 * 1024),
         cost_estimate=pl.CostEstimate(flops=1 << 10, bytes_accessed=1 << 10, transcendentals=0),
     )(*scalars, *arrays, *after)
 
 
 def f32(*shape):
-    return jax.ShapeDtypeStruct(shape, F32)
+    return pltpu.VMEM(shape, F32)
 
 
 def bf16(*shape):
-    return jax.ShapeDtypeStruct(shape, BF16)
+    return pltpu.VMEM(shape, BF16)
 
 
 def shards(orbitals, potential, projectors, atom_planes, kb_energy):
@@ -418,7 +432,8 @@
     g, b = lax.axis_index("grid"), lax.axis_index("band")
     y, c, x = lax.rem(g, 2), lax.rem(b, 2), b // 2
     y1 = y.reshape(1).astype(jnp.int32)
-    b1 = b.reshape(1).astype(jnp.int32)
+    z1 = (g // 2).reshape(1).astype(jnp.int32)
+    yb = jnp.stack([y, b]).astype(jnp.int32)
     yc = jnp.stack([y, c]).astype(jnp.int32)
     yx = jnp.stack([y, x]).astype(jnp.int32)
 
@@ -474,19 +489,14 @@
         after=[other0],
     )[0]
     other1 = partner(sent1)
-    other = [other0, other1]
-    first_made = call(
-        functools.partial(assemble_kernel, 0),
-        [f32(6, cells, LANES)] + [f32(rim_rows, LANES)] * 2,
-        [y1],
-        [field, other0],
-    )
-    part, rim_a, rim_b, v0 = lax.optimization_barrier((part, rim_a, rim_b, first_made[0]))
+    part = call(
+        gather_kernel, [f32(30, 16, cells)], [y1], [part, rim_a, rim_b], after=[sent1]
+    )[0]
     mh, ml, th, tl = call(
         maps_kernel,
         [bf16(6, 256, cells)] * 2 + [bf16(6, cells, 256)] * 2,
         [yc],
-        [dense, part, sibling(part), rim_a, sibling(rim_a), rim_b, sibling(rim_b)],
+        [dense, part, sibling(part)],
     )
     pot = call(
         functools.partial(potential_kernel, -(middle + 0.5 * WEIGHTS[0])),
@@ -497,38 +507,31 @@
     kb = jnp.broadcast_to(jnp.tile(kb_energy, 4)[:, None], (32, LANES))
     ch, cl = (jnp.asarray(m) for m in plane_matrix(ny, nz))
 
-    s = dict(v=v0, prev=None, below=up(first_made[1]), above=down(first_made[2]))
-    s["coef"] = call(coef_kernel, [f32(32, LANES)], [], [v0, mh, ml])[0]
-    s["apart"] = [up(s["coef"]), down(s["coef"])]
-    made = call(
-        functools.partial(assemble_kernel, 1),
-        [f32(6, cells, LANES)] + [f32(rim_rows + 32, LANES)] * 2 + [f32(32, LANES)],
-        [y1],
-        [field, other1, mh, ml],
-        after=[s["coef"]],
-    )
-    up1, down1, s["apart"] = lax.optimization_barrier((made[1], made[2], s["apart"]))
-    chunks = [
-        s,
-        dict(v=made[0], prev=None, below=up(up1), above=down(down1), coef=made[3]),
-    ]
+    chunks = []
+    for k, got in enumerate((other0, other1)):
+        made = call(
+            functools.partial(assemble_kernel, k),
+            [f32(6, cells, LANES)] + [f32(rim_rows + 32, LANES)] * 2 + [f32(32, LANES)],
+            [y1],
+            [field, got, mh, ml],
+        )
+        chunks.append(
+            dict(v=made[0], prev=None, below=up(made[1]), above=down(made[2]), coef=made[3])
+        )
 
     for level in range(DEGREE):
         first, last = level == 0, level == DEGREE - 1
-        for k, s in enumerate(chunks):
-            apart = s.pop("apart", [])
+        for s in chunks:
             arrays = [s["v"]] + ([] if first else [s["prev"]]) + [s["below"], s["above"]]
-            arrays += apart + [s["coef"], kb, ch, cl, th, tl, pot]
+            arrays += [s["coef"], kb, ch, cl, th, tl, pot]
             out = [f32(6, cells, LANES)]
             if last:
-                out += [f32(rim_rows * n, LANES) for n in (1, 2 - k, 1, 1)]
+                out += [f32(rim_rows, LANES)] * 4
             else:
                 arrays += [mh, ml]
                 out += [f32(rim_rows + 32, LANES)] * 2 + [f32(32, LANES)]
             made = call(
-                functools.partial(
-                    level_kernel, scales[level], recall[level], first, bool(apart), last, k == 0
-                ),
+                functools.partial(level_kernel, scales[level], recall[level], first, last),
                 out,
                 [yx] if last else [],
                 arrays,
@@ -537,37 +540,62 @@
             s["prev"], s["v"] = s["v"], made[0]
             if last:
                 s["pieces"] = [made[1], across(made[3]), partner(made[2]), diagonal(made[4])]
-                rest = made[4]
+                s["rest"] = made[4]
             else:
                 s["coef"], s["below"], s["above"] = made[3], up(made[1]), down(made[2])
 
     tiles = [
         call(tile_kernel, [f32(4 * rim_rows, LANES)], [y1], s["pieces"])[0] for s in chunks
     ]
-    mine, theirs = call(
+    quarters = call(
         gram_kernel,
-        [f32(128, bands * 128)] * 2,
+        [f32(64, bands * 128)] * 4,
+        [y1],
+        tiles + [sibling(t) for t in tiles],
+        [pltpu.VMEM((4, 64, bands * 128), F32)],
+    )
+    partial = call(
+        add_kernel,
+        [f32(64, bands * 128)],
         [],
-        tiles + [sibling(t) for t in tiles],
+        [quarters[0], partner(quarters[1]), across(quarters[2]), diagonal(quarters[3])],
+    )[0]
+    rest0, rest1, partial = lax.optimization_barrier(
+        (chunks[0]["rest"], chunks[1]["rest"], partial)
     )
-    rest = partner(rest)
+    rest = [partner(rest0), partner(rest1)]
+    factor = 1.0 / (slab * cells * peers)
+    pairs = peers // 2
+    if pairs <= 4:
+        moved = [partial]
+        for k in range(1, pairs):
+            moved.append(move(partial, "grid", lambda i, k=k: i + 2 * k))
+        total = call(
+            functools.partial(ring_add_kernel, factor),
+            [f32(64, bands * 128)],
+            [z1],
+            moved,
+            [pltpu.VMEM((pairs, 64, bands * 128), F32)],
+            after=rest,
+        )[0]
+    else:
+        groups = [[2 * i + j for i in range(pairs)] for j in range(2)]
+        total = lax.psum(partial, "grid", axis_index_groups=groups)
+        total = call(
+            functools.partial(scale_kernel, factor), [f32(64, bands * 128)], [], [total]
+        )[0]
+    gram = call(
+        order_kernel,
+        [jax.ShapeDtypeStruct((128, bands * 128), F32)],
+        [yb],
+        [total, partner(total)],
+    )[0]
     filtered = call(
         unpack_kernel,
-        [f32(slab, cells, LANES)],
+        [jax.ShapeDtypeStruct((slab, cells, LANES), F32)],
         [yx],
-        [s["v"] for s in chunks] + [s["pieces"][2] for s in chunks] + [rest],
+        [s["v"] for s in chunks] + [s["pieces"][2] for s in chunks] + rest,
     )[0]
-    total = call(
-        functools.partial(order_kernel, 1.0 / (slab * cells * peers)),
-        [f32(128, bands * 128)],
-        [b1],
-        [mine, across(theirs)],
-        after=[rest],
-    )[0]
-    pieces = total.reshape(peers, 128 // peers, bands * 128)
-    pieces = lax.all_to_all(pieces, "grid", 0, 0)
-    piece = jnp.broadcast_to(jnp.sum(pieces, axis=0, keepdims=True), pieces.shape)
-    gram = lax.all_to_all(piece, "grid", 0, 0).reshape(128, bands * 128)
     return (filtered.reshape(orbitals.shape), gram)
 
 

time: 164 us -> 159 us (0.970)
  blocking collectives: 11.1 us -> 0 us
  waiting for transfers between devices: 27.2 us -> 38.3 us
  Pallas kernels: 51.9 us -> 47.9 us
  starting transfers between devices: 60.6 us -> 58.7 us
    all_to_all x1 -> x0, blocking collectives: 11.1 us -> none  [shards(): pieces = lax.all_to_all(pieces, 'grid', 0, 0)]
    ppermute x34 -> x36, waiting for transfers between devices: 21.5 us -> 32.5 us  [move(): lax.ppermute(array, axis, [(i, target(i) % size) for i in range(size)])]
    ppermute x2 -> x3, waiting for transfers between devices: 0.57 us -> 5.81 us  [diagonal(): lax.ppermute(array, ('band', 'grid'), [(i, i ^ flip) for i in range(size)])]
    all_to_all x1 -> x0, waiting for transfers between devices: 5.14 us -> none  [shards(): gram = lax.all_to_all(piece, 'grid', 0, 0).reshape(128, bands * 128)]
    pallas_call x21 -> x23, Pallas kernels: 51.9 us -> 47.9 us  [call(): pl.pallas_call(body, out_shape=out, in_specs=[SMEM] * len(scalars) + [VME...]
    all_to_all x1 -> x0, starting transfers between devices: 3.57 us -> none  [shards(): gram = lax.all_to_all(piece, 'grid', 0, 0).reshape(128, bands * 128)]
    unnamed x65 -> x76, local copies, waits for them, and re-layouts: 10.5 us -> 12.2 us
    ppermute x34 -> x36, starting transfers between devices: 56.4 us -> 57.2 us  [move(): lax.ppermute(array, axis, [(i, target(i) % size) for i in range(size)])]
  transfers between devices with their start and end apart: 37 -> 39, of which waited for: 12 -> 19; matrix products, arithmetic and copies ran while one was open for 0% -> 0% of each run, Pallas kernels for 30% -> 28%
where the time goes in v3:
time: 159 us
  starting transfers between devices  58.7 us (37%)
  Pallas kernels  47.9 us (30%)
  waiting for transfers between devices  38.3 us (24%)
  local copies, waits for them, and re-layouts  12.4 us (8%)
    ppermute x36, starting transfers between devices, move(): lax.ppermute(array, axis, [(i, target(i) % size) for i in range(size)])  57.2 us
    pallas_call x23, Pallas kernels, call(): pl.pallas_call(body, out_shape=out, in_specs=[SMEM] * len(scalars) + [VME...  47.9 us
    ppermute x36, waiting for transfers between devices, move(): lax.ppermute(array, axis, [(i, target(i) % size) for i in range(size)])  32.5 us
    unnamed x76, local copies, waits for them, and re-layouts  12.2 us
    ppermute x3, waiting for transfers between devices, diagonal(): lax.ppermute(array, ('band', 'grid'), [(i, i ^ flip) for i in range(size)])  5.81 us
  transfers between devices with their start and end apart: 39, of which 19 were waited for; matrix products, arithmetic and copies ran while one was open for 0% of the time, Pallas kernels for 28%

profile of v3, /device:TPU:0, one launch (start us, length us, event | category | flops | bytes accessed | tf_op | source)
XLA Modules:
  0.0 158.6 jit_solution(819843279783603851)
XLA Ops:
  2.5 3.0 %collective-permute-start = (f32[768,128]{1,0:T(8,128)S(1)}, f32[768,128]{1,0:T(8,128)S(1)}, u32[]{:S(2)}, u32[]{:S(2)}) collective-permute-start(f32[768,128]{1,0:T(8,128)S(1)} %shard_map.86.refs_3_), channel_id=1, source_target_pairs={{0,1},{1,0},{2,3},{3,2},{4,5},{5,4},{6,7},{7,6},{8,9},{9,8},{10,11... | collective-permute-start | bytes 1179656 | tf_op jit(solution)/shard_map/ppermute | solution.py:442
  8.3 4.1 %collective-permute-start.2 = (f32[6,16,256]{2,1,0:T(8,128)S(1)}, f32[6,16,256]{2,1,0:T(8,128)S(1)}, u32[]{:S(2)}, u32[]{:S(2)}) collective-permute-start(f32[6,16,256]{2,1,0:T(8,128)S(1)} %get-tuple-element.60), channel_id=1, source_target_pairs={{0,6},{1,3},{2,0},{3,5},{4,2},{5,7},{6,4},{7,1},{8,14},{9,11},{10,... | collective-permute-start | bytes 294920 | tf_op jit(solution)/shard_map/ppermute | solution.py:442
  13.7 3.5 %collective-permute-done.refs_3_.refs_2_ = f32[768,128]{1,0:T(8,128)S(1)} collective-permute-done((f32[768,128]{1,0:T(8,128)S(1)}, f32[768,128]{1,0:T(8,128)S(1)}, u32[]{:S(2)}, u32[]{:S(2)}) %collective-permute-start) | collective-permute-done | bytes 393248 | tf_op jit(solution)/shard_map/ppermute | solution.py:442
  17.7 2.1 %collective-permute-done.3.refs_3_ = f32[6,16,256]{2,1,0:T(8,128)S(1)} collective-permute-done((f32[6,16,256]{2,1,0:T(8,128)S(1)}, f32[6,16,256]{2,1,0:T(8,128)S(1)}, u32[]{:S(2)}, u32[]{:S(2)}) %collective-permute-start.3) | collective-permute-done | bytes 98336 | tf_op jit(solution)/shard_map/ppermute | solution.py:442
  19.8 3.3 %collective-permute-done.1.refs_1_ = f32[18,16,256]{2,1,0:T(8,128)S(1)} collective-permute-done((f32[18,16,256]{2,1,0:T(8,128)S(1)}, f32[18,16,256]{2,1,0:T(8,128)S(1)}, u32[]{:S(2)}, u32[]{:S(2)}) %collective-permute-start.1) | collective-permute-done | bytes 294944 | tf_op jit(solution)/shard_map/ppermute | solution.py:442
  30.4 2.1 %collective-permute-start.6 = (f32[416,128]{1,0:T(8,128)}, f32[416,128]{1,0:T(8,128)}, u32[]{:S(2)}, u32[]{:S(2)}) collective-permute-start(f32[416,128]{1,0:T(8,128)} %get-tuple-element.65), channel_id=1, source_target_pairs={{0,6},{1,7},{2,0},{3,1},{4,2},{5,3},{6,4},{7,5},{8,14},{9,15},{10,... | collective-permute-start | bytes 638984 | tf_op jit(solution)/shard_map/ppermute | solution.py:442
  32.5 2.6 %collective-permute-done.7.refs_2_ = f32[792,128]{1,0:T(8,128)S(1)} collective-permute-done((f32[792,128]{1,0:T(8,128)S(1)}, f32[792,128]{1,0:T(8,128)S(1)}, u32[]{:S(2)}, u32[]{:S(2)}) %collective-permute-start.7) | collective-permute-done | bytes 405536 | tf_op jit(solution)/shard_map/ppermute | solution.py:442
  39.5 2.0 %collective-permute-start.15 = (f32[416,128]{1,0:T(8,128)}, f32[416,128]{1,0:T(8,128)}, u32[]{:S(2)}, u32[]{:S(2)}) collective-permute-start(f32[416,128]{1,0:T(8,128)} %get-tuple-element.84), channel_id=1, source_target_pairs={{0,6},{1,7},{2,0},{3,1},{4,2},{5,3},{6,4},{7,5},{8,14},{9,15},{10,... | collective-permute-start | bytes 638984 | tf_op jit(solution)/shard_map/ppermute | solution.py:442
  44.9 4.3 %shard_map.93 = (f32[6,256,128]{2,1,0:T(8,128)S(1)}, f32[416,128]{1,0:T(8,128)S(1)}, f32[416,128]{1,0:T(8,128)S(1)}, f32[32,128]{1,0:T(8,128)S(1)}) custom-call(f32[6,256,128]{2,1,0:T(8,128)S(1)} %copy-done.18, f32[416,128]{1,0:T(8,128)} %collective-permute-done.5.refs_1_, f32[416,128]{1,0:T(8,128)} %collective-permute-done.6.refs_2_, ...), custom_call_target="tpu_custom_call" | custom-call | flops 1024 | bytes 1024 | tf_op jit(solution)/shard_map/pallas_call | solution.py:408
  49.5 3.6 %collective-permute-start.9 = (f32[416,128]{1,0:T(8,128)S(1)}, f32[416,128]{1,0:T(8,128)S(1)}, u32[]{:S(2)}, u32[]{:S(2)}) collective-permute-start(f32[416,128]{1,0:T(8,128)S(1)} %get-tuple-element.71), channel_id=1, source_target_pairs={{0,6},{1,7},{2,0},{3,1},{4,2},{5,3},{6,4},{7,5},{8,14},{9,15},{10,... | collective-permute-start | bytes 638984 | tf_op jit(solution)/shard_map/ppermute | solution.py:442
  53.2 4.4 %shard_map.98 = (f32[6,256,128]{2,1,0:T(8,128)S(1)}, f32[416,128]{1,0:T(8,128)S(1)}, f32[416,128]{1,0:T(8,128)S(1)}, f32[32,128]{1,0:T(8,128)S(1)}) custom-call(f32[6,256,128]{2,1,0:T(8,128)S(1)} %copy-done.16, f32[416,128]{1,0:T(8,128)} %collective-permute-done.14.refs_1_, f32[416,128]{1,0:T(8,128)} %collective-permute-done.15.refs_2_, ...), custom_call_target="tpu_custom_call" | custom-call | flops 1024 | bytes 1024 | tf_op jit(solution)/shard_map/pallas_call | solution.py:408
  57.6 3.8 %collective-permute-start.17 = (f32[416,128]{1,0:T(8,128)S(1)}, f32[416,128]{1,0:T(8,128)S(1)}, u32[]{:S(2)}, u32[]{:S(2)}) collective-permute-start(f32[416,128]{1,0:T(8,128)S(1)} %get-tuple-element.88), channel_id=1, source_target_pairs={{0,6},{1,7},{2,0},{3,1},{4,2},{5,3},{6,4},{7,5},{8,14},{9,15},{10,... | collective-permute-start | bytes 638984 | tf_op jit(solution)/shard_map/ppermute | solution.py:442
  63.0 3.3 %shard_map.94 = (f32[6,256,128]{2,1,0:T(8,128)S(1)}, f32[416,128]{1,0:T(8,128)S(1)}, f32[416,128]{1,0:T(8,128)S(1)}, f32[32,128]{1,0:T(8,128)S(1)}) custom-call(f32[6,256,128]{2,1,0:T(8,128)S(1)} %get-tuple-element.69.refs_0_.refs_1_, f32[6,256,128]{2,1,0:T(8,128)S(1)} %copy-done.19, f32[416,128]{1,0:T(8,128)S(1)} %collective-permute-done.8.refs_2_, ...), custom_call_target="tpu_custom_call" | custom-call | flops 1024 | bytes 1024 | tf_op jit(solution)/shard_map/pallas_call | solution.py:408
  66.3 3.4 %collective-permute-start.10 = (f32[416,128]{1,0:T(8,128)S(1)}, f32[416,128]{1,0:T(8,128)S(1)}, u32[]{:S(2)}, u32[]{:S(2)}) collective-permute-start(f32[416,128]{1,0:T(8,128)S(1)} %get-tuple-element.74), channel_id=1, source_target_pairs={{0,2},{1,3},{2,4},{3,5},{4,6},{5,7},{6,0},{7,1},{8,10},{9,11},{10,... | collective-permute-start | bytes 638984 | tf_op jit(solution)/shard_map/ppermute | solution.py:442
  70.2 1.9 %collective-permute-done.17.refs_3_ = f32[416,128]{1,0:T(8,128)S(1)} collective-permute-done((f32[416,128]{1,0:T(8,128)S(1)}, f32[416,128]{1,0:T(8,128)S(1)}, u32[]{:S(2)}, u32[]{:S(2)}) %collective-permute-start.17) | collective-permute-done | bytes 213024 | tf_op jit(solution)/shard_map/ppermute | solution.py:442
  72.1 4.1 %shard_map.99 = (f32[6,256,128]{2,1,0:T(8,128)S(1)}, f32[416,128]{1,0:T(8,128)}, f32[416,128]{1,0:T(8,128)}, f32[32,128]{1,0:T(8,128)S(1)}) custom-call(f32[6,256,128]{2,1,0:T(8,128)S(1)} %get-tuple-element.86.refs_0_.refs_1_, f32[6,256,128]{2,1,0:T(8,128)S(1)} %copy-done.16, f32[416,128]{1,0:T(8,128)S(1)} %collective-permute-done.16.refs_2_, ...), custom_call_target="tpu_custom_call" | custom-call | flops 1024 | bytes 1024 | tf_op jit(solution)/shard_map/pallas_call | solution.py:408
  78.5 2.3 %collective-permute-start.19 = (f32[416,128]{1,0:T(8,128)}, f32[416,128]{1,0:T(8,128)}, u32[]{:S(2)}, u32[]{:S(2)}) collective-permute-start(f32[416,128]{1,0:T(8,128)} %get-tuple-element.92), channel_id=1, source_target_pairs={{0,6},{1,7},{2,0},{3,1},{4,2},{5,3},{6,4},{7,5},{8,14},{9,15},{10,... | collective-permute-start | bytes 638984 | tf_op jit(solution)/shard_map/ppermute | solution.py:442
  81.7 4.0 %shard_map.95 = (f32[6,256,128]{2,1,0:T(8,128)S(1)}, f32[416,128]{1,0:T(8,128)}, f32[416,128]{1,0:T(8,128)}, f32[32,128]{1,0:T(8,128)S(1)}) custom-call(f32[6,256,128]{2,1,0:T(8,128)S(1)} %get-tuple-element.73.refs_0_.refs_2_, f32[6,256,128]{2,1,0:T(8,128)S(1)} %get-tuple-element.69.refs_0_.refs_1_, f32[416,128]{1,0:T(8,128)S(1)} %collective-permute-done.10.refs_2_, ...), custom_call_target="tpu_custom_call" | custom-call | flops 1024 | bytes 1024 | tf_op jit(solution)/shard_map/pallas_call | solution.py:408
  86.6 3.8 %collective-permute-start.13 = (f32[416,128]{1,0:T(8,128)}, f32[416,128]{1,0:T(8,128)}, u32[]{:S(2)}, u32[]{:S(2)}) collective-permute-start(f32[416,128]{1,0:T(8,128)} %get-tuple-element.79), channel_id=1, source_target_pairs={{0,6},{1,7},{2,0},{3,1},{4,2},{5,3},{6,4},{7,5},{8,14},{9,15},{10,... | collective-permute-start | bytes 638984 | tf_op jit(solution)/shard_map/ppermute | solution.py:442
  94.3 4.4 %shard_map.100 = (f32[6,256,128]{2,1,0:T(8,128)S(1)}, f32[416,128]{1,0:T(8,128)S(1)}, f32[416,128]{1,0:T(8,128)S(1)}, f32[32,128]{1,0:T(8,128)S(1)}) custom-call(f32[6,256,128]{2,1,0:T(8,128)S(1)} %copy-done.9, f32[6,256,128]{2,1,0:T(8,128)S(1)} %copy-done.14, f32[416,128]{1,0:T(8,128)} %collective-permute-done.18.refs_2_, ...), custom_call_target="tpu_custom_call" | custom-call | flops 1024 | bytes 1024 | tf_op jit(solution)/shard_map/pallas_call | solution.py:408
  99.0 3.6 %collective-permute-start.21 = (f32[416,128]{1,0:T(8,128)S(1)}, f32[416,128]{1,0:T(8,128)S(1)}, u32[]{:S(2)}, u32[]{:S(2)}) collective-permute-start(f32[416,128]{1,0:T(8,128)S(1)} %get-tuple-element.96), channel_id=1, source_target_pairs={{0,6},{1,7},{2,0},{3,1},{4,2},{5,3},{6,4},{7,5},{8,14},{9,15},{10,... | collective-permute-start | bytes 638984 | tf_op jit(solution)/shard_map/ppermute | solution.py:442
  102.7 4.0 %shard_map.96 = (f32[6,256,128]{2,1,0:T(8,128)S(1)}, f32[384,128]{1,0:T(8,128)S(1)}, f32[384,128]{1,0:T(8,128)S(1)}, f32[384,128]{1,0:T(8,128)S(1)}, f32[384,128]{1,0:T(8,128)}) custom-call(s32[2]{0:T(128)S(1)} %pad_add_fusion.refs_0_, f32[6,256,128]{2,1,0:T(8,128)S(1)} %copy-done.25, f32[6,256,128]{2,1,0:T(8,128)S(1)} %copy-done.12, ...), custom_call_target="tpu_custom_call" | custom-call | flops 1024 | bytes 1024 | tf_op jit(solution)/shard_map/pallas_call | solution.py:408
  110.2 3.5 %shard_map.101 = (f32[6,256,128]{2,1,0:T(8,128)S(1)}, f32[384,128]{1,0:T(8,128)S(1)}, f32[384,128]{1,0:T(8,128)S(1)}, f32[384,128]{1,0:T(8,128)S(1)}, f32[384,128]{1,0:T(8,128)}) custom-call(s32[2]{0:T(128)S(1)} %pad_add_fusion.refs_0_, f32[6,256,128]{2,1,0:T(8,128)S(1)} %get-tuple-element.94.refs_1_, f32[6,256,128]{2,1,0:T(8,128)S(1)} %copy-done.10, ...), custom_call_target="tpu_custom_call" | custom-call | flops 1024 | bytes 1024 | tf_op jit(solution)/shard_map/pallas_call | solution.py:408
  121.4 2.2 %collective-permute-done.27.refs_4_ = f32[384,128]{1,0:T(8,128)S(1)} collective-permute-done((f32[384,128]{1,0:T(8,128)}, f32[384,128]{1,0:T(8,128)S(1)}, u32[]{:S(2)}, u32[]{:S(2)}) %collective-permute-start.27) | collective-permute-done | bytes 196640 | tf_op jit(solution)/shard_map/ppermute | solution.py:466
  124.6 2.3 %collective-permute-done.29.refs_4_ = f32[1536,128]{1,0:T(8,128)S(1)} collective-permute-done((f32[1536,128]{1,0:T(8,128)S(1)}, f32[1536,128]{1,0:T(8,128)S(1)}, u32[]{:S(2)}, u32[]{:S(2)}) %collective-permute-start.29) | collective-permute-done | bytes 786464 | tf_op jit(solution)/shard_map/ppermute | solution.py:442
  126.8 1.9 %shard_map.104 = (f32[64,512]{1,0:T(8,128)S(1)}, f32[64,512]{1,0:T(8,128)S(1)}, f32[64,512]{1,0:T(8,128)S(1)}, f32[64,512]{1,0:T(8,128)S(1)}) custom-call(s32[1]{0:T(128)} %bitcast.refs_0_, f32[1536,128]{1,0:T(8,128)S(1)} %shard_map.102.refs_1_, f32[1536,128]{1,0:T(8,128)S(1)} %shard_map.103.refs_2_, f32[1536,128]{1,0:T(8,128)S(1)} %collective-permute-done.28.refs_3_, ...), custom_call_target="tpu_custom_call" | custom-call | flops 1024 | bytes 1024 | tf_op jit(solution)/shard_map/pallas_call | solution.py:408
  132.3 2.0 %collective-permute-done.30.refs_1_ = f32[64,512]{1,0:T(8,128)S(1)} collective-permute-done((f32[64,512]{1,0:T(8,128)S(1)}, f32[64,512]{1,0:T(8,128)S(1)}, u32[]{:S(2)}, u32[]{:S(2)}) %collective-permute-start.30) | collective-permute-done | bytes 131104 | tf_op jit(solution)/shard_map/ppermute | solution.py:442
  134.4 2.2 %collective-permute-done.31.refs_2_ = f32[64,512]{1,0:T(8,128)S(1)} collective-permute-done((f32[64,512]{1,0:T(8,128)S(1)}, f32[64,512]{1,0:T(8,128)S(1)}, u32[]{:S(2)}, u32[]{:S(2)}) %collective-permute-start.31) | collective-permute-done | bytes 131104 | tf_op jit(solution)/shard_map/ppermute | solution.py:442
  141.9 2.4 %collective-permute-start.37 = (f32[64,512]{1,0:T(8,128)S(1)}, f32[64,512]{1,0:T(8,128)S(1)}, u32[]{:S(2)}, u32[]{:S(2)}) collective-permute-start(f32[64,512]{1,0:T(8,128)S(1)} %shard_map.105.refs_1_), channel_id=1, source_target_pairs={{0,6},{1,7},{2,0},{3,1},{4,2},{5,3},{6,4},{7,5},{8,14},{9,15},{10,... | collective-permute-start | bytes 393224 | tf_op jit(solution)/shard_map/ppermute | solution.py:442
  144.3 4.5 %collective-permute-done.35.refs_2_ = f32[64,512]{1,0:T(8,128)S(1)} collective-permute-done((f32[64,512]{1,0:T(8,128)S(1)}, f32[64,512]{1,0:T(8,128)S(1)}, u32[]{:S(2)}, u32[]{:S(2)}) %collective-permute-start.35) | collective-permute-done | bytes 131104 | tf_op jit(solution)/shard_map/ppermute | solution.py:442
  148.8 3.5 %collective-permute-done.36.refs_3_ = f32[64,512]{1,0:T(8,128)S(1)} collective-permute-done((f32[64,512]{1,0:T(8,128)S(1)}, f32[64,512]{1,0:T(8,128)S(1)}, u32[]{:S(2)}, u32[]{:S(2)}) %collective-permute-start.36) | collective-permute-done | bytes 131104 | tf_op jit(solution)/shard_map/ppermute | solution.py:442
  153.5 3.4 %shard_map.106 = f32[12,256,128]{2,1,0:T(8,128)} custom-call(s32[2]{0:T(128)S(1)} %pad_add_fusion.refs_0_, f32[6,256,128]{2,1,0:T(8,128)S(1)} %copy-done.27, f32[6,256,128]{2,1,0:T(8,128)S(1)} %copy-done.29, f32[384,128]{1,0:T(8,128)S(1)} %copy-done.23, f32[384,128]{1,0:T(8,128)S(1)} %collective-permute-done.23.refs_3_.refs_4_, ...), custom_call_target="tpu_custom_call" | custom-call | flops 1024 | bytes 1024 | tf_op jit(solution)/shard_map/pallas_call | solution.py:408
  (152 shorter events, 56.1 us)
Async XLA Ops:
  2.5 14.7 %collective-permute-start = (f32[768,128]{1,0:T(8,128)S(1)}, f32[768,128]{1,0:T(8,128)S(1)}, u32[]{:S(2)}, u32[]{:S(2)}) collective-permute-start(f32[768,128]{1,0:T(8,128)S(1)} %shard_map.86.refs_3_), channel_id=1, source_target_pairs={{0,1},{1,0},{2,3},{3,2},{4,5},{5,4},{6,7},{7,6},{8,9},{9,8},{10,11... | collective-permute-start | bytes 1179656 | tf_op jit(solution)/shard_map/ppermute | solution.py:442
  8.3 14.8 %collective-permute-start.1 = (f32[18,16,256]{2,1,0:T(8,128)S(1)}, f32[18,16,256]{2,1,0:T(8,128)S(1)}, u32[]{:S(2)}, u32[]{:S(2)}) collective-permute-start(f32[18,16,256]{2,1,0:T(8,128)S(1)} %get-tuple-element.59), channel_id=1, source_target_pairs={{0,1},{1,0},{2,3},{3,2},{4,5},{5,4},{6,7},{7,6},{8,9},{9,8},{10,11... | collective-permute-start | bytes 884744 | tf_op jit(solution)/shard_map/ppermute | solution.py:442
  8.3 9.4 %collective-permute-start.2 = (f32[6,16,256]{2,1,0:T(8,128)S(1)}, f32[6,16,256]{2,1,0:T(8,128)S(1)}, u32[]{:S(2)}, u32[]{:S(2)}) collective-permute-start(f32[6,16,256]{2,1,0:T(8,128)S(1)} %get-tuple-element.60), channel_id=1, source_target_pairs={{0,6},{1,3},{2,0},{3,5},{4,2},{5,7},{6,4},{7,1},{8,14},{9,11},{10,... | collective-permute-start | bytes 294920 | tf_op jit(solution)/shard_map/ppermute | solution.py:442
  12.4 7.4 %collective-permute-start.3 = (f32[6,16,256]{2,1,0:T(8,128)S(1)}, f32[6,16,256]{2,1,0:T(8,128)S(1)}, u32[]{:S(2)}, u32[]{:S(2)}) collective-permute-start(f32[6,16,256]{2,1,0:T(8,128)S(1)} %get-tuple-element.60), channel_id=1, source_target_pairs={{0,7},{1,2},{2,1},{3,4},{4,3},{5,6},{6,5},{7,0},{8,15},{9,10},{10,... | collective-permute-start | bytes 294920 | tf_op jit(solution)/shard_map/ppermute | solution.py:442
  23.2 11.8 %collective-permute-start.7 = (f32[792,128]{1,0:T(8,128)S(1)}, f32[792,128]{1,0:T(8,128)S(1)}, u32[]{:S(2)}, u32[]{:S(2)}) collective-permute-start(f32[792,128]{1,0:T(8,128)S(1)} %shard_map.88.refs_4_), channel_id=1, source_target_pairs={{0,1},{1,0},{2,3},{3,2},{4,5},{5,4},{6,7},{7,6},{8,9},{9,8},{10,11... | collective-permute-start | bytes 1216520 | tf_op jit(solution)/shard_map/ppermute | solution.py:442
  28.6 15.1 %collective-permute-start.5 = (f32[416,128]{1,0:T(8,128)}, f32[416,128]{1,0:T(8,128)}, u32[]{:S(2)}, u32[]{:S(2)}) collective-permute-start(f32[416,128]{1,0:T(8,128)} %get-tuple-element.64), channel_id=1, source_target_pairs={{0,2},{1,3},{2,4},{3,5},{4,6},{5,7},{6,0},{7,1},{8,10},{9,11},{10,... | collective-permute-start | bytes 638984 | tf_op jit(solution)/shard_map/ppermute | solution.py:442
  30.4 13.3 %collective-permute-start.6 = (f32[416,128]{1,0:T(8,128)}, f32[416,128]{1,0:T(8,128)}, u32[]{:S(2)}, u32[]{:S(2)}) collective-permute-start(f32[416,128]{1,0:T(8,128)} %get-tuple-element.65), channel_id=1, source_target_pairs={{0,6},{1,7},{2,0},{3,1},{4,2},{5,3},{6,4},{7,5},{8,14},{9,15},{10,... | collective-permute-start | bytes 638984 | tf_op jit(solution)/shard_map/ppermute | solution.py:442
  37.7 15.5 %collective-permute-start.14 = (f32[416,128]{1,0:T(8,128)}, f32[416,128]{1,0:T(8,128)}, u32[]{:S(2)}, u32[]{:S(2)}) collective-permute-start(f32[416,128]{1,0:T(8,128)} %get-tuple-element.83), channel_id=1, source_target_pairs={{0,2},{1,3},{2,4},{3,5},{4,6},{5,7},{6,0},{7,1},{8,10},{9,11},{10,... | collective-permute-start | bytes 638984 | tf_op jit(solution)/shard_map/ppermute | solution.py:442
  39.5 13.7 %collective-permute-start.15 = (f32[416,128]{1,0:T(8,128)}, f32[416,128]{1,0:T(8,128)}, u32[]{:S(2)}, u32[]{:S(2)}) collective-permute-start(f32[416,128]{1,0:T(8,128)} %get-tuple-element.84), channel_id=1, source_target_pairs={{0,6},{1,7},{2,0},{3,1},{4,2},{5,3},{6,4},{7,5},{8,14},{9,15},{10,... | collective-permute-start | bytes 638984 | tf_op jit(solution)/shard_map/ppermute | solution.py:442
  49.3 12.2 %collective-permute-start.8 = (f32[416,128]{1,0:T(8,128)S(1)}, f32[416,128]{1,0:T(8,128)S(1)}, u32[]{:S(2)}, u32[]{:S(2)}) collective-permute-start(f32[416,128]{1,0:T(8,128)S(1)} %get-tuple-element.70), channel_id=1, source_target_pairs={{0,2},{1,3},{2,4},{3,5},{4,6},{5,7},{6,0},{7,1},{8,10},{9,11},{10,... | collective-permute-start | bytes 638984 | tf_op jit(solution)/shard_map/ppermute | solution.py:442
  49.5 13.5 %collective-permute-start.9 = (f32[416,128]{1,0:T(8,128)S(1)}, f32[416,128]{1,0:T(8,128)S(1)}, u32[]{:S(2)}, u32[]{:S(2)}) collective-permute-start(f32[416,128]{1,0:T(8,128)S(1)} %get-tuple-element.71), channel_id=1, source_target_pairs={{0,6},{1,7},{2,0},{3,1},{4,2},{5,3},{6,4},{7,5},{8,14},{9,15},{10,... | collective-permute-start | bytes 638984 | tf_op jit(solution)/shard_map/ppermute | solution.py:442
  57.5 12.6 %collective-permute-start.16 = (f32[416,128]{1,0:T(8,128)S(1)}, f32[416,128]{1,0:T(8,128)S(1)}, u32[]{:S(2)}, u32[]{:S(2)}) collective-permute-start(f32[416,128]{1,0:T(8,128)S(1)} %get-tuple-element.87), channel_id=1, source_target_pairs={{0,2},{1,3},{2,4},{3,5},{4,6},{5,7},{6,0},{7,1},{8,10},{9,11},{10,... | collective-permute-start | bytes 638984 | tf_op jit(solution)/shard_map/ppermute | solution.py:442
  57.6 14.5 %collective-permute-start.17 = (f32[416,128]{1,0:T(8,128)S(1)}, f32[416,128]{1,0:T(8,128)S(1)}, u32[]{:S(2)}, u32[]{:S(2)}) collective-permute-start(f32[416,128]{1,0:T(8,128)S(1)} %get-tuple-element.88), channel_id=1, source_target_pairs={{0,6},{1,7},{2,0},{3,1},{4,2},{5,3},{6,4},{7,5},{8,14},{9,15},{10,... | collective-permute-start | bytes 638984 | tf_op jit(solution)/shard_map/ppermute | solution.py:442
  66.3 14.6 %collective-permute-start.10 = (f32[416,128]{1,0:T(8,128)S(1)}, f32[416,128]{1,0:T(8,128)S(1)}, u32[]{:S(2)}, u32[]{:S(2)}) collective-permute-start(f32[416,128]{1,0:T(8,128)S(1)} %get-tuple-element.74), channel_id=1, source_target_pairs={{0,2},{1,3},{2,4},{3,5},{4,6},{5,7},{6,0},{7,1},{8,10},{9,11},{10,... | collective-permute-start | bytes 638984 | tf_op jit(solution)/shard_map/ppermute | solution.py:442
  69.6 12.1 %collective-permute-start.11 = (f32[416,128]{1,0:T(8,128)S(1)}, f32[416,128]{1,0:T(8,128)S(1)}, u32[]{:S(2)}, u32[]{:S(2)}) collective-permute-start(f32[416,128]{1,0:T(8,128)S(1)} %get-tuple-element.75), channel_id=1, source_target_pairs={{0,6},{1,7},{2,0},{3,1},{4,2},{5,3},{6,4},{7,5},{8,14},{9,15},{10,... | collective-permute-start | bytes 638984 | tf_op jit(solution)/shard_map/ppermute | solution.py:442
  77.0 13.4 %collective-permute-start.18 = (f32[416,128]{1,0:T(8,128)}, f32[416,128]{1,0:T(8,128)}, u32[]{:S(2)}, u32[]{:S(2)}) collective-permute-start(f32[416,128]{1,0:T(8,128)} %get-tuple-element.91), channel_id=1, source_target_pairs={{0,2},{1,3},{2,4},{3,5},{4,6},{5,7},{6,0},{7,1},{8,10},{9,11},{10,... | collective-permute-start | bytes 638984 | tf_op jit(solution)/shard_map/ppermute | solution.py:442
  78.5 12.3 %collective-permute-start.19 = (f32[416,128]{1,0:T(8,128)}, f32[416,128]{1,0:T(8,128)}, u32[]{:S(2)}, u32[]{:S(2)}) collective-permute-start(f32[416,128]{1,0:T(8,128)} %get-tuple-element.92), channel_id=1, source_target_pairs={{0,6},{1,7},{2,0},{3,1},{4,2},{5,3},{6,4},{7,5},{8,14},{9,15},{10,... | collective-permute-start | bytes 638984 | tf_op jit(solution)/shard_map/ppermute | solution.py:442
  86.6 16.0 %collective-permute-start.12 = (f32[416,128]{1,0:T(8,128)}, f32[416,128]{1,0:T(8,128)}, u32[]{:S(2)}, u32[]{:S(2)}) collective-permute-start(f32[416,128]{1,0:T(8,128)} %get-tuple-element.78), channel_id=1, source_target_pairs={{0,2},{1,3},{2,4},{3,5},{4,6},{5,7},{6,0},{7,1},{8,10},{9,11},{10,... | collective-permute-start | bytes 638984 | tf_op jit(solution)/shard_map/ppermute | solution.py:442
  86.6 16.0 %collective-permute-start.13 = (f32[416,128]{1,0:T(8,128)}, f32[416,128]{1,0:T(8,128)}, u32[]{:S(2)}, u32[]{:S(2)}) collective-permute-start(f32[416,128]{1,0:T(8,128)} %get-tuple-element.79), channel_id=1, source_target_pairs={{0,6},{1,7},{2,0},{3,1},{4,2},{5,3},{6,4},{7,5},{8,14},{9,15},{10,... | collective-permute-start | bytes 638984 | tf_op jit(solution)/shard_map/ppermute | solution.py:442
  98.7 11.5 %collective-permute-start.20 = (f32[416,128]{1,0:T(8,128)S(1)}, f32[416,128]{1,0:T(8,128)S(1)}, u32[]{:S(2)}, u32[]{:S(2)}) collective-permute-start(f32[416,128]{1,0:T(8,128)S(1)} %get-tuple-element.95), channel_id=1, source_target_pairs={{0,2},{1,3},{2,4},{3,5},{4,6},{5,7},{6,0},{7,1},{8,10},{9,11},{10,... | collective-permute-start | bytes 638984 | tf_op jit(solution)/shard_map/ppermute | solution.py:442
  99.0 11.2 %collective-permute-start.21 = (f32[416,128]{1,0:T(8,128)S(1)}, f32[416,128]{1,0:T(8,128)S(1)}, u32[]{:S(2)}, u32[]{:S(2)}) collective-permute-start(f32[416,128]{1,0:T(8,128)S(1)} %get-tuple-element.96), channel_id=1, source_target_pairs={{0,6},{1,7},{2,0},{3,1},{4,2},{5,3},{6,4},{7,5},{8,14},{9,15},{10,... | collective-permute-start | bytes 638984 | tf_op jit(solution)/shard_map/ppermute | solution.py:442
  106.7 10.1 %collective-permute-start.22 = (f32[384,128]{1,0:T(8,128)S(1)}, f32[384,128]{1,0:T(8,128)S(1)}, u32[]{:S(2)}, u32[]{:S(2)}) collective-permute-start(f32[384,128]{1,0:T(8,128)S(1)} %get-tuple-element.99), channel_id=1, source_target_pairs={{0,1},{1,0},{2,3},{3,2},{4,5},{5,4},{6,7},{7,6},{8,9},{9,8},{10,11... | collective-permute-start | bytes 589832 | tf_op jit(solution)/shard_map/ppermute | solution.py:442
  108.2 9.1 %collective-permute-start.24 = (f32[384,128]{1,0:T(8,128)S(1)}, f32[384,128]{1,0:T(8,128)S(1)}, u32[]{:S(2)}, u32[]{:S(2)}) collective-permute-start(f32[384,128]{1,0:T(8,128)S(1)} %get-tuple-element.104), channel_id=1, source_target_pairs={{0,16},{8,24},{16,0},{24,8},{1,17},{9,25},{17,1},{25,9},{2,18},{10... | collective-permute-start | bytes 589832 | tf_op jit(solution)/shard_map/ppermute | solution.py:442
  109.7 9.4 %collective-permute-start.25 = (f32[384,128]{1,0:T(8,128)}, f32[384,128]{1,0:T(8,128)S(1)}, u32[]{:S(2)}, u32[]{:S(2)}) collective-permute-start(f32[384,128]{1,0:T(8,128)} %get-tuple-element.111), channel_id=1, source_target_pairs={{0,17},{1,16},{2,19},{3,18},{4,21},{5,20},{6,23},{7,22},{8,25},{9,... | collective-permute-start | bytes 589832 | tf_op jit(solution)/shard_map/ppermute | solution.py:466
  113.8 7.4 %collective-permute-start.23 = (f32[384,128]{1,0:T(8,128)S(1)}, f32[384,128]{1,0:T(8,128)S(1)}, u32[]{:S(2)}, u32[]{:S(2)}) collective-permute-start(f32[384,128]{1,0:T(8,128)S(1)} %get-tuple-element.100), channel_id=1, source_target_pairs={{0,1},{1,0},{2,3},{3,2},{4,5},{5,4},{6,7},{7,6},{8,9},{9,8},{10,11... | collective-permute-start | bytes 589832 | tf_op jit(solution)/shard_map/ppermute | solution.py:442
  116.8 6.8 %collective-permute-start.27 = (f32[384,128]{1,0:T(8,128)}, f32[384,128]{1,0:T(8,128)S(1)}, u32[]{:S(2)}, u32[]{:S(2)}) collective-permute-start(f32[384,128]{1,0:T(8,128)} %get-tuple-element.112), channel_id=1, source_target_pairs={{0,17},{1,16},{2,19},{3,18},{4,21},{5,20},{6,23},{7,22},{8,25},{9,... | collective-permute-start | bytes 589832 | tf_op jit(solution)/shard_map/ppermute | solution.py:466
  131.7 6.7 %collective-permute-start.32 = (f32[64,512]{1,0:T(8,128)S(1)}, f32[64,512]{1,0:T(8,128)S(1)}, u32[]{:S(2)}, u32[]{:S(2)}) collective-permute-start(f32[64,512]{1,0:T(8,128)S(1)} %get-tuple-element.110), channel_id=1, source_target_pairs={{0,17},{1,16},{2,19},{3,18},{4,21},{5,20},{6,23},{7,22},{8,25},{9,... | collective-permute-start | bytes 393224 | tf_op jit(solution)/shard_map/ppermute | solution.py:466
  138.4 13.9 %collective-permute-start.33 = (f32[384,128]{1,0:T(8,128)}, f32[384,128]{1,0:T(8,128)S(1)}, u32[]{:S(2)}, u32[]{:S(2)}) collective-permute-start(f32[384,128]{1,0:T(8,128)} %get-tuple-element.111), channel_id=1, source_target_pairs={{0,1},{1,0},{2,3},{3,2},{4,5},{5,4},{6,7},{7,6},{8,9},{9,8},{10,11... | collective-permute-start | bytes 589832 | tf_op jit(solution)/shard_map/ppermute | solution.py:442
  139.8 12.4 %collective-permute-start.34 = (f32[384,128]{1,0:T(8,128)}, f32[384,128]{1,0:T(8,128)S(1)}, u32[]{:S(2)}, u32[]{:S(2)}) collective-permute-start(f32[384,128]{1,0:T(8,128)} %get-tuple-element.112), channel_id=1, source_target_pairs={{0,1},{1,0},{2,3},{3,2},{4,5},{5,4},{6,7},{7,6},{8,9},{9,8},{10,11... | collective-permute-start | bytes 589832 | tf_op jit(solution)/shard_map/ppermute | solution.py:442
  140.5 8.3 %collective-permute-start.35 = (f32[64,512]{1,0:T(8,128)S(1)}, f32[64,512]{1,0:T(8,128)S(1)}, u32[]{:S(2)}, u32[]{:S(2)}) collective-permute-start(f32[64,512]{1,0:T(8,128)S(1)} %shard_map.105.refs_1_), channel_id=1, source_target_pairs={{0,2},{1,3},{2,4},{3,5},{4,6},{5,7},{6,0},{7,1},{8,10},{9,11},{10,... | collective-permute-start | bytes 393224 | tf_op jit(solution)/shard_map/ppermute | solution.py:442
  140.5 11.8 %collective-permute-start.36 = (f32[64,512]{1,0:T(8,128)S(1)}, f32[64,512]{1,0:T(8,128)S(1)}, u32[]{:S(2)}, u32[]{:S(2)}) collective-permute-start(f32[64,512]{1,0:T(8,128)S(1)} %shard_map.105.refs_1_), channel_id=1, source_target_pairs={{0,4},{1,5},{2,6},{3,7},{4,0},{5,1},{6,2},{7,3},{8,12},{9,13},{10,... | collective-permute-start | bytes 393224 | tf_op jit(solution)/shard_map/ppermute | solution.py:442
  141.9 10.3 %collective-permute-start.37 = (f32[64,512]{1,0:T(8,128)S(1)}, f32[64,512]{1,0:T(8,128)S(1)}, u32[]{:S(2)}, u32[]{:S(2)}) collective-permute-start(f32[64,512]{1,0:T(8,128)S(1)} %shard_map.105.refs_1_), channel_id=1, source_target_pairs={{0,6},{1,7},{2,0},{3,1},{4,2},{5,3},{6,4},{7,5},{8,14},{9,15},{10,... | collective-permute-start | bytes 393224 | tf_op jit(solution)/shard_map/ppermute | solution.py:442
  (45 other events, 340.3 us)

commit v4 on v3

--- a/solution.py
+++ b/solution.py
@@ -142,9 +142,11 @@
 def share_coef(coef, coef_ref, up_ref, down_ref):
     packed = collapse(coef)
     coef_ref[...] = packed
-    rim = up_ref.shape[0] - 32
-    up_ref[pl.ds(rim, 32), :] = packed
-    down_ref[pl.ds(rim, 32), :] = packed
+    rim = up_ref.shape[0] - 16
+    group = lane_ids((16, LANES)) // QUARTER
+    top, bottom = packed[:16], packed[16:]
+    up_ref[pl.ds(rim, 16), :] = jnp.where(group % 2 == 0, turn(top, -QUARTER), bottom)
+    down_ref[pl.ds(rim, 16), :] = jnp.where(group % 2 == 0, top, turn(bottom, QUARTER))
 
 
 def collapse(blocks):
@@ -180,9 +182,10 @@
     rim = 6 * part
     part_group = lane_ids((part, LANES)) // QUARTER
     cg = lane_ids((32, LANES)) // QUARTER
-    from_below = below_ref[pl.ds(rim, 32), :]
-    from_above = above_ref[pl.ds(rim, 32), :]
-    total = own_ref[...] + jnp.where(cg % 2 == 0, turn(from_below, 32), turn(from_above, -32))
+    low, high = below_ref[pl.ds(rim, 16), :], above_ref[pl.ds(rim, 16), :]
+    from_below = jnp.concatenate([turn(low, 2 * QUARTER), turn(low, QUARTER)], axis=0)
+    from_above = jnp.concatenate([turn(high, -QUARTER), turn(high, 2 * QUARTER)], axis=0)
+    total = own_ref[...] + jnp.where(cg % 2 == 0, from_below, from_above)
     total = total * kb_ref[...]
     rows = []
     for i, s, source in (
@@ -511,7 +514,7 @@
     for k, got in enumerate((other0, other1)):
         made = call(
             functools.partial(assemble_kernel, k),
-            [f32(6, cells, LANES)] + [f32(rim_rows + 32, LANES)] * 2 + [f32(32, LANES)],
+            [f32(6, cells, LANES)] + [f32(rim_rows + 16, LANES)] * 2 + [f32(32, LANES)],
             [y1],
             [field, got, mh, ml],
         )
@@ -529,7 +532,7 @@
                 out += [f32(rim_rows, LANES)] * 4
             else:
                 arrays += [mh, ml]
-                out += [f32(rim_rows + 32, LANES)] * 2 + [f32(32, LANES)]
+                out += [f32(rim_rows + 16, LANES)] * 2 + [f32(32, LANES)]
             made = call(
                 functools.partial(level_kernel, scales[level], recall[level], first, last),
                 out,

time: 159 us -> 158 us (level)
  waiting for transfers between devices: 38.3 us -> 35.7 us
    ppermute x36, waiting for transfers between devices: 32.5 us -> 29.1 us  [move(): lax.ppermute(array, axis, [(i, target(i) % size) for i in range(size)])]
  transfers between devices with their start and end apart: 39 -> 39, of which waited for: 19 -> 16; matrix products, arithmetic and copies ran while one was open for 0% -> 0% of each run, Pallas kernels for 28% -> 28%
where the time goes in v4:
time: 158 us; the launch traced here: 157 us
  starting transfers between devices  59.5 us (38%)
  Pallas kernels  48.3 us (31%)
  waiting for transfers between devices  35.7 us (23%)
  local copies, waits for them, and re-layouts  12.4 us (8%)
    ppermute x36, starting transfers between devices, move(): lax.ppermute(array, axis, [(i, target(i) % size) for i in range(size)])  58.4 us
    pallas_call x23, Pallas kernels, call(): pl.pallas_call(body, out_shape=out, in_specs=[SMEM] * len(scalars) + [VME...  48.3 us
    ppermute x36, waiting for transfers between devices, move(): lax.ppermute(array, axis, [(i, target(i) % size) for i in range(size)])  29.1 us
    unnamed x76, local copies, waits for them, and re-layouts  12.2 us
    ppermute x3, waiting for transfers between devices, diagonal(): lax.ppermute(array, ('band', 'grid'), [(i, i ^ flip) for i in range(size)])  6.67 us
  transfers between devices with their start and end apart: 39, of which 16 were waited for; matrix products, arithmetic and copies ran while one was open for 0% of the time, Pallas kernels for 28%

profile of v4, /device:TPU:0, one launch (start us, length us, event | category | flops | bytes accessed | tf_op | source)
XLA Modules:
  0.0 157.2 jit_solution(1731675494229455246)
XLA Ops:
  2.5 3.0 %collective-permute-start = (f32[768,128]{1,0:T(8,128)S(1)}, f32[768,128]{1,0:T(8,128)S(1)}, u32[]{:S(2)}, u32[]{:S(2)}) collective-permute-start(f32[768,128]{1,0:T(8,128)S(1)} %shard_map.86.refs_3_), channel_id=1, source_target_pairs={{0,1},{1,0},{2,3},{3,2},{4,5},{5,4},{6,7},{7,6},{8,9},{9,8},{10,11... | collective-permute-start | bytes 1179656 | tf_op jit(solution)/shard_map/ppermute | solution.py:445
  8.3 4.1 %collective-permute-start.2 = (f32[6,16,256]{2,1,0:T(8,128)S(1)}, f32[6,16,256]{2,1,0:T(8,128)S(1)}, u32[]{:S(2)}, u32[]{:S(2)}) collective-permute-start(f32[6,16,256]{2,1,0:T(8,128)S(1)} %get-tuple-element.60), channel_id=1, source_target_pairs={{0,6},{1,3},{2,0},{3,5},{4,2},{5,7},{6,4},{7,1},{8,14},{9,11},{10,... | collective-permute-start | bytes 294920 | tf_op jit(solution)/shard_map/ppermute | solution.py:445
  13.7 3.5 %collective-permute-done.refs_3_.refs_2_ = f32[768,128]{1,0:T(8,128)S(1)} collective-permute-done((f32[768,128]{1,0:T(8,128)S(1)}, f32[768,128]{1,0:T(8,128)S(1)}, u32[]{:S(2)}, u32[]{:S(2)}) %collective-permute-start) | collective-permute-done | bytes 393248 | tf_op jit(solution)/shard_map/ppermute | solution.py:445
  17.7 2.1 %collective-permute-done.3.refs_3_ = f32[6,16,256]{2,1,0:T(8,128)S(1)} collective-permute-done((f32[6,16,256]{2,1,0:T(8,128)S(1)}, f32[6,16,256]{2,1,0:T(8,128)S(1)}, u32[]{:S(2)}, u32[]{:S(2)}) %collective-permute-start.3) | collective-permute-done | bytes 98336 | tf_op jit(solution)/shard_map/ppermute | solution.py:445
  19.8 3.3 %collective-permute-done.1.refs_1_ = f32[18,16,256]{2,1,0:T(8,128)S(1)} collective-permute-done((f32[18,16,256]{2,1,0:T(8,128)S(1)}, f32[18,16,256]{2,1,0:T(8,128)S(1)}, u32[]{:S(2)}, u32[]{:S(2)}) %collective-permute-start.1) | collective-permute-done | bytes 294944 | tf_op jit(solution)/shard_map/ppermute | solution.py:445
  30.4 2.1 %collective-permute-start.6 = (f32[400,128]{1,0:T(8,128)}, f32[400,128]{1,0:T(8,128)}, u32[]{:S(2)}, u32[]{:S(2)}) collective-permute-start(f32[400,128]{1,0:T(8,128)} %get-tuple-element.65), channel_id=1, source_target_pairs={{0,6},{1,7},{2,0},{3,1},{4,2},{5,3},{6,4},{7,5},{8,14},{9,15},{10,... | collective-permute-start | bytes 614408 | tf_op jit(solution)/shard_map/ppermute | solution.py:445
  32.5 2.5 %collective-permute-done.7.refs_2_ = f32[792,128]{1,0:T(8,128)S(1)} collective-permute-done((f32[792,128]{1,0:T(8,128)S(1)}, f32[792,128]{1,0:T(8,128)S(1)}, u32[]{:S(2)}, u32[]{:S(2)}) %collective-permute-start.7) | collective-permute-done | bytes 405536 | tf_op jit(solution)/shard_map/ppermute | solution.py:445
  39.5 2.0 %collective-permute-start.15 = (f32[400,128]{1,0:T(8,128)}, f32[400,128]{1,0:T(8,128)}, u32[]{:S(2)}, u32[]{:S(2)}) collective-permute-start(f32[400,128]{1,0:T(8,128)} %get-tuple-element.84), channel_id=1, source_target_pairs={{0,6},{1,7},{2,0},{3,1},{4,2},{5,3},{6,4},{7,5},{8,14},{9,15},{10,... | collective-permute-start | bytes 614408 | tf_op jit(solution)/shard_map/ppermute | solution.py:445
  45.0 4.4 %shard_map.93 = (f32[6,256,128]{2,1,0:T(8,128)S(1)}, f32[400,128]{1,0:T(8,128)S(1)}, f32[400,128]{1,0:T(8,128)S(1)}, f32[32,128]{1,0:T(8,128)S(1)}) custom-call(f32[6,256,128]{2,1,0:T(8,128)S(1)} %copy-done.18, f32[400,128]{1,0:T(8,128)} %collective-permute-done.5.refs_1_, f32[400,128]{1,0:T(8,128)} %collective-permute-done.6.refs_2_, ...), custom_call_target="tpu_custom_call" | custom-call | flops 1024 | bytes 1024 | tf_op jit(solution)/shard_map/pallas_call | solution.py:411
  49.4 3.8 %collective-permute-start.9 = (f32[400,128]{1,0:T(8,128)S(1)}, f32[400,128]{1,0:T(8,128)S(1)}, u32[]{:S(2)}, u32[]{:S(2)}) collective-permute-start(f32[400,128]{1,0:T(8,128)S(1)} %get-tuple-element.71), channel_id=1, source_target_pairs={{0,6},{1,7},{2,0},{3,1},{4,2},{5,3},{6,4},{7,5},{8,14},{9,15},{10,... | collective-permute-start | bytes 614408 | tf_op jit(solution)/shard_map/ppermute | solution.py:445
  53.3 4.4 %shard_map.98 = (f32[6,256,128]{2,1,0:T(8,128)S(1)}, f32[400,128]{1,0:T(8,128)S(1)}, f32[400,128]{1,0:T(8,128)S(1)}, f32[32,128]{1,0:T(8,128)S(1)}) custom-call(f32[6,256,128]{2,1,0:T(8,128)S(1)} %copy-done.16, f32[400,128]{1,0:T(8,128)} %collective-permute-done.14.refs_1_, f32[400,128]{1,0:T(8,128)} %collective-permute-done.15.refs_2_, ...), custom_call_target="tpu_custom_call" | custom-call | flops 1024 | bytes 1024 | tf_op jit(solution)/shard_map/pallas_call | solution.py:411
  57.7 3.8 %collective-permute-start.17 = (f32[400,128]{1,0:T(8,128)S(1)}, f32[400,128]{1,0:T(8,128)S(1)}, u32[]{:S(2)}, u32[]{:S(2)}) collective-permute-start(f32[400,128]{1,0:T(8,128)S(1)} %get-tuple-element.88), channel_id=1, source_target_pairs={{0,6},{1,7},{2,0},{3,1},{4,2},{5,3},{6,4},{7,5},{8,14},{9,15},{10,... | collective-permute-start | bytes 614408 | tf_op jit(solution)/shard_map/ppermute | solution.py:445
  61.5 3.3 %shard_map.94 = (f32[6,256,128]{2,1,0:T(8,128)S(1)}, f32[400,128]{1,0:T(8,128)S(1)}, f32[400,128]{1,0:T(8,128)S(1)}, f32[32,128]{1,0:T(8,128)S(1)}) custom-call(f32[6,256,128]{2,1,0:T(8,128)S(1)} %get-tuple-element.69.refs_0_.refs_1_, f32[6,256,128]{2,1,0:T(8,128)S(1)} %copy-done.19, f32[400,128]{1,0:T(8,128)S(1)} %collective-permute-done.8.refs_2_, ...), custom_call_target="tpu_custom_call" | custom-call | flops 1024 | bytes 1024 | tf_op jit(solution)/shard_map/pallas_call | solution.py:411
  64.9 4.7 %collective-permute-start.10 = (f32[400,128]{1,0:T(8,128)S(1)}, f32[400,128]{1,0:T(8,128)S(1)}, u32[]{:S(2)}, u32[]{:S(2)}) collective-permute-start(f32[400,128]{1,0:T(8,128)S(1)} %get-tuple-element.74), channel_id=1, source_target_pairs={{0,2},{1,3},{2,4},{3,5},{4,6},{5,7},{6,0},{7,1},{8,10},{9,11},{10,... | collective-permute-start | bytes 614408 | tf_op jit(solution)/shard_map/ppermute | solution.py:445
  70.4 4.1 %shard_map.99 = (f32[6,256,128]{2,1,0:T(8,128)S(1)}, f32[400,128]{1,0:T(8,128)}, f32[400,128]{1,0:T(8,128)}, f32[32,128]{1,0:T(8,128)S(1)}) custom-call(f32[6,256,128]{2,1,0:T(8,128)S(1)} %get-tuple-element.86.refs_0_.refs_1_, f32[6,256,128]{2,1,0:T(8,128)S(1)} %copy-done.16, f32[400,128]{1,0:T(8,128)S(1)} %collective-permute-done.16.refs_2_, ...), custom_call_target="tpu_custom_call" | custom-call | flops 1024 | bytes 1024 | tf_op jit(solution)/shard_map/pallas_call | solution.py:411
  75.4 2.2 %collective-permute-start.18 = (f32[400,128]{1,0:T(8,128)}, f32[400,128]{1,0:T(8,128)}, u32[]{:S(2)}, u32[]{:S(2)}) collective-permute-start(f32[400,128]{1,0:T(8,128)} %get-tuple-element.91), channel_id=1, source_target_pairs={{0,2},{1,3},{2,4},{3,5},{4,6},{5,7},{6,0},{7,1},{8,10},{9,11},{10,... | collective-permute-start | bytes 614408 | tf_op jit(solution)/shard_map/ppermute | solution.py:445
  79.2 4.1 %shard_map.95 = (f32[6,256,128]{2,1,0:T(8,128)S(1)}, f32[400,128]{1,0:T(8,128)}, f32[400,128]{1,0:T(8,128)}, f32[32,128]{1,0:T(8,128)S(1)}) custom-call(f32[6,256,128]{2,1,0:T(8,128)S(1)} %get-tuple-element.73.refs_0_.refs_2_, f32[6,256,128]{2,1,0:T(8,128)S(1)} %get-tuple-element.69.refs_0_.refs_1_, f32[400,128]{1,0:T(8,128)S(1)} %collective-permute-done.10.refs_2_, ...), custom_call_target="tpu_custom_call" | custom-call | flops 1024 | bytes 1024 | tf_op jit(solution)/shard_map/pallas_call | solution.py:411
  84.6 3.4 %collective-permute-start.13 = (f32[400,128]{1,0:T(8,128)}, f32[400,128]{1,0:T(8,128)}, u32[]{:S(2)}, u32[]{:S(2)}) collective-permute-start(f32[400,128]{1,0:T(8,128)} %get-tuple-element.79), channel_id=1, source_target_pairs={{0,6},{1,7},{2,0},{3,1},{4,2},{5,3},{6,4},{7,5},{8,14},{9,15},{10,... | collective-permute-start | bytes 614408 | tf_op jit(solution)/shard_map/ppermute | solution.py:445
  91.4 4.5 %shard_map.100 = (f32[6,256,128]{2,1,0:T(8,128)S(1)}, f32[400,128]{1,0:T(8,128)S(1)}, f32[400,128]{1,0:T(8,128)S(1)}, f32[32,128]{1,0:T(8,128)S(1)}) custom-call(f32[6,256,128]{2,1,0:T(8,128)S(1)} %copy-done.9, f32[6,256,128]{2,1,0:T(8,128)S(1)} %copy-done.14, f32[400,128]{1,0:T(8,128)} %collective-permute-done.18.refs_2_, ...), custom_call_target="tpu_custom_call" | custom-call | flops 1024 | bytes 1024 | tf_op jit(solution)/shard_map/pallas_call | solution.py:411
  95.9 3.8 %collective-permute-start.21 = (f32[400,128]{1,0:T(8,128)S(1)}, f32[400,128]{1,0:T(8,128)S(1)}, u32[]{:S(2)}, u32[]{:S(2)}) collective-permute-start(f32[400,128]{1,0:T(8,128)S(1)} %get-tuple-element.96), channel_id=1, source_target_pairs={{0,6},{1,7},{2,0},{3,1},{4,2},{5,3},{6,4},{7,5},{8,14},{9,15},{10,... | collective-permute-start | bytes 614408 | tf_op jit(solution)/shard_map/ppermute | solution.py:445
  99.9 4.0 %shard_map.96 = (f32[6,256,128]{2,1,0:T(8,128)S(1)}, f32[384,128]{1,0:T(8,128)S(1)}, f32[384,128]{1,0:T(8,128)S(1)}, f32[384,128]{1,0:T(8,128)S(1)}, f32[384,128]{1,0:T(8,128)}) custom-call(s32[2]{0:T(128)S(1)} %pad_add_fusion.refs_0_, f32[6,256,128]{2,1,0:T(8,128)S(1)} %copy-done.25, f32[6,256,128]{2,1,0:T(8,128)S(1)} %copy-done.12, ...), custom_call_target="tpu_custom_call" | custom-call | flops 1024 | bytes 1024 | tf_op jit(solution)/shard_map/pallas_call | solution.py:411
  107.4 3.5 %shard_map.101 = (f32[6,256,128]{2,1,0:T(8,128)S(1)}, f32[384,128]{1,0:T(8,128)S(1)}, f32[384,128]{1,0:T(8,128)S(1)}, f32[384,128]{1,0:T(8,128)S(1)}, f32[384,128]{1,0:T(8,128)}) custom-call(s32[2]{0:T(128)S(1)} %pad_add_fusion.refs_0_, f32[6,256,128]{2,1,0:T(8,128)S(1)} %get-tuple-element.94.refs_1_, f32[6,256,128]{2,1,0:T(8,128)S(1)} %copy-done.10, ...), custom_call_target="tpu_custom_call" | custom-call | flops 1024 | bytes 1024 | tf_op jit(solution)/shard_map/pallas_call | solution.py:411
  110.9 1.9 %collective-permute-start.23 = (f32[384,128]{1,0:T(8,128)S(1)}, f32[384,128]{1,0:T(8,128)S(1)}, u32[]{:S(2)}, u32[]{:S(2)}) collective-permute-start(f32[384,128]{1,0:T(8,128)S(1)} %get-tuple-element.100), channel_id=1, source_target_pairs={{0,1},{1,0},{2,3},{3,2},{4,5},{5,4},{6,7},{7,6},{8,9},{9,8},{10,11... | collective-permute-start | bytes 589832 | tf_op jit(solution)/shard_map/ppermute | solution.py:445
  114.4 2.0 %collective-permute-done.25.refs_4_ = f32[384,128]{1,0:T(8,128)S(1)} collective-permute-done((f32[384,128]{1,0:T(8,128)}, f32[384,128]{1,0:T(8,128)S(1)}, u32[]{:S(2)}, u32[]{:S(2)}) %collective-permute-start.25) | collective-permute-done | bytes 196640 | tf_op jit(solution)/shard_map/ppermute | solution.py:469
  119.9 2.6 %collective-permute-done.27.refs_4_ = f32[384,128]{1,0:T(8,128)S(1)} collective-permute-done((f32[384,128]{1,0:T(8,128)}, f32[384,128]{1,0:T(8,128)S(1)}, u32[]{:S(2)}, u32[]{:S(2)}) %collective-permute-start.27) | collective-permute-done | bytes 196640 | tf_op jit(solution)/shard_map/ppermute | solution.py:469
  123.5 2.3 %collective-permute-done.29.refs_4_ = f32[1536,128]{1,0:T(8,128)S(1)} collective-permute-done((f32[1536,128]{1,0:T(8,128)S(1)}, f32[1536,128]{1,0:T(8,128)S(1)}, u32[]{:S(2)}, u32[]{:S(2)}) %collective-permute-start.29) | collective-permute-done | bytes 786464 | tf_op jit(solution)/shard_map/ppermute | solution.py:445
  131.3 2.0 %collective-permute-done.30.refs_1_ = f32[64,512]{1,0:T(8,128)S(1)} collective-permute-done((f32[64,512]{1,0:T(8,128)S(1)}, f32[64,512]{1,0:T(8,128)S(1)}, u32[]{:S(2)}, u32[]{:S(2)}) %collective-permute-start.30) | collective-permute-done | bytes 131104 | tf_op jit(solution)/shard_map/ppermute | solution.py:445
  135.2 2.1 %collective-permute-done.32.refs_3_ = f32[64,512]{1,0:T(8,128)S(1)} collective-permute-done((f32[64,512]{1,0:T(8,128)S(1)}, f32[64,512]{1,0:T(8,128)S(1)}, u32[]{:S(2)}, u32[]{:S(2)}) %collective-permute-start.32) | collective-permute-done | bytes 131104 | tf_op jit(solution)/shard_map/ppermute | solution.py:469
  140.0 3.3 %collective-permute-start.37 = (f32[64,512]{1,0:T(8,128)S(1)}, f32[64,512]{1,0:T(8,128)S(1)}, u32[]{:S(2)}, u32[]{:S(2)}) collective-permute-start(f32[64,512]{1,0:T(8,128)S(1)} %shard_map.105.refs_1_), channel_id=1, source_target_pairs={{0,6},{1,7},{2,0},{3,1},{4,2},{5,3},{6,4},{7,5},{8,14},{9,15},{10,... | collective-permute-start | bytes 393224 | tf_op jit(solution)/shard_map/ppermute | solution.py:445
  143.2 4.4 %collective-permute-done.35.refs_2_ = f32[64,512]{1,0:T(8,128)S(1)} collective-permute-done((f32[64,512]{1,0:T(8,128)S(1)}, f32[64,512]{1,0:T(8,128)S(1)}, u32[]{:S(2)}, u32[]{:S(2)}) %collective-permute-start.35) | collective-permute-done | bytes 131104 | tf_op jit(solution)/shard_map/ppermute | solution.py:445
  147.7 3.2 %collective-permute-done.36.refs_3_ = f32[64,512]{1,0:T(8,128)S(1)} collective-permute-done((f32[64,512]{1,0:T(8,128)S(1)}, f32[64,512]{1,0:T(8,128)S(1)}, u32[]{:S(2)}, u32[]{:S(2)}) %collective-permute-start.36) | collective-permute-done | bytes 131104 | tf_op jit(solution)/shard_map/ppermute | solution.py:445
  152.1 3.4 %shard_map.106 = f32[12,256,128]{2,1,0:T(8,128)} custom-call(s32[2]{0:T(128)S(1)} %pad_add_fusion.refs_0_, f32[6,256,128]{2,1,0:T(8,128)S(1)} %copy-done.27, f32[6,256,128]{2,1,0:T(8,128)S(1)} %copy-done.29, f32[384,128]{1,0:T(8,128)S(1)} %copy-done.23, f32[384,128]{1,0:T(8,128)S(1)} %collective-permute-done.23.refs_3_.refs_4_, ...), custom_call_target="tpu_custom_call" | custom-call | flops 1024 | bytes 1024 | tf_op jit(solution)/shard_map/pallas_call | solution.py:411
  (152 shorter events, 52.3 us)
Async XLA Ops:
  2.5 14.7 %collective-permute-start = (f32[768,128]{1,0:T(8,128)S(1)}, f32[768,128]{1,0:T(8,128)S(1)}, u32[]{:S(2)}, u32[]{:S(2)}) collective-permute-start(f32[768,128]{1,0:T(8,128)S(1)} %shard_map.86.refs_3_), channel_id=1, source_target_pairs={{0,1},{1,0},{2,3},{3,2},{4,5},{5,4},{6,7},{7,6},{8,9},{9,8},{10,11... | collective-permute-start | bytes 1179656 | tf_op jit(solution)/shard_map/ppermute | solution.py:445
  8.3 14.8 %collective-permute-start.1 = (f32[18,16,256]{2,1,0:T(8,128)S(1)}, f32[18,16,256]{2,1,0:T(8,128)S(1)}, u32[]{:S(2)}, u32[]{:S(2)}) collective-permute-start(f32[18,16,256]{2,1,0:T(8,128)S(1)} %get-tuple-element.59), channel_id=1, source_target_pairs={{0,1},{1,0},{2,3},{3,2},{4,5},{5,4},{6,7},{7,6},{8,9},{9,8},{10,11... | collective-permute-start | bytes 884744 | tf_op jit(solution)/shard_map/ppermute | solution.py:445
  8.3 9.4 %collective-permute-start.2 = (f32[6,16,256]{2,1,0:T(8,128)S(1)}, f32[6,16,256]{2,1,0:T(8,128)S(1)}, u32[]{:S(2)}, u32[]{:S(2)}) collective-permute-start(f32[6,16,256]{2,1,0:T(8,128)S(1)} %get-tuple-element.60), channel_id=1, source_target_pairs={{0,6},{1,3},{2,0},{3,5},{4,2},{5,7},{6,4},{7,1},{8,14},{9,11},{10,... | collective-permute-start | bytes 294920 | tf_op jit(solution)/shard_map/ppermute | solution.py:445
  12.4 7.4 %collective-permute-start.3 = (f32[6,16,256]{2,1,0:T(8,128)S(1)}, f32[6,16,256]{2,1,0:T(8,128)S(1)}, u32[]{:S(2)}, u32[]{:S(2)}) collective-permute-start(f32[6,16,256]{2,1,0:T(8,128)S(1)} %get-tuple-element.60), channel_id=1, source_target_pairs={{0,7},{1,2},{2,1},{3,4},{4,3},{5,6},{6,5},{7,0},{8,15},{9,10},{10,... | collective-permute-start | bytes 294920 | tf_op jit(solution)/shard_map/ppermute | solution.py:445
  23.2 11.8 %collective-permute-start.7 = (f32[792,128]{1,0:T(8,128)S(1)}, f32[792,128]{1,0:T(8,128)S(1)}, u32[]{:S(2)}, u32[]{:S(2)}) collective-permute-start(f32[792,128]{1,0:T(8,128)S(1)} %shard_map.88.refs_4_), channel_id=1, source_target_pairs={{0,1},{1,0},{2,3},{3,2},{4,5},{5,4},{6,7},{7,6},{8,9},{9,8},{10,11... | collective-permute-start | bytes 1216520 | tf_op jit(solution)/shard_map/ppermute | solution.py:445
  28.6 15.1 %collective-permute-start.5 = (f32[400,128]{1,0:T(8,128)}, f32[400,128]{1,0:T(8,128)}, u32[]{:S(2)}, u32[]{:S(2)}) collective-permute-start(f32[400,128]{1,0:T(8,128)} %get-tuple-element.64), channel_id=1, source_target_pairs={{0,2},{1,3},{2,4},{3,5},{4,6},{5,7},{6,0},{7,1},{8,10},{9,11},{10,... | collective-permute-start | bytes 614408 | tf_op jit(solution)/shard_map/ppermute | solution.py:445
  30.4 13.3 %collective-permute-start.6 = (f32[400,128]{1,0:T(8,128)}, f32[400,128]{1,0:T(8,128)}, u32[]{:S(2)}, u32[]{:S(2)}) collective-permute-start(f32[400,128]{1,0:T(8,128)} %get-tuple-element.65), channel_id=1, source_target_pairs={{0,6},{1,7},{2,0},{3,1},{4,2},{5,3},{6,4},{7,5},{8,14},{9,15},{10,... | collective-permute-start | bytes 614408 | tf_op jit(solution)/shard_map/ppermute | solution.py:445
  37.7 15.5 %collective-permute-start.14 = (f32[400,128]{1,0:T(8,128)}, f32[400,128]{1,0:T(8,128)}, u32[]{:S(2)}, u32[]{:S(2)}) collective-permute-start(f32[400,128]{1,0:T(8,128)} %get-tuple-element.83), channel_id=1, source_target_pairs={{0,2},{1,3},{2,4},{3,5},{4,6},{5,7},{6,0},{7,1},{8,10},{9,11},{10,... | collective-permute-start | bytes 614408 | tf_op jit(solution)/shard_map/ppermute | solution.py:445
  39.5 13.7 %collective-permute-start.15 = (f32[400,128]{1,0:T(8,128)}, f32[400,128]{1,0:T(8,128)}, u32[]{:S(2)}, u32[]{:S(2)}) collective-permute-start(f32[400,128]{1,0:T(8,128)} %get-tuple-element.84), channel_id=1, source_target_pairs={{0,6},{1,7},{2,0},{3,1},{4,2},{5,3},{6,4},{7,5},{8,14},{9,15},{10,... | collective-permute-start | bytes 614408 | tf_op jit(solution)/shard_map/ppermute | solution.py:445
  49.4 12.1 %collective-permute-start.8 = (f32[400,128]{1,0:T(8,128)S(1)}, f32[400,128]{1,0:T(8,128)S(1)}, u32[]{:S(2)}, u32[]{:S(2)}) collective-permute-start(f32[400,128]{1,0:T(8,128)S(1)} %get-tuple-element.70), channel_id=1, source_target_pairs={{0,2},{1,3},{2,4},{3,5},{4,6},{5,7},{6,0},{7,1},{8,10},{9,11},{10,... | collective-permute-start | bytes 614408 | tf_op jit(solution)/shard_map/ppermute | solution.py:445
  49.4 12.1 %collective-permute-start.9 = (f32[400,128]{1,0:T(8,128)S(1)}, f32[400,128]{1,0:T(8,128)S(1)}, u32[]{:S(2)}, u32[]{:S(2)}) collective-permute-start(f32[400,128]{1,0:T(8,128)S(1)} %get-tuple-element.71), channel_id=1, source_target_pairs={{0,6},{1,7},{2,0},{3,1},{4,2},{5,3},{6,4},{7,5},{8,14},{9,15},{10,... | collective-permute-start | bytes 614408 | tf_op jit(solution)/shard_map/ppermute | solution.py:445
  57.6 12.0 %collective-permute-start.16 = (f32[400,128]{1,0:T(8,128)S(1)}, f32[400,128]{1,0:T(8,128)S(1)}, u32[]{:S(2)}, u32[]{:S(2)}) collective-permute-start(f32[400,128]{1,0:T(8,128)S(1)} %get-tuple-element.87), channel_id=1, source_target_pairs={{0,2},{1,3},{2,4},{3,5},{4,6},{5,7},{6,0},{7,1},{8,10},{9,11},{10,... | collective-permute-start | bytes 614408 | tf_op jit(solution)/shard_map/ppermute | solution.py:445
  57.7 12.6 %collective-permute-start.17 = (f32[400,128]{1,0:T(8,128)S(1)}, f32[400,128]{1,0:T(8,128)S(1)}, u32[]{:S(2)}, u32[]{:S(2)}) collective-permute-start(f32[400,128]{1,0:T(8,128)S(1)} %get-tuple-element.88), channel_id=1, source_target_pairs={{0,6},{1,7},{2,0},{3,1},{4,2},{5,3},{6,4},{7,5},{8,14},{9,15},{10,... | collective-permute-start | bytes 614408 | tf_op jit(solution)/shard_map/ppermute | solution.py:445
  64.9 14.3 %collective-permute-start.10 = (f32[400,128]{1,0:T(8,128)S(1)}, f32[400,128]{1,0:T(8,128)S(1)}, u32[]{:S(2)}, u32[]{:S(2)}) collective-permute-start(f32[400,128]{1,0:T(8,128)S(1)} %get-tuple-element.74), channel_id=1, source_target_pairs={{0,2},{1,3},{2,4},{3,5},{4,6},{5,7},{6,0},{7,1},{8,10},{9,11},{10,... | collective-permute-start | bytes 614408 | tf_op jit(solution)/shard_map/ppermute | solution.py:445
  69.6 9.6 %collective-permute-start.11 = (f32[400,128]{1,0:T(8,128)S(1)}, f32[400,128]{1,0:T(8,128)S(1)}, u32[]{:S(2)}, u32[]{:S(2)}) collective-permute-start(f32[400,128]{1,0:T(8,128)S(1)} %get-tuple-element.75), channel_id=1, source_target_pairs={{0,6},{1,7},{2,0},{3,1},{4,2},{5,3},{6,4},{7,5},{8,14},{9,15},{10,... | collective-permute-start | bytes 614408 | tf_op jit(solution)/shard_map/ppermute | solution.py:445
  75.4 12.7 %collective-permute-start.18 = (f32[400,128]{1,0:T(8,128)}, f32[400,128]{1,0:T(8,128)}, u32[]{:S(2)}, u32[]{:S(2)}) collective-permute-start(f32[400,128]{1,0:T(8,128)} %get-tuple-element.91), channel_id=1, source_target_pairs={{0,2},{1,3},{2,4},{3,5},{4,6},{5,7},{6,0},{7,1},{8,10},{9,11},{10,... | collective-permute-start | bytes 614408 | tf_op jit(solution)/shard_map/ppermute | solution.py:445
  77.6 10.4 %collective-permute-start.19 = (f32[400,128]{1,0:T(8,128)}, f32[400,128]{1,0:T(8,128)}, u32[]{:S(2)}, u32[]{:S(2)}) collective-permute-start(f32[400,128]{1,0:T(8,128)} %get-tuple-element.92), channel_id=1, source_target_pairs={{0,6},{1,7},{2,0},{3,1},{4,2},{5,3},{6,4},{7,5},{8,14},{9,15},{10,... | collective-permute-start | bytes 614408 | tf_op jit(solution)/shard_map/ppermute | solution.py:445
  84.2 15.6 %collective-permute-start.12 = (f32[400,128]{1,0:T(8,128)}, f32[400,128]{1,0:T(8,128)}, u32[]{:S(2)}, u32[]{:S(2)}) collective-permute-start(f32[400,128]{1,0:T(8,128)} %get-tuple-element.78), channel_id=1, source_target_pairs={{0,2},{1,3},{2,4},{3,5},{4,6},{5,7},{6,0},{7,1},{8,10},{9,11},{10,... | collective-permute-start | bytes 614408 | tf_op jit(solution)/shard_map/ppermute | solution.py:445
  84.6 15.2 %collective-permute-start.13 = (f32[400,128]{1,0:T(8,128)}, f32[400,128]{1,0:T(8,128)}, u32[]{:S(2)}, u32[]{:S(2)}) collective-permute-start(f32[400,128]{1,0:T(8,128)} %get-tuple-element.79), channel_id=1, source_target_pairs={{0,6},{1,7},{2,0},{3,1},{4,2},{5,3},{6,4},{7,5},{8,14},{9,15},{10,... | collective-permute-start | bytes 614408 | tf_op jit(solution)/shard_map/ppermute | solution.py:445
  95.9 11.5 %collective-permute-start.20 = (f32[400,128]{1,0:T(8,128)S(1)}, f32[400,128]{1,0:T(8,128)S(1)}, u32[]{:S(2)}, u32[]{:S(2)}) collective-permute-start(f32[400,128]{1,0:T(8,128)S(1)} %get-tuple-element.95), channel_id=1, source_target_pairs={{0,2},{1,3},{2,4},{3,5},{4,6},{5,7},{6,0},{7,1},{8,10},{9,11},{10,... | collective-permute-start | bytes 614408 | tf_op jit(solution)/shard_map/ppermute | solution.py:445
  95.9 11.4 %collective-permute-start.21 = (f32[400,128]{1,0:T(8,128)S(1)}, f32[400,128]{1,0:T(8,128)S(1)}, u32[]{:S(2)}, u32[]{:S(2)}) collective-permute-start(f32[400,128]{1,0:T(8,128)S(1)} %get-tuple-element.96), channel_id=1, source_target_pairs={{0,6},{1,7},{2,0},{3,1},{4,2},{5,3},{6,4},{7,5},{8,14},{9,15},{10,... | collective-permute-start | bytes 614408 | tf_op jit(solution)/shard_map/ppermute | solution.py:445
  103.9 10.5 %collective-permute-start.22 = (f32[384,128]{1,0:T(8,128)S(1)}, f32[384,128]{1,0:T(8,128)S(1)}, u32[]{:S(2)}, u32[]{:S(2)}) collective-permute-start(f32[384,128]{1,0:T(8,128)S(1)} %get-tuple-element.99), channel_id=1, source_target_pairs={{0,1},{1,0},{2,3},{3,2},{4,5},{5,4},{6,7},{7,6},{8,9},{9,8},{10,11... | collective-permute-start | bytes 589832 | tf_op jit(solution)/shard_map/ppermute | solution.py:445
  105.8 8.6 %collective-permute-start.24 = (f32[384,128]{1,0:T(8,128)S(1)}, f32[384,128]{1,0:T(8,128)S(1)}, u32[]{:S(2)}, u32[]{:S(2)}) collective-permute-start(f32[384,128]{1,0:T(8,128)S(1)} %get-tuple-element.104), channel_id=1, source_target_pairs={{0,16},{8,24},{16,0},{24,8},{1,17},{9,25},{17,1},{25,9},{2,18},{10... | collective-permute-start | bytes 589832 | tf_op jit(solution)/shard_map/ppermute | solution.py:445
  107.3 9.1 %collective-permute-start.25 = (f32[384,128]{1,0:T(8,128)}, f32[384,128]{1,0:T(8,128)S(1)}, u32[]{:S(2)}, u32[]{:S(2)}) collective-permute-start(f32[384,128]{1,0:T(8,128)} %get-tuple-element.111), channel_id=1, source_target_pairs={{0,17},{1,16},{2,19},{3,18},{4,21},{5,20},{6,23},{7,22},{8,25},{9,... | collective-permute-start | bytes 589832 | tf_op jit(solution)/shard_map/ppermute | solution.py:469
  110.9 7.8 %collective-permute-start.23 = (f32[384,128]{1,0:T(8,128)S(1)}, f32[384,128]{1,0:T(8,128)S(1)}, u32[]{:S(2)}, u32[]{:S(2)}) collective-permute-start(f32[384,128]{1,0:T(8,128)S(1)} %get-tuple-element.100), channel_id=1, source_target_pairs={{0,1},{1,0},{2,3},{3,2},{4,5},{5,4},{6,7},{7,6},{8,9},{9,8},{10,11... | collective-permute-start | bytes 589832 | tf_op jit(solution)/shard_map/ppermute | solution.py:445
  112.8 7.1 %collective-permute-start.26 = (f32[384,128]{1,0:T(8,128)S(1)}, f32[384,128]{1,0:T(8,128)S(1)}, u32[]{:S(2)}, u32[]{:S(2)}) collective-permute-start(f32[384,128]{1,0:T(8,128)S(1)} %get-tuple-element.106), channel_id=1, source_target_pairs={{0,16},{8,24},{16,0},{24,8},{1,17},{9,25},{17,1},{25,9},{2,18},{10... | collective-permute-start | bytes 589832 | tf_op jit(solution)/shard_map/ppermute | solution.py:445
  114.4 8.2 %collective-permute-start.27 = (f32[384,128]{1,0:T(8,128)}, f32[384,128]{1,0:T(8,128)S(1)}, u32[]{:S(2)}, u32[]{:S(2)}) collective-permute-start(f32[384,128]{1,0:T(8,128)} %get-tuple-element.112), channel_id=1, source_target_pairs={{0,17},{1,16},{2,19},{3,18},{4,21},{5,20},{6,23},{7,22},{8,25},{9,... | collective-permute-start | bytes 589832 | tf_op jit(solution)/shard_map/ppermute | solution.py:469
  137.3 13.5 %collective-permute-start.33 = (f32[384,128]{1,0:T(8,128)}, f32[384,128]{1,0:T(8,128)S(1)}, u32[]{:S(2)}, u32[]{:S(2)}) collective-permute-start(f32[384,128]{1,0:T(8,128)} %get-tuple-element.111), channel_id=1, source_target_pairs={{0,1},{1,0},{2,3},{3,2},{4,5},{5,4},{6,7},{7,6},{8,9},{9,8},{10,11... | collective-permute-start | bytes 589832 | tf_op jit(solution)/shard_map/ppermute | solution.py:445
  138.4 12.4 %collective-permute-start.34 = (f32[384,128]{1,0:T(8,128)}, f32[384,128]{1,0:T(8,128)S(1)}, u32[]{:S(2)}, u32[]{:S(2)}) collective-permute-start(f32[384,128]{1,0:T(8,128)} %get-tuple-element.112), channel_id=1, source_target_pairs={{0,1},{1,0},{2,3},{3,2},{4,5},{5,4},{6,7},{7,6},{8,9},{9,8},{10,11... | collective-permute-start | bytes 589832 | tf_op jit(solution)/shard_map/ppermute | solution.py:445
  139.4 8.2 %collective-permute-start.35 = (f32[64,512]{1,0:T(8,128)S(1)}, f32[64,512]{1,0:T(8,128)S(1)}, u32[]{:S(2)}, u32[]{:S(2)}) collective-permute-start(f32[64,512]{1,0:T(8,128)S(1)} %shard_map.105.refs_1_), channel_id=1, source_target_pairs={{0,2},{1,3},{2,4},{3,5},{4,6},{5,7},{6,0},{7,1},{8,10},{9,11},{10,... | collective-permute-start | bytes 393224 | tf_op jit(solution)/shard_map/ppermute | solution.py:445
  139.4 11.4 %collective-permute-start.36 = (f32[64,512]{1,0:T(8,128)S(1)}, f32[64,512]{1,0:T(8,128)S(1)}, u32[]{:S(2)}, u32[]{:S(2)}) collective-permute-start(f32[64,512]{1,0:T(8,128)S(1)} %shard_map.105.refs_1_), channel_id=1, source_target_pairs={{0,4},{1,5},{2,6},{3,7},{4,0},{5,1},{6,2},{7,3},{8,12},{9,13},{10,... | collective-permute-start | bytes 393224 | tf_op jit(solution)/shard_map/ppermute | solution.py:445
  140.0 10.9 %collective-permute-start.37 = (f32[64,512]{1,0:T(8,128)S(1)}, f32[64,512]{1,0:T(8,128)S(1)}, u32[]{:S(2)}, u32[]{:S(2)}) collective-permute-start(f32[64,512]{1,0:T(8,128)S(1)} %shard_map.105.refs_1_), channel_id=1, source_target_pairs={{0,6},{1,7},{2,0},{3,1},{4,2},{5,3},{6,4},{7,5},{8,14},{9,15},{10,... | collective-permute-start | bytes 393224 | tf_op jit(solution)/shard_map/ppermute | solution.py:445
  (45 other events, 340.5 us)
